TPU v7x, 32 devices: a whole 2x2x4 slice. The times are simulated.
32 devices in a mesh: dp: 8 (over z, x), space: 4 (over y, core).
Axes of the slice: x: 2, y: 2, z: 4, core: 2. Of those that a mesh axis runs over, the one named last changes fastest.
Arguments:
- features: float32 [256, 24, 4, 384], P('dp', None, 'space'), may hold values from -11.25 to 11.25
- cotangent: float32 [256, 24, 4, 384], P('dp', None, 'space'), may hold values from -6 to 6
- segment_ids: int32 [256, 96], P('dp'), may hold values from 0 to 3, as said below
- w_expand: float32 [24, 144], replicated, may hold values from -1.25 to 1.25
- w_depth: float32 [9, 144], replicated, may hold values from -2 to 2
- w_reduce: float32 [144, 6], replicated, may hold values from -0.5 to 0.5
- w_excite: float32 [6, 144], replicated, may hold values from -2.5 to 2.5
- w_project: float32 [144, 24], replicated, may hold values from -0.5 to 0.5
- vector_params: float32 [774], replicated, may hold values from -0.5 to 1.4
- vector_moments: float32 [774], replicated, may hold values from 43690 to 174762
- big_stats: float32 [5, 144, 144], replicated, may hold values from 0 to 25165824
- in_stats: float32 [2, 24, 24], replicated, may hold values from 0 to 25165824
- sq_stats: float32 [2, 6, 6], replicated, may hold values from 0 to 25165824
- tap_stats: float32 [9, 9], replicated, may hold values from 0 to 25165824
Outputs:
- output: float32 [256, 24, 4, 384], P('dp', None, 'space')
- input_grad: float32 [256, 24, 4, 384], P('dp', None, 'space')
- grad_expand: float32 [24, 144], replicated
- grad_depth: float32 [9, 144], replicated
- grad_reduce: float32 [144, 6], replicated
- grad_excite: float32 [6, 144], replicated
- grad_project: float32 [144, 24], replicated
- new_expand: float32 [24, 144], replicated
- new_depth: float32 [9, 144], replicated
- new_reduce: float32 [144, 6], replicated
- new_excite: float32 [6, 144], replicated
- new_project: float32 [144, 24], replicated
- big_stats_new: float32 [5, 144, 144], replicated
- in_stats_new: float32 [2, 24, 24], replicated
- sq_stats_new: float32 [2, 6, 6], replicated
- tap_stats_new: float32 [9, 9], replicated
- vector_grads: float32 [774], replicated
- vector_moments_new: float32 [774], replicated
- vector_new: float32 [774], replicated
Inputs may be any that keep to these rules, and one draw needn't show every extreme that they name: `segment_ids`: each slot's frames fall into 4 runs with ids 0, 1, 2, 3 in order, each of two frames or more.
All inputs are finite; a program needn't handle non-finite values.
Results may differ from a plain program's by a relative error of at most 0.0003.
Values sent between devices are 32-bit elements; how exact they have to be, the bound alone decides.
A program may use at most 256 MiB of HBM per device.

v0:
```python
import math

import jax
import jax.numpy as jnp
from jax import lax
from jax.sharding import PartitionSpec as P

IN = 24
EXP = 144
SQZ = 6
FRAMES = 96
BINS = 16
REGIONS = 4
ROOT_ITERS = 10


PRECISE = lax.Precision.HIGHEST
NORM_EPS = 0.001
DECAY = 0.9
STEP_FRACTION = 0.5
VECTOR_RATE = 0.15


def passed_along(value, axis, steps):
    count = lax.axis_size(axis)
    leading, last = (max(0, -steps), min(count, count - steps))
    return lax.ppermute(value, axis, [(source, source + steps) for source in range(leading, last)])


def swish(entries):
    return entries * jax.nn.sigmoid(entries)


def exact_dot(left, right):
    return jnp.dot(left, right, precision=PRECISE)


def split_vector(vector):
    start = 4 * EXP + 2 * IN
    return (
        vector[0:EXP],
        vector[EXP : 2 * EXP],
        vector[2 * EXP : 3 * EXP],
        vector[3 * EXP : 4 * EXP],
        vector[4 * EXP : 4 * EXP + IN],
        vector[4 * EXP + IN : start],
        vector[start : start + SQZ],
        vector[start + SQZ :],
    )


def excitation(pooled, w_reduce, reduce_bias, w_excite, excite_bias):
    squeezed = swish(jnp.einsum("sre,eq->srq", pooled, w_reduce, precision=PRECISE) + reduce_bias)
    return jax.nn.sigmoid(
        jnp.einsum("srq,qe->sre", squeezed, w_excite, precision=PRECISE) + excite_bias
    )


def inverse_root(matrix):
    dimension = matrix.shape[0]
    identity = jnp.eye(dimension, dtype=matrix.dtype)
    scaling = 2.5 / jnp.sqrt(jnp.sum(matrix * matrix))
    current = scaling * matrix
    result = jnp.sqrt(jnp.sqrt(scaling)) * identity
    for iteration in range(ROOT_ITERS):
        factor = 1.25 * identity - 0.25 * current
        result = exact_dot(result, factor)
        square = exact_dot(factor, factor)
        current = exact_dot(exact_dot(square, square), current)
    return result


def precondition(weight, gradient, left_root, right_root):
    direction = exact_dot(exact_dot(left_root, gradient), right_root)
    step_rate = STEP_FRACTION / math.sqrt(weight.shape[0])
    return weight - step_rate * direction * lax.rsqrt(jnp.mean(direction * direction) + 1e-06)


def renew(old_stat, fresh):
    return DECAY * old_stat + (1.0 - DECAY) * fresh


def moments(array, axes, position_total):
    center = lax.psum(jnp.sum(array, axis=axes, keepdims=True), ("dp", "space")) / position_total
    centered = array - center
    spread = (
        lax.psum(jnp.sum(centered * centered, axis=axes, keepdims=True), ("dp", "space"))
        / position_total
    )
    return (center, lax.rsqrt(spread + NORM_EPS))


def norm_back(upstream, normed, scaling, axes, position_total):
    bias_sum, gain_sum = lax.psum(
        (
            jnp.sum(upstream, axis=axes, keepdims=True),
            jnp.sum(upstream * normed, axis=axes, keepdims=True),
        ),
        ("dp", "space"),
    )
    result = scaling * (upstream - bias_sum / position_total - normed * gain_sum / position_total)
    return (result, gain_sum.reshape(-1), bias_sum.reshape(-1))


def extend(field, bin_half):
    before = passed_along(field[:, -1:], "space", 2)
    after = passed_along(field[:, :1], "space", -2)
    tall = jnp.concatenate([before, field, after], axis=1)
    lower_flag = (bin_half == 0).astype(jnp.float32)
    upper_flag = (bin_half == 1).astype(jnp.float32)
    left_edge = passed_along(tall[:, :, -1:], "space", 1) * upper_flag
    right_edge = passed_along(tall[:, :, :1], "space", -1) * lower_flag
    return jnp.concatenate([left_edge, tall, right_edge], axis=2)


def depth_apply(extended, kernel, matches, frame_half, bin_width):
    result = jnp.zeros(
        extended.shape[:1] + (frame_half, bin_width) + extended.shape[3:], jnp.float32
    )
    for row_step in (-1, 0, 1):
        for col_step in (-1, 0, 1):
            tap_index = (row_step + 1) * 3 + col_step + 1
            window = extended[
                :,
                1 + row_step : 1 + row_step + frame_half,
                1 + col_step : 1 + col_step + bin_width,
                :,
            ]
            result = result + kernel[tap_index] * window * matches[row_step + 1]
    return result


def on_device(
    features,
    cotangent,
    segment_ids,
    w_expand,
    w_depth,
    w_reduce,
    w_excite,
    w_project,
    vector_params,
    vector_moments,
    big_stats,
    in_stats,
    sq_stats,
    tap_stats,
):
    space_rank = lax.axis_index("space")
    time_half = space_rank // 2
    bin_half = space_rank % 2
    slot_count = features.shape[0]
    cell_count = features.shape[3]
    frame_half = FRAMES // 2
    bin_width = BINS // 2
    position_total = float(slot_count * lax.axis_size("dp") * FRAMES * BINS)
    gain_one, shift_one, gain_two, shift_two, gain_three, shift_three, reduce_bias, excite_bias = (
        split_vector(vector_params)
    )
    inputs = features[:, :, 0, :]
    upstream = cotangent[:, :, 0, :]
    padded_ids = jnp.pad(segment_ids, ((0, 0), (1, 1)), constant_values=-1)
    local_ids = lax.dynamic_slice_in_dim(padded_ids, time_half * frame_half, frame_half + 2, 1)
    own_ids = local_ids[:, 1:-1]
    matches = [
        (local_ids[:, 1 + offset : 1 + offset + frame_half] == own_ids).astype(jnp.float32)[
            :, :, None, None
        ]
        for offset in (-1, 0, 1)
    ]
    expanded = jnp.einsum("sic,ie->sce", inputs, w_expand, precision=PRECISE).reshape(
        slot_count, frame_half, bin_width, EXP
    )
    mean_one, scale_one = moments(expanded, (0, 1, 2), position_total)
    normal_one = (expanded - mean_one) * scale_one
    shaped_one = normal_one * gain_one + shift_one
    sigma_one = jax.nn.sigmoid(shaped_one)
    hidden_one = shaped_one * sigma_one
    hidden_ext = extend(hidden_one, bin_half)
    mixed = depth_apply(hidden_ext, w_depth, matches, frame_half, bin_width)
    mean_two, scale_two = moments(mixed, (0, 1, 2), position_total)
    normal_two = (mixed - mean_two) * scale_two
    shaped_two = normal_two * gain_two + shift_two
    sigma_two = jax.nn.sigmoid(shaped_two)
    hidden_two = shaped_two * sigma_two
    region_range = jnp.arange(REGIONS, dtype=jnp.int32)
    regions_hot = (own_ids[:, :, None] == region_range).astype(jnp.float32)
    region_counts = (
        jnp.sum((segment_ids[:, :, None] == region_range).astype(jnp.float32), axis=1) * BINS
    )
    region_total = lax.psum(
        jnp.einsum("sfbe,sfr->sre", hidden_two, regions_hot, precision=PRECISE), "space"
    )
    pooled = region_total / region_counts[:, :, None]
    gate, excite_back = jax.vjp(excitation, pooled, w_reduce, reduce_bias, w_excite, excite_bias)
    gate_rows = jnp.einsum("sfr,sre->sfe", regions_hot, gate, precision=PRECISE)[:, :, None, :]
    gated = (hidden_two * gate_rows).reshape(slot_count, cell_count, EXP)
    projected = jnp.einsum("sce,eo->soc", gated, w_project, precision=PRECISE)
    mean_three, scale_three = moments(projected, (0, 2), position_total)
    normal_three = (projected - mean_three) * scale_three
    gain_column = gain_three.reshape(1, IN, 1)
    output = inputs + normal_three * gain_column + shift_three.reshape(1, IN, 1)
    back_three, gain_three_grad, shift_three_grad = norm_back(
        upstream, normal_three, gain_column * scale_three, (0, 2), position_total
    )
    grad_project = jnp.einsum("sce,soc->eo", gated, back_three, precision=PRECISE)
    back_gated = jnp.einsum("soc,eo->sce", back_three, w_project, precision=PRECISE).reshape(
        slot_count, frame_half, bin_width, EXP
    )
    gate_back = lax.psum(
        jnp.einsum("sfbe,sfr->sre", back_gated * hidden_two, regions_hot, precision=PRECISE),
        "space",
    )
    pooled_back, reduce_grad, reduce_bias_grad, excite_grad, excite_bias_grad = excite_back(
        gate_back
    )
    spread_back = jnp.einsum(
        "sfr,sre->sfe", regions_hot, pooled_back / region_counts[:, :, None], precision=PRECISE
    )[:, :, None, :]
    back_hidden_two = back_gated * gate_rows + spread_back
    back_shaped_two = back_hidden_two * sigma_two * (1.0 + shaped_two * (1.0 - sigma_two))
    back_mixed, gain_two_grad, shift_two_grad = norm_back(
        back_shaped_two, normal_two, gain_two * scale_two, (0, 1, 2), position_total
    )
    mixed_ext = extend(back_mixed, bin_half)
    depth_terms = []
    hidden_back = jnp.zeros_like(hidden_one)
    for row_step in (-1, 0, 1):
        for col_step in (-1, 0, 1):
            tap_index = (row_step + 1) * 3 + col_step + 1
            window = hidden_ext[
                :,
                1 + row_step : 1 + row_step + frame_half,
                1 + col_step : 1 + col_step + bin_width,
                :,
            ]
            depth_terms.append(jnp.sum(back_mixed * window * matches[row_step + 1], axis=(0, 1, 2)))
            back_window = mixed_ext[
                :,
                1 - row_step : 1 - row_step + frame_half,
                1 - col_step : 1 - col_step + bin_width,
                :,
            ]
            hidden_back = hidden_back + w_depth[tap_index] * back_window * matches[1 - row_step]
    grad_depth = jnp.stack(depth_terms)
    back_shaped_one = hidden_back * sigma_one * (1.0 + shaped_one * (1.0 - sigma_one))
    back_expanded, gain_one_grad, shift_one_grad = norm_back(
        back_shaped_one, normal_one, gain_one * scale_one, (0, 1, 2), position_total
    )
    back_flat = back_expanded.reshape(slot_count, cell_count, EXP)
    grad_expand = jnp.einsum("sic,sce->ie", inputs, back_flat, precision=PRECISE)
    input_back = upstream + jnp.einsum("sce,ie->sic", back_flat, w_expand, precision=PRECISE)
    owner_space = (space_rank == 0).astype(jnp.float32)
    sum_expand, sum_depth, sum_reduce, sum_excite, sum_project, sum_reduce_bias, sum_excite_bias = (
        lax.psum(
            (
                grad_expand,
                grad_depth,
                reduce_grad * owner_space,
                excite_grad * owner_space,
                grad_project,
                reduce_bias_grad * owner_space,
                excite_bias_grad * owner_space,
            ),
            ("dp", "space"),
        )
    )
    vector_grads = jnp.concatenate(
        [
            gain_one_grad,
            shift_one_grad,
            gain_two_grad,
            shift_two_grad,
            gain_three_grad,
            shift_three_grad,
            sum_reduce_bias,
            sum_excite_bias,
        ]
    )
    big_new = renew(
        big_stats,
        jnp.stack(
            [
                exact_dot(sum_expand.T, sum_expand),
                exact_dot(sum_project, sum_project.T),
                exact_dot(sum_reduce, sum_reduce.T),
                exact_dot(sum_excite.T, sum_excite),
                exact_dot(sum_depth.T, sum_depth),
            ]
        ),
    )
    in_new = renew(
        in_stats,
        jnp.stack([exact_dot(sum_expand, sum_expand.T), exact_dot(sum_project.T, sum_project)]),
    )
    sq_new = renew(
        sq_stats,
        jnp.stack([exact_dot(sum_reduce.T, sum_reduce), exact_dot(sum_excite, sum_excite.T)]),
    )
    tap_new = renew(tap_stats, exact_dot(sum_depth, sum_depth.T))
    owner_rank = lax.axis_index("dp")
    mine = lax.dynamic_index_in_dim(big_new, jnp.minimum(owner_rank, 4), 0, keepdims=False)
    slot_mask = (jnp.arange(5, dtype=jnp.int32) == owner_rank).astype(jnp.float32)
    big_roots = lax.psum(slot_mask[:, None, None] * inverse_root(mine)[None], "dp")
    new_expand = precondition(w_expand, sum_expand, inverse_root(in_new[0]), big_roots[0])
    new_depth = precondition(w_depth, sum_depth, inverse_root(tap_new), big_roots[4])
    new_reduce = precondition(w_reduce, sum_reduce, big_roots[2], inverse_root(sq_new[0]))
    new_excite = precondition(w_excite, sum_excite, inverse_root(sq_new[1]), big_roots[3])
    new_project = precondition(w_project, sum_project, big_roots[1], inverse_root(in_new[1]))
    moments_new = DECAY * vector_moments + (1.0 - DECAY) * vector_grads * vector_grads
    vector_new = vector_params - VECTOR_RATE * vector_grads / (jnp.sqrt(moments_new) + 1e-08)
    return (
        output[:, :, None, :],
        input_back[:, :, None, :],
        sum_expand,
        sum_depth,
        sum_reduce,
        sum_excite,
        sum_project,
        new_expand,
        new_depth,
        new_reduce,
        new_excite,
        new_project,
        big_new,
        in_new,
        sq_new,
        tap_new,
        vector_grads,
        moments_new,
        vector_new,
    )


def solution(mesh):
    return jax.shard_map(
        on_device,
        mesh=mesh,
        in_specs=(
            P("dp", None, "space", None),
            P("dp", None, "space", None),
            P("dp", None),
            P(),
            P(),
            P(),
            P(),
            P(),
            P(),
            P(),
            P(),
            P(),
            P(),
            P(),
        ),
        out_specs=(
            P("dp", None, "space", None),
            P("dp", None, "space", None),
            P(),
            P(),
            P(),
            P(),
            P(),
            P(),
            P(),
            P(),
            P(),
            P(),
            P(),
            P(),
            P(),
            P(),
            P(),
            P(),
            P(),
        ),
        check_vma=False,
    )
```

profile of v0, /device:TPU:0, one launch (start us, length us, event | category | flops | bytes accessed | tf_op | source)
XLA Modules:
  0.0 1109.7 jit_solution(2955053200679656732)
XLA Ops:
  8.2 6.2 copy.103
  14.4 14.7 %fusion.963 = (f32[144]{0:T(256)S(1)}, f32[32,48,8,144]{3,2,1,0:T(8,128)}) fusion(f32[24,144]{1,0:T(8,128)} %param.17, f32[32,24,1,384]{1,3,0,2:T(8,128)} %copy.103), kind=kOutput, calls=%fused_computation.1139 | convolution fusion | flops 511377280 | bytes 8271936 | tf_op jit(solution)/shard_map/sic,ie->sce/dot_general | solution.py:171
  29.1 42.0 %psum.154 = f32[1,1,1,144]{3,2,1,0:T(1,128)S(1)} all-reduce(f32[1,1,1,144]{3,2,1,0:T(1,128)S(1)} %bitcast.639), channel_id=1, replica_groups=mesh['dp'=8,'space'=4] {'dp','space'}, use_global_device_ids=true, to_apply=%region_1.2 | all-reduce | flops 144 | bytes 1152 | tf_op jit(solution)/shard_map/psum | solution.py:84
  71.1 6.2 multiply_reduce_fusion.12
  77.3 40.2 %psum.155 = f32[1,1,1,144]{3,2,1,0:T(1,128)S(1)} all-reduce(f32[1,1,1,144]{3,2,1,0:T(1,128)S(1)} %bitcast.642), channel_id=1, replica_groups=mesh['dp'=8,'space'=4] {'dp','space'}, use_global_device_ids=true, to_apply=%region_3.4 | all-reduce | flops 144 | bytes 1152 | tf_op jit(solution)/shard_map/psum | solution.py:87
  118.0 6.9 fusion.34
  125.0 4.3 collective-permute-start
  129.4 1.3 collective-permute-start.1
  130.7 3.4 collective-permute-done
  134.0 4.1 collective-permute-done.1
  138.1 3.6 pad_maximum_fusion.11
  141.7 1.4 collective-permute-start.2
  143.3 1.4 fusion.961
  144.7 1.5 collective-permute-start.3
  146.4 1.1 broadcast_multiply_fusion.3
  147.6 2.8 collective-permute-done.3
  150.3 1.1 broadcast_multiply_fusion.1
  151.5 28.4 %maximum_maximum_fusion = (f32[32,50,9,144]{3,2,1,0:T(8,128)}, f32[32,50,9,144]{3,2,1,0:T(8,128)}) fusion(f32[32,1,8,144]{3,2,1,0:T(8,128)S(1)} %collective-permute-done.1, f32[32,48,8,144]{3,2,1,0:T(8,128)} %copy-done, f32[32,1,8,144]{3,2,1,0:T(8,128)S(1)} %collective-permute-done, f32[32,50,1,144]{3,2,1,0:T(1,128)S(1)} %broadcast_multiply_fusion.3, ...), kind=kLoop, calls=%fused_computation | loop fusion | flops 12441600 | bytes 25804800 | tf_op jit(solution)/shard_map/concatenate | solution.py:113
  180.0 52.1 %fusion.956 = (f32[144]{0:T(256)S(1)}, f32[32,48,8,144]{3,2,1,0:T(8,128)}) fusion(f32[32,50,9,144]{3,2,1,0:T(8,128)} %get-tuple-element.147, f32[144]{0:T(256)S(1)} %bitcast.631, f32[32,1,8,144]{3,2,1,0:T(8,128)S(1)} %collective-permute-done.1, f32[32,48,8,144]{3,2,1,0:T(8,128)} %copy-done, f32[144]{0:T(256)S(1)} %bitcast.617, f32[32,48]{1,0:T(8,128)S(1)} %fusion.193, ...), kind=kLoop, calls=%fused_computation.1133 | loop fusion | flops 42467184 | bytes 56936064 | tf_op jit(solution)/shard_map/reduce_sum | solution.py:84
  232.1 54.3 %psum.156 = f32[1,1,1,144]{3,2,1,0:T(1,128)S(1)} all-reduce(f32[1,1,1,144]{3,2,1,0:T(1,128)S(1)} %bitcast.654), channel_id=1, replica_groups=mesh['dp'=8,'space'=4] {'dp','space'}, use_global_device_ids=true, to_apply=%region_5.6 | all-reduce | flops 144 | bytes 1152 | tf_op jit(solution)/shard_map/psum | solution.py:84
  286.4 6.2 multiply_reduce_fusion.11
  292.7 41.1 %psum.157 = f32[1,1,1,144]{3,2,1,0:T(1,128)S(1)} all-reduce(f32[1,1,1,144]{3,2,1,0:T(1,128)S(1)} %bitcast.643), channel_id=1, replica_groups=mesh['dp'=8,'space'=4] {'dp','space'}, use_global_device_ids=true, to_apply=%region_7.8 | all-reduce | flops 144 | bytes 1152 | tf_op jit(solution)/shard_map/psum | solution.py:87
  334.4 16.2 %fusion.954 = (f32[32,48,144]{2,1,0:T(8,128)S(1)}, f32[32,48,8,144]{3,2,1,0:T(8,128)}) fusion(f32[144]{0:T(256)S(1)} %get-tuple-element.168, f32[144]{0:T(256)S(1)} %get-tuple-element.169, f32[144]{0:T(256)S(1)} %bitcast.612, f32[32,48,8,144]{3,2,1,0:T(8,128)} %get-tuple-element.139, f32[144]{0:T(256)S(1)} %bitcast.607), kind=kLoop, calls=%fused_computation.1132 | loop fusion | flops 15704064 | bytes 15042816 | tf_op jit(solution)/shard_map/sfbe,sfr->sre/reduce_sum | solution.py:192
  352.8 1.4 reduce_sum.349
  354.1 29.4 %all-reduce.9.cloned.1.call-done = f32[32,4,144]{2,0,1:T(8,128)} async-done(((f32[32,4,144]{2,0,1:T(8,128)}), f32[32,4,144]{2,0,1:T(8,128)}) %all-reduce.9.cloned.1.call-update) | async-done | bytes 73744 | tf_op jit(solution)/shard_map/psum | solution.py:191
  383.6 1.3 convolution_add_fusion.1
  386.2 1.2 copy-done.4
  387.3 14.8 %fusion.964 = (f32[24]{0:T(128)}, f32[32,384,24]{1,2,0:T(8,128)S(1)}) fusion(f32[144,24]{0,1:T(8,128)} %param.21, f32[32,48,8,144]{3,2,1,0:T(8,128)} %get-tuple-element.137, f32[32,48,144]{2,1,0:T(8,128)S(1)} %fusion.101), kind=kOutput, calls=%fused_computation.1140 | convolution fusion | flops 511672288 | bytes 9156192 | tf_op jit(solution)/shard_map/sce,eo->soc/dot_general | solution.py:198
  402.2 39.7 %psum.159 = f32[1,24,1]{1,2,0:T(1,128)} all-reduce(f32[1,24,1]{1,2,0:T(1,128)} %bitcast.656), channel_id=1, replica_groups=mesh['dp'=8,'space'=4] {'dp','space'}, use_global_device_ids=true, to_apply=%region_12.13 | all-reduce | flops 24 | bytes 192 | tf_op jit(solution)/shard_map/psum | solution.py:84
  443.9 41.4 %psum.160 = f32[1,24,1]{1,2,0:T(1,128)} all-reduce(f32[1,24,1]{1,2,0:T(1,128)} %bitcast.658), channel_id=1, replica_groups=mesh['dp'=8,'space'=4] {'dp','space'}, use_global_device_ids=true, to_apply=%region_14.15 | all-reduce | flops 24 | bytes 192 | tf_op jit(solution)/shard_map/psum | solution.py:87
  485.3 1.3 fusion.612
  487.2 2.6 fusion.52
  489.8 39.6 %all-reduce.4 = (f32[24]{0:T(128)}, f32[1,24,1]{1,2,0:T(1,128)}) all-reduce(f32[24]{0:T(128)} %get-tuple-element.154, f32[1,24,1]{1,2,0:T(1,128)} %bitcast.657), channel_id=1, replica_groups=mesh['dp'=8,'space'=4] {'dp','space'}, use_global_device_ids=true, to_apply=%region_18.19 | all-reduce | flops 48 | bytes 384 | tf_op jit(solution)/shard_map/psum | solution.py:94
  530.0 17.8 %fusion.23 = (f32[32,48,144]{2,1,0:T(8,128)S(1)}, f32[32,384,144]{2,1,0:T(8,128)}) fusion(f32[32,48,8,144]{3,2,1,0:T(8,128)} %get-tuple-element.137, f32[144,24]{0,1:T(8,128)} %param.21, f32[32,24,1,384]{3,2,1,0:T(1,128)S(1)} %copy-done.3, f32[32,384,24]{1,2,0:T(8,128)S(1)} %get-tuple-element.181, f32[24]{0:T(128)} %get-tuple-element.129, ...), kind=kOutput, calls=%fused_computation.39 | convolution fusion | flops 514990080 | bytes 17414112 | tf_op jit(solution)/shard_map/soc,eo->sce/dot_general | solution.py:207
  549.7 31.9 %all-reduce.11.cloned.1.call-done = f32[32,4,144]{2,0,1:T(8,128)} async-done(((f32[32,4,144]{2,0,1:T(8,128)}), f32[32,4,144]{2,0,1:T(8,128)}) %all-reduce.11.cloned.1.call-update) | async-done | bytes 73744 | tf_op jit(solution)/shard_map/psum | solution.py:210
  581.6 2.0 fusion.965
  585.5 18.3 %fusion.950 = (f32[144]{0:T(256)}, f32[144]{0:T(256)}, f32[32,48,8,144]{3,2,1,0:T(8,128)}) fusion(f32[144]{0:T(256)} %bitcast.613, f32[32,48,8,144]{3,2,1,0:T(8,128)} %get-tuple-element.139, f32[144]{0:T(256)} %bitcast.608, f32[144]{0:T(256)} %copy-done.80, f32[144]{0:T(256)} %copy-done.55, f32[32,48,144]{2,1,0:T(8,128)S(1)} %fusion.99, ...), kind=kLoop, calls=%fused_computation.1131 | loop fusion | flops 30080736 | bytes 23006592 | tf_op jit(solution)/shard_map/reduce_sum | solution.py:96
  603.8 39.8 %all-reduce.3 = (f32[144]{0:T(256)}, f32[1,1,1,144]{3,2,1,0:T(1,128)}) all-reduce(f32[144]{0:T(256)} %get-tuple-element.113, f32[1,1,1,144]{3,2,1,0:T(1,128)} %bitcast.638), channel_id=1, replica_groups=mesh['dp'=8,'space'=4] {'dp','space'}, use_global_device_ids=true, to_apply=%region_24.25 | all-reduce | flops 288 | bytes 2304 | tf_op jit(solution)/shard_map/psum | solution.py:94
  644.3 59.8 %multiply_reduce_fusion.1 = (f32[144]{0:T(256)}, f32[144]{0:T(256)}, f32[144]{0:T(256)}, f32[144]{0:T(256)}, f32[144]{0:T(256)}, /*index=5*/f32[144]{0:T(256)}, ...) fusion(f32[32,1,8,144]{3,2,1,0:T(8,128)} %copy-done.9, f32[32,48,8,144]{3,2,1,0:T(8,128)} %copy-done, ...), kind=kLoop, calls=%fused_computation.51 | loop fusion | flops 58391280 | bytes 71094144 | tf_op jit(solution)/shard_map/reduce_sum | solution.py:237
  704.2 1.2 fusion.958
  705.4 4.7 collective-permute-start.4
  710.1 1.3 collective-permute-start.5
  711.5 10.5 fusion.67
  722.2 2.2 copy.91
  724.4 3.6 pad_maximum_fusion.8
  728.1 1.3 collective-permute-start.6
  730.9 4.6 collective-permute-start.7
  736.0 1.2 stack.75
  738.1 2.6 broadcast_multiply_fusion
  740.7 2.6 broadcast_multiply_fusion.2
  743.4 29.5 %pad_maximum_fusion.1 = (f32[32,50,9,144]{3,2,1,0:T(8,128)}, f32[32,50,9,144]{3,2,1,0:T(8,128)}) fusion(f32[32,50,1,144]{3,2,1,0:T(1,128)S(1)} %broadcast_multiply_fusion, f32[32,1,8,144]{3,2,1,0:T(8,128)} %copy-done.12, f32[32,48,8,144]{3,2,1,0:T(8,128)} %get-tuple-element.133, f32[32,1,8,144]{3,2,1,0:T(8,128)} %copy-done.10, ...), kind=kLoop, calls=%fused_computation.2 | loop fusion | flops 12441600 | bytes 25804800 | tf_op jit(solution)/shard_map/concatenate | solution.py:113
  773.1 56.9 %fusion.949 = (f32[144]{0:T(256)S(1)}, f32[144]{0:T(256)S(1)}, f32[32,48,8,144]{3,2,1,0:T(8,128)}) fusion(f32[144]{0:T(256)S(1)} %bitcast.603, f32[32,48,8,144]{3,2,1,0:T(8,128)} %get-tuple-element.179, f32[144]{0:T(256)S(1)} %bitcast.599, f32[144]{0:T(256)S(1)} %copy-done.61, f32[144]{0:T(256)S(1)} %copy-done.54, ...), kind=kLoop, calls=%fused_computation.1130 | loop fusion | flops 67239648 | bytes 64016832 | tf_op jit(solution)/shard_map/reduce_sum | solution.py:96
  830.0 55.0 %all-reduce.2 = (f32[144]{0:T(256)S(1)}, f32[1,1,1,144]{3,2,1,0:T(1,128)S(1)}) all-reduce(f32[144]{0:T(256)S(1)} %get-tuple-element.111, f32[1,1,1,144]{3,2,1,0:T(1,128)S(1)} %bitcast.637), channel_id=1, replica_groups=mesh['dp'=8,'space'=4] {'dp','space'}, use_global_device_ids=true, to_apply=%region_28.29 | all-reduce | flops 288 | bytes 2304 | tf_op jit(solution)/shard_map/psum | solution.py:94
  885.0 17.7 %fusion.70 = f32[24,144]{1,0:T(8,128)} fusion(f32[32,24,1,384]{3,2,1,0:T(1,128)S(1)} %copy-done.6, f32[32,48,8,144]{3,2,1,0:T(8,128)} %get-tuple-element.134, f32[32,48,8,144]{3,2,1,0:T(8,128)} %get-tuple-element.179, f32[144]{0:T(256)S(1)} %get-tuple-element.125, f32[144]{0:T(256)S(1)} %bitcast.633, f32[144]{0:T(256)S(1)} %bitcast.635, ...), kind=kOutput, calls=%fused_computation.120 | convolution fusion | flops 521994240 | bytes 15352128 | tf_op jit(solution)/shard_map/sic,sce->ie/dot_general | solution.py:251
  902.9 16.6 %fusion.47 = f32[32,24,1,384]{3,1,0,2:T(8,128)S(1)} fusion(f32[32,48,8,144]{3,2,1,0:T(8,128)S(1)} %copy-done.2, f32[32,48,8,144]{3,2,1,0:T(8,128)} %get-tuple-element.179, f32[144]{0:T(256)S(1)} %get-tuple-element.125, f32[144]{0:T(256)S(1)} %bitcast.634, f32[144]{0:T(256)S(1)} %bitcast.636, f32[144]{0:T(256)S(1)} %bitcast.605, f32[144]{0:T(256)S(1)} %bitcast.601, ...), kind=kOutput, calls=%fused_computation.87 | convolution fusion | flops 522289152 | bytes 16531776 | tf_op jit(solution)/shard_map/sce,ie->sic/dot_general | solution.py:252
  919.6 40.9 %all-reduce.1 = (f32[24,144]{1,0:T(8,128)S(1)}, f32[9,144]{1,0:T(8,128)S(1)}, f32[144,6]{0,1:T(8,128)S(1)}, f32[6,144]{1,0:T(8,128)S(1)}, f32[144,24]{0,1:T(8,128)S(1)}, /*index=5*/f32[6]{0:T(128)S(1)}, f32[144]{0:T(256)S(1)}) all-reduce(f32[24,144]{1,0:T(8,128)S(1)} %copy-done.33, ...), channel_id=1, replica_groups=mesh['dp'=8,'space'=4] {'dp','space'}, use_global_device_ids=true, to_apply=%region_29.30 | all-reduce | flops 10086 | bytes 80688 | tf_op jit(solution)/shard_map/psum | solution.py:255
  970.2 2.2 copy.92
  1011.0 1.0 broadcast_multiply_fusion.4
  1013.4 73.7 %all-reduce.13.cloned.1.call-done = f32[5,144,144]{2,1,0:T(8,128)} async-done(((f32[5,144,144]{2,1,0:T(8,128)}), f32[5,144,144]{2,1,0:T(8,128)}) %all-reduce.13.cloned.1.call-update) | async-done | bytes 414736 | tf_op jit(solution)/shard_map/psum | solution.py:304
  1087.1 1.7 multiply_reduce_fusion.20
  1089.5 1.7 multiply_reduce_fusion.17
  1091.9 1.7 multiply_reduce_fusion.16
  1094.3 1.2 fusion.85
  1097.0 1.1 fusion.87
  (526 shorter events, 65.4 us)
Async XLA Ops:
  7.2 376.4 %all-reduce.9.cloned.1.call-start = ((), (), s32[]{:S(2)}) async-start(), calls=%async_computation | async-start | bytes 262144 | tf_op jit(solution)/shard_map/psum | solution.py:191
  8.2 109.8 %copy-start.53 = (f32[144]{0:T(256)}, f32[144]{0:T(256)S(1)}, u32[]{:S(2)}) copy-start(f32[144]{0:T(256)S(1)} %get-tuple-element.171) | copy-start | bytes 1732
  8.2 109.8 %copy-start.60 = (f32[144]{0:T(256)}, f32[144]{0:T(256)S(1)}, u32[]{:S(2)}) copy-start(f32[144]{0:T(256)S(1)} %get-tuple-element.170) | copy-start | bytes 1732
  8.2 326.1 %copy-start.55 = (f32[144]{0:T(256)}, f32[144]{0:T(256)S(1)}, u32[]{:S(2)}) copy-start(f32[144]{0:T(256)S(1)} %get-tuple-element.169) | copy-start | bytes 1732
  8.2 326.1 %copy-start.80 = (f32[144]{0:T(256)}, f32[144]{0:T(256)S(1)}, u32[]{:S(2)}) copy-start(f32[144]{0:T(256)S(1)} %get-tuple-element.168) | copy-start | bytes 1732
  71.1 53.9 %copy-start.41 = (f32[1,1,1,144]{3,2,1,0:T(1,128)}, f32[1,1,1,144]{3,2,1,0:T(1,128)S(1)}, u32[]{:S(2)}) copy-start(f32[1,1,1,144]{3,2,1,0:T(1,128)S(1)} %broadcast_multiply_fusion.10) | copy-start | bytes 1732
  125.0 9.0 collective-permute-start
  129.4 8.8 collective-permute-start.1
  134.0 45.9 %copy-start.8 = (f32[32,1,8,144]{3,2,1,0:T(8,128)}, f32[32,1,8,144]{3,2,1,0:T(8,128)S(1)}, u32[]{:S(2)}) copy-start(f32[32,1,8,144]{3,2,1,0:T(8,128)S(1)} %collective-permute-done) | copy-start | bytes 442372
  138.1 41.7 %copy-start.9 = (f32[32,1,8,144]{3,2,1,0:T(8,128)}, f32[32,1,8,144]{3,2,1,0:T(8,128)S(1)}, u32[]{:S(2)}) copy-start(f32[32,1,8,144]{3,2,1,0:T(8,128)S(1)} %collective-permute-done.1) | copy-start | bytes 442372
  141.7 4.7 collective-permute-start.2
  144.6 35.2 %copy-start.62 = (f32[1,144]{1,0:T(1,128)}, f32[1,144]{1,0:T(1,128)S(1)}, u32[]{:S(2)}) copy-start(f32[1,144]{1,0:T(1,128)S(1)} %get-tuple-element.156) | copy-start | bytes 1732
  144.7 35.2 %copy-start.64 = (f32[1,144]{1,0:T(1,128)}, f32[1,144]{1,0:T(1,128)S(1)}, u32[]{:S(2)}) copy-start(f32[1,144]{1,0:T(1,128)S(1)} %get-tuple-element.157) | copy-start | bytes 1732
  144.7 35.2 %copy-start.66 = (f32[1,144]{1,0:T(1,128)}, f32[1,144]{1,0:T(1,128)S(1)}, u32[]{:S(2)}) copy-start(f32[1,144]{1,0:T(1,128)S(1)} %get-tuple-element.158) | copy-start | bytes 1732
  144.7 35.2 %copy-start.68 = (f32[1,144]{1,0:T(1,128)}, f32[1,144]{1,0:T(1,128)S(1)}, u32[]{:S(2)}) copy-start(f32[1,144]{1,0:T(1,128)S(1)} %get-tuple-element.159) | copy-start | bytes 1732
  144.7 35.2 %copy-start.70 = (f32[1,144]{1,0:T(1,128)}, f32[1,144]{1,0:T(1,128)S(1)}, u32[]{:S(2)}) copy-start(f32[1,144]{1,0:T(1,128)S(1)} %get-tuple-element.160) | copy-start | bytes 1732
  144.7 35.2 %copy-start.72 = (f32[1,144]{1,0:T(1,128)}, f32[1,144]{1,0:T(1,128)S(1)}, u32[]{:S(2)}) copy-start(f32[1,144]{1,0:T(1,128)S(1)} %get-tuple-element.161) | copy-start | bytes 1732
  144.7 35.2 %copy-start.74 = (f32[1,144]{1,0:T(1,128)}, f32[1,144]{1,0:T(1,128)S(1)}, u32[]{:S(2)}) copy-start(f32[1,144]{1,0:T(1,128)S(1)} %get-tuple-element.162) | copy-start | bytes 1732
  144.7 35.2 %copy-start.76 = (f32[1,144]{1,0:T(1,128)}, f32[1,144]{1,0:T(1,128)S(1)}, u32[]{:S(2)}) copy-start(f32[1,144]{1,0:T(1,128)S(1)} %get-tuple-element.163) | copy-start | bytes 1732
  144.7 35.2 %copy-start.78 = (f32[1,144]{1,0:T(1,128)}, f32[1,144]{1,0:T(1,128)S(1)}, u32[]{:S(2)}) copy-start(f32[1,144]{1,0:T(1,128)S(1)} %get-tuple-element.164) | copy-start | bytes 1732
  144.7 5.6 collective-permute-start.3
  286.4 64.2 %copy-start.51 = (f32[1,1,1,144]{3,2,1,0:T(1,128)}, f32[1,1,1,144]{3,2,1,0:T(1,128)S(1)}, u32[]{:S(2)}) copy-start(f32[1,1,1,144]{3,2,1,0:T(1,128)S(1)} %broadcast_multiply_fusion.9) | copy-start | bytes 1732
  334.3 49.2 %copy-start.88 = (f32[144,6]{0,1:T(8,128)S(1)}, f32[144,6]{0,1:T(8,128)}, u32[]{:S(2)}) copy-start(f32[144,6]{0,1:T(8,128)} %param.19) | copy-start | bytes 10372
  334.3 50.6 %copy-start.44 = (f32[6,144]{1,0:T(8,128)S(1)}, f32[6,144]{1,0:T(8,128)}, u32[]{:S(2)}) copy-start(f32[6,144]{1,0:T(8,128)} %param.20) | copy-start | bytes 10372
  350.6 136.6 %copy-start.6 = (f32[32,24,1,384]{3,2,1,0:T(1,128)S(1)}, f32[32,24,1,384]{3,2,1,0:T(1,128)}, u32[]{:S(2)}) copy-start(f32[32,24,1,384]{3,2,1,0:T(1,128)} %param.14) | copy-start | bytes 3538948
  351.9 229.7 %all-reduce.11.cloned.1.call-start = ((), (), s32[]{:S(2)}) async-start(), calls=%async_computation.1 | async-start | bytes 262144 | tf_op jit(solution)/shard_map/psum | solution.py:210
  549.1 538.1 %all-reduce.13.cloned.1.call-start = ((), (), s32[]{:S(2)}) async-start(), calls=%async_computation.2 | async-start | bytes 1474560 | tf_op jit(solution)/shard_map/psum | solution.py:304
  585.5 58.8 %copy-start.24 = (f32[32,48]{1,0:T(8,128)S(1)}, f32[32,48]{1,0:T(8,128)}, u32[]{:S(2)}) copy-start(f32[32,48]{1,0:T(8,128)} %copy-done.23) | copy-start | bytes 18436
  644.3 67.1 %copy-start.5 = (f32[32,48,144]{2,1,0:T(8,128)S(1)}, f32[32,48,144]{2,1,0:T(8,128)}, u32[]{:S(2)}) copy-start(f32[32,48,144]{2,1,0:T(8,128)} %copy-done.4) | copy-start | bytes 2654212
  644.3 67.1 %copy-start.84 = (f32[24]{0:T(128)S(1)}, f32[24]{0:T(128)}, u32[]{:S(2)}) copy-start(f32[24]{0:T(128)} %copy-done.83) | copy-start | bytes 292
  644.3 67.1 %copy-start.86 = (f32[24]{0:T(128)S(1)}, f32[24]{0:T(128)}, u32[]{:S(2)}) copy-start(f32[24]{0:T(128)} %copy-done.85) | copy-start | bytes 292
  644.3 67.2 %copy-start.92 = (f32[24]{0:T(128)S(1)}, f32[24]{0:T(128)}, u32[]{:S(2)}) copy-start(f32[24]{0:T(128)} %get-tuple-element.176) | copy-start | bytes 292
  644.3 67.2 %copy-start.93 = (f32[24]{0:T(128)S(1)}, f32[24]{0:T(128)}, u32[]{:S(2)}) copy-start(f32[24]{0:T(128)} %get-tuple-element.129) | copy-start | bytes 292
  644.3 67.2 %copy-start.109 = (f32[24]{0:T(128)S(1)}, f32[24]{0:T(128)}, u32[]{:S(2)}) copy-start(f32[24]{0:T(128)} %copy-done.108) | copy-start | bytes 292
  705.4 19.0 %collective-permute-start.4 = (f32[32,1,8,144]{3,2,1,0:T(8,128)S(1)}, f32[32,1,8,144]{3,2,1,0:T(8,128)S(1)}, u32[]{:S(2)}, u32[]{:S(2)}) collective-permute-start(f32[32,1,8,144]{3,2,1,0:T(8,128)S(1)} %get-tuple-element.150), channel_id=1, source_target_pairs={{0,2},{1,3},{4,6},{5,7},{8,10},{9,11},{12,14},{13,15},{16,18},{17,... | collective-permute-start | bytes 442376 | tf_op jit(solution)/shard_map/ppermute | solution.py:27
  710.1 14.3 %collective-permute-start.5 = (f32[32,1,8,144]{3,2,1,0:T(8,128)S(1)}, f32[32,1,8,144]{3,2,1,0:T(8,128)S(1)}, u32[]{:S(2)}, u32[]{:S(2)}) collective-permute-start(f32[32,1,8,144]{3,2,1,0:T(8,128)S(1)} %get-tuple-element.151), channel_id=1, source_target_pairs={{2,0},{3,1},{6,4},{7,5},{10,8},{11,9},{14,12},{15,13},{18,16},{19,... | collective-permute-start | bytes 442376 | tf_op jit(solution)/shard_map/ppermute | solution.py:27
  728.1 10.1 collective-permute-start.6
  730.9 9.8 collective-permute-start.7
  773.1 111.9 %copy-start.81 = (f32[1,1,1,144]{3,2,1,0:T(1,128)S(1)}, f32[1,1,1,144]{3,2,1,0:T(1,128)}, u32[]{:S(2)}) copy-start(f32[1,1,1,144]{3,2,1,0:T(1,128)} %get-tuple-element.172) | copy-start | bytes 1732
  902.9 57.9 %copy-start.91 = (f32[2,6,6]{2,0,1:T(2,128)S(1)}, f32[2,6,6]{2,0,1:T(2,128)}, u32[]{:S(2)}) copy-start(f32[2,6,6]{2,0,1:T(2,128)} %param.26) | copy-start | bytes 868
  902.9 61.2 %copy-start.52 = (f32[2,24,24]{2,1,0:T(8,128)S(1)}, f32[2,24,24]{2,1,0:T(8,128)}, u32[]{:S(2)}) copy-start(f32[2,24,24]{2,1,0:T(8,128)} %param.25) | copy-start | bytes 13828
  902.9 65.4 %copy-start.18 = (f32[5,144,144]{2,1,0:T(8,128)S(1)}, f32[5,144,144]{2,1,0:T(8,128)}, u32[]{:S(2)}) copy-start(f32[5,144,144]{2,1,0:T(8,128)} %param.24) | copy-start | bytes 1244164
  902.9 79.5 %copy-start.87 = (f32[9,9]{1,0:T(8,128)S(1)}, f32[9,9]{1,0:T(8,128)}, u32[]{:S(2)}) copy-start(f32[9,9]{1,0:T(8,128)} %param.27) | copy-start | bytes 976
  960.5 51.6 %copy-start.21 = (f32[9,144]{1,0:T(8,128)}, f32[9,144]{1,0:T(8,128)S(1)}, u32[]{:S(2)}) copy-start(f32[9,144]{1,0:T(8,128)S(1)} %get-tuple-element.119) | copy-start | bytes 15556
  960.5 51.6 %copy-start.31 = (f32[6,144]{1,0:T(8,128)}, f32[6,144]{1,0:T(8,128)S(1)}, u32[]{:S(2)}) copy-start(f32[6,144]{1,0:T(8,128)S(1)} %get-tuple-element.121) | copy-start | bytes 10372
  960.5 52.8 %copy-start.20 = (f32[24,144]{1,0:T(8,128)}, f32[24,144]{1,0:T(8,128)S(1)}, u32[]{:S(2)}) copy-start(f32[24,144]{1,0:T(8,128)S(1)} %get-tuple-element.118) | copy-start | bytes 41476
  960.5 133.8 %copy-start.19 = (f32[144,24]{0,1:T(8,128)}, f32[144,24]{0,1:T(8,128)S(1)}, u32[]{:S(2)}) copy-start(f32[144,24]{0,1:T(8,128)S(1)} %get-tuple-element.122) | copy-start | bytes 41476
  960.5 136.5 %copy-start.30 = (f32[144,6]{0,1:T(8,128)}, f32[144,6]{0,1:T(8,128)S(1)}, u32[]{:S(2)}) copy-start(f32[144,6]{0,1:T(8,128)S(1)} %get-tuple-element.120) | copy-start | bytes 10372
  960.5 50.4 %copy-start.112 = (f32[5]{0:T(128)S(1)}, f32[5]{0:T(128)}, u32[]{:S(2)}) copy-start(f32[5]{0:T(128)} %compare_convert_fusion) | copy-start | bytes 64
  964.1 47.9 %copy-start.22 = (f32[2,24,24]{2,1,0:T(8,128)}, f32[2,24,24]{2,1,0:T(8,128)S(1)}, u32[]{:S(2)}) copy-start(f32[2,24,24]{2,1,0:T(8,128)S(1)} %fusion.183) | copy-start | bytes 13828
  968.3 43.8 %copy-start.94 = (f32[24]{0:T(128)S(1)}, f32[24]{0:T(128)}, u32[]{:S(2)}) copy-start(f32[24]{0:T(128)} %get-tuple-element.129) | copy-start | bytes 292
  968.3 43.8 %copy-start.96 = (f32[1,1,1,144]{3,2,1,0:T(1,128)S(1)}, f32[1,1,1,144]{3,2,1,0:T(1,128)}, u32[]{:S(2)}) copy-start(f32[1,1,1,144]{3,2,1,0:T(1,128)} %get-tuple-element.128) | copy-start | bytes 1732
  968.3 43.8 %copy-start.107 = (f32[144]{0:T(256)S(1)}, f32[144]{0:T(256)}, u32[]{:S(2)}) copy-start(f32[144]{0:T(256)} %get-tuple-element.127) | copy-start | bytes 1732
  968.3 43.8 %copy-start.115 = (f32[1,24,1]{1,2,0:T(1,128)S(1)}, f32[1,24,1]{1,2,0:T(1,128)}, u32[]{:S(2)}) copy-start(f32[1,24,1]{1,2,0:T(1,128)} %get-tuple-element.130) | copy-start | bytes 292
  968.3 43.9 %copy-start.47 = (f32[774]{0:T(1024)S(1)}, f32[774]{0:T(1024)}, u32[]{:S(2)}) copy-start(f32[774]{0:T(1024)} %param.22) | copy-start | bytes 9292
  968.3 43.9 %copy-start.95 = (f32[774]{0:T(1024)S(1)}, f32[774]{0:T(1024)}, u32[]{:S(2)}) copy-start(f32[774]{0:T(1024)} %param.23) | copy-start | bytes 9292
  968.4 134.3 %copy-start.16 = (f32[5,144,144]{2,1,0:T(8,128)}, f32[5,144,144]{2,1,0:T(8,128)S(1)}, u32[]{:S(2)}) copy-start(f32[5,144,144]{2,1,0:T(8,128)S(1)} %multiply_add_fusion.3) | copy-start | bytes 1244164
  968.5 131.2 %copy-start.45 = (f32[6,144]{1,0:T(8,128)S(1)}, f32[6,144]{1,0:T(8,128)}, u32[]{:S(2)}) copy-start(f32[6,144]{1,0:T(8,128)} %param.20) | copy-start | bytes 10372
  968.5 131.8 %copy-start.40 = (f32[9,144]{1,0:T(8,128)S(1)}, f32[9,144]{1,0:T(8,128)}, u32[]{:S(2)}) copy-start(f32[9,144]{1,0:T(8,128)} %param.18) | copy-start | bytes 15556
  968.5 132.4 %copy-start.28 = (f32[24,144]{1,0:T(8,128)S(1)}, f32[24,144]{1,0:T(8,128)}, u32[]{:S(2)}) copy-start(f32[24,144]{1,0:T(8,128)} %param.17) | copy-start | bytes 41476
  968.5 133.0 %copy-start.89 = (f32[144,6]{0,1:T(8,128)S(1)}, f32[144,6]{0,1:T(8,128)}, u32[]{:S(2)}) copy-start(f32[144,6]{0,1:T(8,128)} %param.19) | copy-start | bytes 10372
  968.5 133.6 %copy-start.29 = (f32[144,24]{0,1:T(8,128)S(1)}, f32[144,24]{0,1:T(8,128)}, u32[]{:S(2)}) copy-start(f32[144,24]{0,1:T(8,128)} %param.21) | copy-start | bytes 41476
  983.2 119.6 %copy-start.35 = (f32[9,9]{1,0:T(8,128)}, f32[9,9]{1,0:T(8,128)S(1)}, u32[]{:S(2)}) copy-start(f32[9,9]{1,0:T(8,128)S(1)} %get-tuple-element.189) | copy-start | bytes 976
  1012.2 90.5 %copy-start.58 = (f32[774]{0:T(1024)}, f32[774]{0:T(1024)S(1)}, u32[]{:S(2)}) copy-start(f32[774]{0:T(1024)S(1)} %concatenate.53) | copy-start | bytes 9292
  (64 other events, 1155.0 us)
Sparse Core Ops, SparseCore 0:
  352.1 31.4 all-reduce.8
  549.2 32.3 all-reduce.10
  1012.2 74.9 all-reduce.12
where the time goes:
time: 1120 us; the launch traced here: 1110 us
  blocking collectives  434 us (39%)
  other arithmetic  313 us (28%)
  matrix products  151 us (13%)
  waiting for transfers between devices  145 us (13%)
  between operations  24.8 us (2%)
  local copies, waits for them, and re-layouts  21.1 us (2%)
  starting transfers between devices  20.5 us (2%)
    psum x3, blocking collectives, moments(): lax.psum(jnp.sum(array, axis=axes, keepdims=True), ('dp', 'space'))  136 us
    psum x3, blocking collectives, norm_back(): lax.psum((jnp.sum(upstream, axis=axes, keepdims=True), jnp.sum(upstream *...  134 us
    psum x3, blocking collectives, moments(): lax.psum(jnp.sum(centered * centered, axis=axes, keepdims=True), ('dp', '...  123 us
    reduce_sum x3, other arithmetic, norm_back(): jnp.sum(upstream, axis=axes, keepdims=True)  76.5 us
    psum x1, waiting for transfers between devices, on_device(): lax.psum(slot_mask[:, None, None] * inverse_root(mine)[None], 'dp')  73.7 us
    reduce_sum x1, other arithmetic, on_device(): jnp.sum(back_mixed * window * matches[row_step + 1], axis=(0, 1, 2))  59.8 us
    concatenate x2, other arithmetic, extend(): return jnp.concatenate([left_edge, tall, right_edge], axis=2)  57.9 us
    reduce_sum x1, other arithmetic, moments(): jnp.sum(array, axis=axes, keepdims=True)  52.1 us
  transfers between devices with their start and end apart: 11, of which 6 were waited for; matrix products, arithmetic and copies ran while one was open for 2% of the time, Pallas kernels for 0%

commit v1 on v0

v1 whole, which is shorter than its diff:
```python
import functools
import math

import jax
import jax.numpy as jnp
from jax import lax
from jax.experimental import pallas as pl
from jax.experimental.pallas import tpu as pltpu
from jax.sharding import PartitionSpec as P

IN = 24
EXP = 144
SQZ = 6
TAPS = 9
FRAMES = 96
BINS = 16
REGIONS = 4
QUADS = 4
ROOT_ITERS = 10
NORM_EPS = 0.001
DECAY = 0.9
FRESH = 1.0 - DECAY
STEP_FRACTION = 0.5
VECTOR_RATE = 0.15

LANES = 128
HALF_W = 6
WIDE = 2 * HALF_W
ROWS = IN * 3
GROUP = 8
BULK = 16

F32 = jnp.float32
BF16 = jnp.bfloat16
FULL = lax.Precision.HIGHEST
MID = lax.Precision.HIGH
MESH = pl.DeviceIdType.MESH


def mm(left, right, dims, precision=None):
    return lax.dot_general(
        left, right, ((dims[:1], dims[1:]), ((), ())), precision=precision, preferred_element_type=F32
    )


def nn(left, right, precision=None):
    return mm(left, right, (1, 0), precision)


def nt(left, right, precision=None):
    return mm(left, right, (1, 1), precision)


def tn(left, right, precision=None):
    return mm(left, right, (0, 0), precision)


def halves(value):
    high = value.astype(BF16)
    return high, (value - high.astype(F32)).astype(BF16)


def column(rows, index, width):
    pick = (lax.broadcasted_iota(jnp.int32, (rows.shape[0], LANES), 0) == index).astype(F32)
    return tn(rows, pick, FULL)[:width]


def lane_sums(table):
    return nt(jnp.ones((8, table.shape[1]), F32), table, FULL)[0:1]


def split_row(row):
    return jnp.concatenate(
        [row[:, :LANES], jnp.concatenate([row[:, LANES:], jnp.zeros((1, 2 * LANES - EXP), F32)], axis=1)], axis=0
    )


def join_row(pair):
    return jnp.concatenate([pair[0:1], pair[1:2, : EXP - LANES]], axis=1)


def tile_quad(n):
    return 2 * ((n % HALF_W) // 3) + n // HALF_W


def on_lane(n):
    return pl.ds(n * LANES, LANES)


def block_kernel(
    n_dev, n_space, slots, n_pos,
    feat, cot, ids_ref, w_exp, w_dep, w_red_t, w_exc, w_pro_t, prm, big, in_st, sq_st, tap_st,
    out, ing, gs_out, nw_out, vr_out,
    xloc, xq, cq, xs, v1, a2, hh, dn2, dh, a3, hot, dcat, tab, msk, reg, acc, w1t, wlow,
    small, pooled, gates, dgate, bulk, bulk_in, bulk_all, rb1, rb, nws, fold,
    loc_sem, x_send, x_recv, c_send, c_recv, o_send, o_recv, g_send, g_recv,
    r_send, r_recv, own_sem,
):
    space = lax.axis_index("space")
    me = lax.axis_index("dp") * n_space + space
    n_loc = float(slots * FRAMES * BINS)
    total = float(n_pos)

    def device(index):
        return (lax.div(index, n_space), lax.rem(index, n_space))

    def peer(step):
        return lax.rem(space + step, QUADS)

    def space_device(step):
        return (lax.axis_index("dp"), peer(step))

    barrier = pltpu.get_barrier_semaphore()

    def greet(step, carry):
        pl.semaphore_signal(
            barrier, inc=1, device_id=device(lax.rem(me + step, n_dev)), device_id_type=MESH
        )
        return carry

    lax.fori_loop(1, n_dev, greet, 0)
    loads = [
        pltpu.make_async_copy(feat.at[pl.ds(slots * q, slots)], xloc.at[q], loc_sem.at[q]) for q in range(QUADS)
    ]
    for load in loads:
        load.start()
    own_x = pltpu.make_async_copy(feat.at[pl.ds(slots * space, slots)], xq.at[space], own_sem.at[0])
    own_c = pltpu.make_async_copy(cot.at[pl.ds(slots * space, slots)], cq.at[space], own_sem.at[1])
    own_x.start()
    own_c.start()

    lane = lax.broadcasted_iota(jnp.int32, (8, LANES), 1)
    low_bin = lax.rem(lane, 8) == 0
    high_bin = lax.rem(lane, 8) == 7
    first_row = lane < 8
    last_row = lane >= LANES - 8
    zero_tile = jnp.zeros((8, LANES), F32)

    half_lanes = HALF_W * LANES
    own_ids = ids_ref[pl.ds(pl.multiple_of(slots * space, 8), slots), :].astype(F32)
    spread = (
        lax.broadcasted_iota(jnp.int32, (FRAMES, half_lanes), 1) // 8
        == lax.broadcasted_iota(jnp.int32, (FRAMES, half_lanes), 0)
    )
    wide_ids = nn(own_ids.astype(BF16), spread.astype(F32).astype(BF16))
    wide_lane = lax.broadcasted_iota(jnp.int32, (slots, half_lanes), 1)
    before = pltpu.roll(wide_ids, 8, 1)
    after = pltpu.roll(wide_ids, half_lanes - 8, 1)
    from_ok = jnp.where((before == wide_ids) & (wide_lane >= 8), 1.0, 0.0)
    to_ok = jnp.where((after == wide_ids) & (wide_lane < half_lanes - 8), 1.0, 0.0)
    for s in range(slots):
        msk[0, s] = jnp.broadcast_to(from_ok[s : s + 1], (8, half_lanes))
        msk[1, s] = jnp.broadcast_to(to_ok[s : s + 1], (8, half_lanes))
        for r in range(REGIONS):
            reg[r, s] = jnp.broadcast_to((wide_ids[s : s + 1] == float(r)).astype(F32), (8, half_lanes))
    row_index = lax.broadcasted_iota(jnp.int32, (slots * REGIONS, half_lanes), 0)
    row_region = lax.rem(row_index, REGIONS).astype(F32)
    counts = jnp.zeros((slots * REGIONS, 1), F32)
    for s in range(slots):
        row = jnp.where(
            (lax.div(row_index, REGIONS) == s) & (wide_ids[s : s + 1] == row_region), 1.0, 0.0
        )
        counts = counts + 2.0 * jnp.sum(row, axis=1, keepdims=True)
        hot[s, :, :half_lanes] = row.astype(BF16)
        hot[s, :, half_lanes:] = row.astype(BF16)
    taps = w_dep[...]
    for t in range(TAPS):
        tab[t] = column(taps, t, EXP)

    for load in loads:
        load.wait()
    first = jnp.concatenate([xloc[0, 0, pl.ds(k, IN, stride=3), :] for k in range(3)], axis=1)
    shift_col = nn(first, jnp.ones((3 * LANES, LANES), F32), FULL) * (1.0 / (3 * LANES))
    shift_row = nt(jnp.ones((8, 3 * LANES), F32), first, FULL)[0:1] * (1.0 / (3 * LANES))
    one_rows = (lax.broadcasted_iota(jnp.int32, (8, LANES), 0) == 0).astype(F32)

    def gram_step(s, gram):
        parts = []
        for q in range(QUADS):
            for k in range(3):
                parts.append(
                    jnp.concatenate([xloc[q, s, pl.ds(k, IN, stride=3), :] - shift_col, one_rows], axis=0)
                )
        high, low = halves(jnp.concatenate(parts, axis=1))
        both = jnp.concatenate([high, low], axis=0)
        return gram + nt(both, both)

    gram = lax.fori_loop(0, slots, gram_step, jnp.zeros((64, 64), F32))
    gram = gram[:32, :32] + gram[32:, :32] + gram[:32, 32:] + gram[32:, 32:]
    off_row = gram[IN : IN + 1, :IN] * (1.0 / n_loc)
    off_col = gram[:IN, IN : IN + 1] * (1.0 / n_loc)
    local_m2 = gram[:IN, :IN] - n_loc * off_col * off_row
    fold[...] = jnp.zeros((IN, LANES), F32)
    fold[:, :IN] = local_m2
    packed = jnp.zeros((6, LANES), F32)
    for g in range(4):
        piece = fold[pl.ds(g, 6, stride=4), :]
        packed = packed + (pltpu.roll(piece, 32 * g, 1) if g else piece)
    rb1[me, 0:6, :] = packed
    rb1[me, 6:7, :] = jnp.concatenate([shift_row + off_row, jnp.zeros((1, LANES - IN), F32)], axis=1)
    rb1[me, 7:8, :] = jnp.zeros((1, LANES), F32)

    pl.semaphore_wait(barrier, n_dev - 1)

    def spread_start(source, target, index):
        def send(step, carry):
            pltpu.make_async_remote_copy(
                src_ref=source, dst_ref=target, send_sem=r_send.at[index], recv_sem=r_recv.at[index],
                device_id=device(lax.rem(me + step, n_dev)), device_id_type=MESH,
            ).start()
            return carry

        lax.fori_loop(1, n_dev, send, 0)

    def spread_wait(window, index):
        done = pltpu.make_async_remote_copy(
            src_ref=window, dst_ref=window, send_sem=r_send.at[index], recv_sem=r_recv.at[index],
            device_id=device(me), device_id_type=MESH,
        )
        done.wait_send()
        done.wait_recv()

    def quad_copy(source, target, send, recv, step, s):
        return pltpu.make_async_remote_copy(
            src_ref=source, dst_ref=target, send_sem=send.at[step, s], recv_sem=recv.at[step, s],
            device_id=space_device(step), device_id_type=MESH,
        )

    def x_copy(step, s):
        return quad_copy(feat.at[slots * peer(step) + s], xq.at[space, s], x_send, x_recv, step, s)

    def c_copy(step, s):
        return quad_copy(cot.at[slots * peer(step) + s], cq.at[space, s], c_send, c_recv, step, s)

    def o_copy(step, s):
        return quad_copy(xloc.at[peer(step), s], out.at[slots * space + s], o_send, o_recv, step, s)

    def g_copy(step, s):
        return quad_copy(xq.at[peer(step), s], ing.at[slots * space + s], g_send, g_recv, step, s)

    spread_start(rb1.at[me], rb1.at[me], 0)

    def x_start(s, carry):
        for step in range(1, QUADS):
            x_copy(step, s).start()
        return carry

    lax.fori_loop(0, slots, x_start, 0)

    spread_wait(rb1.at[pl.ds(0, n_dev - 1)], 0)
    gathered = jnp.sum(rb1[...], axis=0)
    means = rb1[:, 6, :]
    mean_row = jnp.sum(means, axis=0, keepdims=True) * (1.0 / n_dev)
    apart = means - mean_row
    between = tn(apart, apart, FULL)[:IN, :IN]
    for g in range(4):
        piece = gathered[0:6]
        piece = pltpu.roll(piece, LANES - 32 * g, 1) if g else piece
        fold[pl.ds(g, 6, stride=4), :] = piece
    moment = fold[:, :IN] + n_loc * between
    eye24 = (
        lax.broadcasted_iota(jnp.int32, (IN, IN), 0) == lax.broadcasted_iota(jnp.int32, (IN, IN), 1)
    )
    mean_col = nn(jnp.where(eye24, mean_row[:, :IN], 0.0), jnp.ones((IN, LANES), F32), FULL)
    weight = w_exp[...]
    moment_w = nn(moment, weight, FULL)
    scale1 = lax.rsqrt(jnp.sum(moment_w * weight, axis=0, keepdims=True) * (1.0 / total) + NORM_EPS)
    grow1 = prm[0:1, :] * scale1
    shaped = jnp.concatenate(
        [weight * (0.5 * grow1), 0.5 * prm[1:2, :], jnp.zeros((7, EXP), F32)], axis=0
    )
    shaped_high = shaped.astype(BF16).astype(F32)
    w1t[...] = jnp.transpose(
        jnp.concatenate([shaped_high, shaped_high, shaped - shaped_high], axis=0)
    ).astype(BF16)

    own_x.wait()
    acc[0] = jnp.zeros((EXP, LANES), F32)

    def x_tile(s, n):
        return xq[tile_quad(n), s, pl.ds(n % 3, IN, stride=3), :]

    def c_tile(s, n):
        return cq[tile_quad(n), s, pl.ds(n % 3, IN, stride=3), :]

    def later_bin(low, high):
        return (
            jnp.where(high_bin, pltpu.roll(high, 7, 1), pltpu.roll(low, LANES - 1, 1)),
            jnp.where(high_bin, 0.0, pltpu.roll(high, LANES - 1, 1)),
        )

    def earlier_bin(low, high):
        return (
            jnp.where(low_bin, 0.0, pltpu.roll(low, 1, 1)),
            jnp.where(low_bin, pltpu.roll(low, LANES - 7, 1), pltpu.roll(high, 1, 1)),
        )

    def from_before(tiles, k):
        return pltpu.roll(jnp.where(last_row, tiles[max(k - 1, 0)], tiles[k]), 8, 1)

    def from_after(tiles, k):
        return pltpu.roll(jnp.where(first_row, tiles[min(k + 1, HALF_W - 1)], tiles[k]), LANES - 8, 1)

    def forward_slot(s, carry):
        for step in range(1, QUADS):
            x_copy(step, s).wait_recv()
        for n in range(WIDE):
            tile = jnp.concatenate([x_tile(s, n) - mean_col, one_rows], axis=0)
            high, low = halves(tile)
            xs[s, 0:32, on_lane(n)] = high
            xs[s, 32:64, on_lane(n)] = low
            xs[s, 64:96, on_lane(n)] = high
        for step in range(1, QUADS):
            c_copy(step, s).start()
        v1[s] = nn(w1t[...], xs[s])

        def taps_step(j, carry):
            rows = pl.ds(pl.multiple_of(8 * j, 8), 8)
            wt = [tab[t, rows, :] for t in range(TAPS)]
            keep = [[[None] * HALF_W for _ in range(2)] for _ in range(3)]
            for k in range(HALF_W):
                pair = []
                for half in range(2):
                    v = v1[s, rows, on_lane(half * HALF_W + k)]
                    pair.append(v + v * jnp.tanh(v))
                nxt = later_bin(*pair)
                prv = earlier_bin(*pair)
                for half in range(2):
                    for p in range(3):
                        keep[p][half][k] = (
                            wt[3 * p] * prv[half] + wt[3 * p + 1] * pair[half] + wt[3 * p + 2] * nxt[half]
                        )
            got = zero_tile
            for k in range(HALF_W):
                back_ok = msk[0, s, :, on_lane(k)]
                fore_ok = msk[1, s, :, on_lane(k)]
                for half in range(2):
                    value = (
                        keep[1][half][k]
                        + back_ok * from_before(keep[0][half], k)
                        + fore_ok * from_after(keep[2][half], k)
                    )
                    a2[s, rows, on_lane(half * HALF_W + k)] = value
                    got = got + value
            acc[0, rows, :] = acc[0, rows, :] + got
            return carry

        lax.fori_loop(0, EXP // 8, taps_step, 0)
        return carry

    lax.fori_loop(0, slots, forward_slot, 0)

    acc[1] = nn(acc[0], jnp.ones((LANES, LANES), F32), FULL) * (1.0 / n_loc)
    acc[2] = jnp.zeros((EXP, LANES), F32)

    def square_step(s, carry):
        def tile_step(j, carry):
            rows = pl.ds(pl.multiple_of(8 * j, 8), 8)
            center = acc[1, rows, :]
            got = zero_tile
            for n in range(WIDE):
                off = a2[s, rows, on_lane(n)] - center
                got = got + off * off
            acc[2, rows, :] = acc[2, rows, :] + got
            return carry

        return lax.fori_loop(0, EXP // 8, tile_step, carry)

    lax.fori_loop(0, slots, square_step, 0)
    rb[0, me, 0:2, :] = split_row(lane_sums(acc[0]) * (1.0 / n_loc))
    rb[0, me, 2:4, :] = split_row(lane_sums(acc[2]))
    spread_start(rb.at[0, me], rb.at[0, me], 1)
    spread_wait(rb.at[0, pl.ds(0, n_dev - 1)], 1)
    sums = jnp.sum(rb[0], axis=0)
    mean2 = sums[0:2] * (1.0 / n_dev)
    gaps = rb[0][:, 0:2, :] - mean2[None]
    spread2 = sums[2:4] + n_loc * jnp.sum(gaps * gaps, axis=0)
    scale2 = lax.rsqrt(join_row(spread2) * (1.0 / total) + NORM_EPS)
    mean2 = join_row(mean2)
    rows8 = jnp.concatenate(
        [mean2, 0.5 * prm[2:3, :] * scale2, 0.5 * prm[3:4, :], jnp.zeros((5, EXP), F32)], axis=0
    )
    for i in range(3):
        tab[TAPS + i] = column(rows8, i, EXP)

    pooled[...] = jnp.zeros((slots * REGIONS, EXP), F32)

    def activate_slot(s, carry):
        def step(j, carry):
            rows = pl.ds(pl.multiple_of(16 * j, 16), 16)
            low_rows = pl.ds(pl.multiple_of(EXP + 16 * j, 16), 16)
            center, grow, lift = (tab[TAPS + i, rows, :] for i in range(3))
            for n in range(WIDE):
                off = a2[s, rows, on_lane(n)] - center
                a2[s, rows, on_lane(n)] = off
                v = off * grow + lift
                high, low = halves(v + v * jnp.tanh(v))
                hh[s, rows, on_lane(n)] = high
                hh[s, low_rows, on_lane(n)] = low
            return carry

        lax.fori_loop(0, EXP // 16, step, 0)
        pooled[...] = pooled[...] + nt(hot[s], hh[s, 0:EXP, :]) + nt(hot[s], hh[s, EXP:, :])
        return carry

    lax.fori_loop(0, slots, activate_slot, 0)

    per_count = 1.0 / counts
    mean_pool = pooled[...] * per_count
    squeeze = nt(mean_pool, w_red_t[...], FULL) + prm[6:7, :SQZ]
    squeeze_sig = jax.nn.sigmoid(squeeze)
    squeezed = squeeze * squeeze_sig
    gate = jax.nn.sigmoid(nn(squeezed, w_exc[...], FULL) + prm[7:8, :])
    for s in range(slots):
        gates[s] = gate[REGIONS * s : REGIONS * (s + 1)]

    def gated_weights(s):
        project = w_pro_t[...]
        rows = gates[s]
        return jnp.concatenate([project * rows[r : r + 1] for r in range(REGIONS)], axis=0)

    def region_tile(r, s, n):
        return jnp.concatenate([reg[r, s, :, on_lane(n % HALF_W)]] * (IN // 8), axis=0)

    def project_slot(s, carry):
        total_a, total_c = carry
        high, low = halves(gated_weights(s))
        body = nn(jnp.concatenate([high, low], axis=0), hh[s, 0:EXP, :])
        body = body[:96] + body[96:] + nn(high, hh[s, EXP:, :])
        for step in range(1, QUADS):
            c_copy(step, s).wait_recv()
        for n in range(WIDE):
            value = jnp.zeros((IN, LANES), F32)
            for r in range(REGIONS):
                value = value + (
                    body[IN * r : IN * (r + 1), n * LANES : (n + 1) * LANES]
                    * region_tile(r, s, n)
                )
            a3[s, :, on_lane(n)] = value
            total_a = total_a + value
            total_c = total_c + c_tile(s, n)
        return total_a, total_c

    own_c.wait()
    zero24 = jnp.zeros((IN, LANES), F32)
    total_a, total_c = lax.fori_loop(0, slots, project_slot, (zero24, zero24))
    center3 = nn(total_a, jnp.ones((LANES, LANES), F32), FULL) * (1.0 / n_loc)

    def third_step(s, carry):
        square, cross = carry
        for n in range(WIDE):
            off = a3[s, :, on_lane(n)] - center3
            square = square + off * off
            cross = cross + off * c_tile(s, n)
        return square, cross

    square3, cross3 = lax.fori_loop(0, slots, third_step, (zero24, zero24))

    def pad_row(row):
        return jnp.concatenate([row, jnp.zeros((1, LANES - IN), F32)], axis=1)

    rb[1, me] = jnp.concatenate(
        [
            pad_row(lane_sums(total_a) * (1.0 / n_loc)),
            pad_row(lane_sums(square3)),
            pad_row(lane_sums(total_c)),
            pad_row(lane_sums(cross3)),
        ],
        axis=0,
    )
    spread_start(rb.at[1, me], rb.at[1, me], 2)
    spread_wait(rb.at[1, pl.ds(0, n_dev - 1)], 2)
    third = rb[1]
    sums = jnp.sum(third, axis=0)
    mean3 = sums[0:1] * (1.0 / n_dev)
    gaps = third[:, 0, :] - mean3
    spread3 = sums[1:2] + n_loc * jnp.sum(gaps * gaps, axis=0, keepdims=True)
    scale3 = lax.rsqrt(spread3 * (1.0 / total) + NORM_EPS)
    bias3_grad = sums[2:3]
    cross_sum = sums[3:4] + jnp.sum(third[:, 2, :] * gaps, axis=0, keepdims=True)
    gain3_grad = scale3 * cross_sum
    grow3 = prm[4:5, :LANES] * scale3
    rows8 = jnp.concatenate(
        [
            mean3,
            grow3,
            prm[5:6, :LANES],
            grow3 * bias3_grad * (1.0 / total),
            grow3 * scale3 * gain3_grad * (1.0 / total),
            jnp.zeros((3, LANES), F32),
        ],
        axis=0,
    )
    mean3_c, grow3_c, lift3_c, flat3_c, lean3_c = (column(rows8, i, IN) for i in range(5))

    small[0] = jnp.zeros((IN, EXP), F32)

    def back_slot(s, carry):
        for n in range(WIDE):
            off = a3[s, :, on_lane(n)] - mean3_c
            xloc[tile_quad(n), s, pl.ds(n % 3, IN, stride=3), :] = x_tile(s, n) + off * grow3_c + lift3_c
            grad = grow3_c * c_tile(s, n) - flat3_c - off * lean3_c
            high, low = halves(
                jnp.concatenate(
                    [grad * region_tile(r, s, n) for r in range(REGIONS)], axis=0
                )
            )
            dcat[s, 0:96, on_lane(n)] = high
            dcat[s, 128:224, on_lane(n)] = low
        dcat[s, 96:128, :] = hot[s]
        dcat[s, 224:256, :] = hot[s]
        for step in range(1, QUADS):
            o_copy(step, s).start()
        main = nt(dcat[s, 0:224, :], hh[s, 0:EXP, :])
        main = main[0:96] + main[128:224] + nt(dcat[s, 0:96, :], hh[s, EXP:, :])
        project = w_pro_t[...]
        gp = small[0]
        rows = gates[s]
        for r in range(REGIONS):
            part = main[IN * r : IN * (r + 1)]
            dgate[s, r : r + 1, :] = jnp.sum(part * project, axis=0, keepdims=True)
            gp = gp + part * rows[r : r + 1]
        small[0] = gp
        return carry

    lax.fori_loop(0, slots, back_slot, 0)
    own_o = pltpu.make_async_copy(xloc.at[space], out.at[pl.ds(slots * space, slots)], own_sem.at[2])
    own_o.start()

    dgate_rows = jnp.concatenate([dgate[s] for s in range(slots)], axis=0)
    dpre_x = dgate_rows * gate * (1.0 - gate)
    excite_grad = tn(squeezed, dpre_x, FULL)
    excite_bias_grad = jnp.sum(dpre_x, axis=0, keepdims=True)
    dsqueezed = nt(dpre_x, w_exc[...], FULL)
    dpre_r = dsqueezed * squeeze_sig * (1.0 + squeeze * (1.0 - squeeze_sig))
    reduce_grad = tn(dpre_r, mean_pool, FULL)
    reduce_bias_grad = jnp.sum(dpre_r, axis=0, keepdims=True)
    dpool = nn(dpre_r, w_red_t[...], FULL) * per_count
    pooled[...] = 0.5 * dpool

    acc[0] = jnp.zeros((EXP, LANES), F32)
    acc[1] = jnp.zeros((EXP, LANES), F32)

    def second_back_slot(s, carry):
        high, low = halves(0.5 * gated_weights(s))
        pool_high, pool_low = halves(pooled[...])
        left = jnp.concatenate([high, pool_high, high, pool_low], axis=0)
        dh[...] = tn(left, dcat[s]) + tn(low, dcat[s, 0:96, :])

        def step(j, carry):
            rows = pl.ds(pl.multiple_of(8 * j, 8), 8)
            grow, lift = (tab[TAPS + i, rows, :] for i in (1, 2))
            plain, cross = zero_tile, zero_tile
            for n in range(WIDE):
                off = a2[s, rows, on_lane(n)]
                v = off * grow + lift
                u = 1.0 + jnp.tanh(v)
                d = dh[rows, on_lane(n)] * (u + (v * u) * (2.0 - u))
                dn2[s, rows, on_lane(n)] = d
                plain = plain + d
                cross = cross + d * off
            acc[0, rows, :] = acc[0, rows, :] + plain
            acc[1, rows, :] = acc[1, rows, :] + cross
            return carry

        lax.fori_loop(0, EXP // 8, step, 0)
        return carry

    lax.fori_loop(0, slots, second_back_slot, 0)
    rb[2, me, 0:2, :] = split_row(lane_sums(acc[0]))
    rb[2, me, 2:4, :] = split_row(lane_sums(acc[1]))
    spread_start(rb.at[2, me], rb.at[2, me], 3)
    spread_wait(rb.at[2, pl.ds(0, n_dev - 1)], 3)
    sums = jnp.sum(rb[2], axis=0)
    bias2_grad = join_row(sums[0:2])
    cross2 = join_row(sums[2:4])
    gain2_grad = cross2 * scale2
    grow2 = prm[2:3, :] * scale2
    rows8 = jnp.concatenate(
        [
            grow2,
            -grow2 * scale2 * gain2_grad * (1.0 / total),
            -grow2 * bias2_grad * (1.0 / total),
            jnp.zeros((5, EXP), F32),
        ],
        axis=0,
    )
    for i in range(3):
        tab[TAPS + i] = column(rows8, i, EXP)

    for t in range(TAPS):
        acc[t] = jnp.zeros((EXP, LANES), F32)
    small[1] = jnp.zeros((IN, EXP), F32)
    small[2] = jnp.zeros((IN, EXP), F32)

    def taps_back_slot(s, carry):
        def step(j, carry):
            rows = pl.ds(pl.multiple_of(8 * j, 8), 8)
            wt = [tab[t, rows, :] for t in range(TAPS)]
            k1, k2, k3 = (tab[TAPS + i, rows, :] for i in range(3))
            grads = [[], []]
            for half in range(2):
                for k in range(HALF_W):
                    where = on_lane(half * HALF_W + k)
                    grads[half].append(k1 * dn2[s, rows, where] + k2 * a2[s, rows, where] + k3)
            sums = [zero_tile] * TAPS
            for k in range(HALF_W):
                back_ok = msk[0, s, :, on_lane(k)]
                fore_ok = msk[1, s, :, on_lane(k)]
                vs, us, hs = [], [], []
                for half in range(2):
                    v = v1[s, rows, on_lane(half * HALF_W + k)]
                    u = 1.0 + jnp.tanh(v)
                    vs.append(v)
                    us.append(u)
                    hs.append(v * u)
                near = [earlier_bin(*hs), hs, later_bin(*hs)]
                mix = [[], [], []]
                for half in range(2):
                    moved = [
                        fore_ok * from_after(grads[half], k),
                        grads[half][k],
                        back_ok * from_before(grads[half], k),
                    ]
                    for q in range(3):
                        mix[q].append(
                            wt[q] * moved[0] + wt[3 + q] * moved[1] + wt[6 + q] * moved[2]
                        )
                        for p in range(3):
                            sums[3 * p + q] = sums[3 * p + q] + moved[p] * near[q][half]
                left = later_bin(*mix[0])
                right = earlier_bin(*mix[2])
                for half in range(2):
                    d = (left[half] + mix[1][half] + right[half]) * (
                        us[half] + hs[half] * (2.0 - us[half])
                    )
                    dh[rows, on_lane(half * HALF_W + k)] = d
            for t in range(TAPS):
                acc[t, rows, :] = acc[t, rows, :] + sums[t]
            return carry

        lax.fori_loop(0, EXP // 8, step, 0)

        def pack(j, carry):
            rows = pl.ds(pl.multiple_of(16 * j, 16), 16)
            low_rows = pl.ds(pl.multiple_of(EXP + 16 * j, 16), 16)
            for n in range(WIDE):
                high, low = halves(0.5 * dh[rows, on_lane(n)])
                hh[s, rows, on_lane(n)] = high
                hh[s, low_rows, on_lane(n)] = low
            return carry

        lax.fori_loop(0, EXP // 16, pack, 0)
        main = nt(xs[s, 0:64, :], hh[s, 0:EXP, :])
        main = main[0:32] + main[32:64] + nt(xs[s, 0:32, :], hh[s, EXP:, :])
        small[1] = small[1] + main[0:IN]
        small[2, 0:8, :] = small[2, 0:8, :] + main[IN:32]
        return carry

    lax.fori_loop(0, slots, taps_back_slot, 0)

    stacked = [small[0], small[1], small[2, 0:8, :]]
    tail = [lane_sums(acc[t]) for t in range(TAPS)]
    tail.append(excite_bias_grad)
    tail.append(jnp.concatenate([reduce_bias_grad, jnp.zeros((1, EXP - SQZ), F32)], axis=1))
    tail.append(jnp.zeros((5, EXP), F32))
    stacked.append(jnp.concatenate(tail, axis=0))
    for part in (excite_grad, reduce_grad):
        stacked.append(jnp.concatenate([part, jnp.zeros((8 - SQZ, EXP), F32)], axis=0))
    stacked = jnp.concatenate(stacked, axis=0)
    n_heads = 11
    for i in range(n_heads):
        bulk[i] = stacked[8 * i : 8 * i + 8, :LANES]
    ends = [stacked[8 * i : 8 * i + 8, LANES:] for i in range(n_heads)]
    bulk[n_heads] = jnp.concatenate(ends[:8], axis=1)
    bulk[n_heads + 1] = jnp.concatenate(ends[8:] + [jnp.zeros((8, LANES - 16 * (n_heads - 8)), F32)], axis=1)
    for i in range(n_heads + 2, BULK):
        bulk[i] = zero_tile
    each = BULK // GROUP
    base = lax.div(me, GROUP) * GROUP
    place = lax.rem(me, GROUP)

    def group_copy(source, target, index, step):
        return pltpu.make_async_remote_copy(
            src_ref=source, dst_ref=target, send_sem=r_send.at[index], recv_sem=r_recv.at[index],
            device_id=device(base + lax.rem(place + step, GROUP)), device_id_type=MESH,
        )

    for step in range(1, GROUP):
        other = lax.rem(place + step, GROUP)
        group_copy(bulk.at[pl.ds(each * other, each)], bulk_in.at[place], 4, step).start()
    bulk_in[place] = bulk[pl.ds(each * place, each)]
    done = group_copy(bulk_in.at[pl.ds(0, GROUP - 1)], bulk_in.at[pl.ds(0, GROUP - 1)], 4, 1)
    done.wait_send()
    done.wait_recv()
    bulk_all[me] = jnp.sum(bulk_in[...], axis=0)
    spread_start(bulk_all.at[me], bulk_all.at[me], 5)
    spread_wait(bulk_all.at[pl.ds(0, n_dev - 1)], 5)
    summed = []
    for i in range(n_heads + 2):
        tile = zero_tile
        for g in range(n_dev // GROUP):
            tile = tile + bulk_all[g * GROUP + i // each, i % each]
        summed.append(tile)

    def row_tile(i):
        rest = summed[n_heads + i // 8][:, 16 * (i % 8) : 16 * (i % 8) + 16]
        return jnp.concatenate([summed[i], rest], axis=1)

    project_grad = jnp.concatenate([row_tile(i) for i in range(3)], axis=0)
    expand_cross = jnp.concatenate([row_tile(i) for i in range(3, 6)], axis=0)
    bias1_grad = row_tile(6)[0:1]
    depth_tiles = jnp.concatenate([row_tile(7), row_tile(8)], axis=0)
    excite_tile = row_tile(9)
    reduce_tile = row_tile(10)
    cross1 = jnp.sum(expand_cross * weight, axis=0, keepdims=True)
    gain1_grad = scale1 * cross1
    lean1 = scale1 * gain1_grad * (1.0 / total)
    expand_grad = grow1 * (expand_cross - lean1 * moment_w)
    zero_rows = jnp.zeros((16, EXP), F32)
    gs_out[0] = expand_grad
    gs_out[1] = project_grad
    gs_out[2] = jnp.concatenate([reduce_tile, zero_rows], axis=0)
    gs_out[3] = jnp.concatenate([excite_tile, zero_rows], axis=0)
    row16 = lax.broadcasted_iota(jnp.int32, (16, EXP), 0)
    gs_out[4] = jnp.concatenate([jnp.where(row16 < TAPS, depth_tiles, 0.0), zero_rows[:8]], axis=0)
    vr_out[...] = jnp.concatenate(
        [
            gain1_grad,
            bias1_grad,
            gain2_grad,
            bias2_grad,
            jnp.concatenate([gain3_grad, jnp.zeros((1, EXP - LANES), F32)], axis=1),
            jnp.concatenate([bias3_grad, jnp.zeros((1, EXP - LANES), F32)], axis=1),
            depth_tiles[TAPS + 1 : TAPS + 2],
            depth_tiles[TAPS : TAPS + 1],
        ],
        axis=0,
    )

    for step in range(1, QUADS):
        def o_done(s, carry, step=step):
            o_copy(step, s).wait_send()
            x_copy(step, s).wait_send()
            c_copy(step, s).wait_send()
            return carry

        lax.fori_loop(0, slots, o_done, 0)
    grown = weight * grow1
    grown_high = grown.astype(BF16)
    grown_both = jnp.concatenate([grown_high.astype(F32), grown - grown_high.astype(F32)], axis=0).astype(BF16)
    lean_map = -nt(grown * lean1, weight, FULL)
    flat_col = -jnp.sum(grown * (bias1_grad * (1.0 / total)), axis=1, keepdims=True)
    side = jnp.concatenate([lean_map, flat_col, jnp.zeros((IN, 7), F32)], axis=1)
    side_high = side.astype(BF16).astype(F32)
    wlow[...] = jnp.concatenate([side_high, side_high, side - side_high], axis=1).astype(BF16)

    def last_slot(s, carry):
        main = nn(grown_both, hh[s, 0:EXP, :])
        main = main[:IN] + main[IN:] + nn(grown_high, hh[s, EXP:, :]) + nn(wlow[...], xs[s])
        for n in range(WIDE):
            xq[tile_quad(n), s, pl.ds(n % 3, IN, stride=3), :] = (
                c_tile(s, n) + main[:, n * LANES : (n + 1) * LANES]
            )
        for step in range(1, QUADS):
            g_copy(step, s).start()
        return carry

    lax.fori_loop(0, slots, last_slot, 0)
    own_g = pltpu.make_async_copy(xq.at[space], ing.at[pl.ds(slots * space, slots)], own_sem.at[3])
    own_g.start()

    mine = jnp.minimum(place, 4)
    grad = gs_out[mine]
    turned = (mine == 1) | (mine == 2)
    small[...] = jnp.zeros(small.shape, F32)
    small[0, :, :IN] = in_st[0]
    small[1, :, :IN] = jnp.transpose(in_st[1])
    small[2, :SQZ, :SQZ] = jnp.transpose(sq_st[0])
    small[3, :SQZ, :SQZ] = sq_st[1]
    small[4, :TAPS, :TAPS] = tap_st[...]
    old_big = big[mine]
    old_big = jnp.where(turned, jnp.transpose(old_big), old_big)
    big_m = DECAY * old_big + FRESH * tn(grad, grad, FULL)
    small_m = DECAY * small[mine][:, :IN] + FRESH * nt(grad, grad, FULL)
    big_eye = (
        lax.broadcasted_iota(jnp.int32, (EXP, EXP), 0) == lax.broadcasted_iota(jnp.int32, (EXP, EXP), 1)
    ).astype(F32)
    small_eye = eye24.astype(F32)
    big_c = 2.5 * lax.rsqrt(jnp.sum(jnp.sum(big_m * big_m, axis=0, keepdims=True), axis=1, keepdims=True))
    small_c = 2.5 * lax.rsqrt(jnp.sum(jnp.sum(small_m * small_m, axis=0, keepdims=True), axis=1, keepdims=True))
    big_m = big_c * big_m
    small_m = small_c * small_m
    direction = jnp.sqrt(jnp.sqrt(big_c)) * grad
    small_h = jnp.sqrt(jnp.sqrt(small_c)) * small_eye

    def root_step(i, carry):
        big_m, small_m, direction, small_h = carry
        big_k = 1.25 * big_eye - 0.25 * big_m
        small_k = 1.25 * small_eye - 0.25 * small_m
        direction = nn(direction, big_k, FULL)
        small_h = nn(small_h, small_k, FULL)
        big_k = nn(big_k, big_k, FULL)
        small_k = nn(small_k, small_k, FULL)
        big_k = nn(big_k, big_k, FULL)
        small_k = nn(small_k, small_k, FULL)
        return nn(big_k, big_m, FULL), nn(small_k, small_m, FULL), direction, small_h

    _, _, direction, small_h = lax.fori_loop(
        0, ROOT_ITERS, root_step, (big_m, small_m, direction, small_h)
    )
    direction = nn(small_h, direction, FULL)
    short = jnp.where(mine < 2, float(IN), jnp.where(mine == 4, float(TAPS), float(SQZ)))
    lead = jnp.where(turned, float(EXP), short)
    power = jnp.sum(jnp.sum(direction * direction, axis=0, keepdims=True), axis=1, keepdims=True)
    power = power / jnp.full((1, 1), short * float(EXP), F32)
    step_size = STEP_FRACTION * lax.rsqrt(jnp.full((1, 1), lead, F32)) * lax.rsqrt(power + 1e-06)
    small[0] = weight
    small[1] = w_pro_t[...]
    for i, source in ((2, w_red_t), (3, w_exc), (4, w_dep)):
        small[i] = jnp.zeros((IN, EXP), F32)
        small[i, : source.shape[0], :] = source[...]
    nws[place] = small[mine] - step_size * direction
    for step in range(1, GROUP):
        group_copy(nws.at[place], nws.at[place], 6, step).start()
    done = group_copy(nws.at[pl.ds(0, GROUP - 1)], nws.at[pl.ds(0, GROUP - 1)], 6, 1)
    done.wait_send()
    done.wait_recv()
    nw_out[...] = nws[0:5]

    for step in range(1, QUADS):
        def all_done(s, carry, step=step):
            o_copy(step, s).wait_recv()
            g_copy(step, s).wait()
            return carry

        lax.fori_loop(0, slots, all_done, 0)
    own_o.wait()
    own_g.wait()


def finish_kernel(
    gs, nw, big, in_st, sq_st, tap_st,
    ge, gd, gr_t, gx, gp_t, ne, nd, nr_t, nx, np_t, big_new, in_new, sq_new, tap_new,
):
    ge[...], gp_t[...], gr_t[...], gx[...], gd[...] = gs[0], gs[1], gs[2, :SQZ], gs[3, :SQZ], gs[4, :TAPS]
    ne[...], np_t[...], nr_t[...], nx[...], nd[...] = nw[0], nw[1], nw[2, :SQZ], nw[3, :SQZ], nw[4, :TAPS]
    for i in range(5):
        grad = gs[i]
        big_new[i] = DECAY * big[i] + FRESH * tn(grad, grad, FULL)
        inner = FRESH * nt(grad, grad, FULL)
        if i < 2:
            in_new[i] = DECAY * in_st[i] + inner
        elif i < 4:
            sq_new[i - 2] = DECAY * sq_st[i - 2] + inner[:SQZ, :SQZ]
        else:
            tap_new[...] = DECAY * tap_st[...] + inner[:TAPS, :TAPS]


def on_device(
    n_dev, n_space,
    features, cotangent, segment_ids, w_expand, w_depth, w_reduce, w_excite, w_project,
    vector_params, vector_moments, big_stats, in_stats, sq_stats, tap_stats,
):
    slot_count = features.shape[0]
    slots = slot_count // QUADS
    n_pos = slot_count * (n_dev // n_space) * FRAMES * BINS
    cuts = [0, EXP, 2 * EXP, 3 * EXP, 4 * EXP, 4 * EXP + IN, 4 * EXP + 2 * IN, 4 * EXP + 2 * IN + SQZ]
    cuts.append(cuts[-1] + EXP)
    pieces = [vector_params[a:b] for a, b in zip(cuts[:-1], cuts[1:])]
    prm = jnp.stack([jnp.pad(piece, (0, EXP - piece.shape[0])) for piece in pieces])
    vm = pl.BlockSpec(memory_space=pltpu.VMEM)
    hbm = pl.BlockSpec(memory_space=pl.ANY)
    grid_shape = jax.ShapeDtypeStruct((slot_count, ROWS, LANES), F32)
    wide = WIDE * LANES
    vmem = pltpu.VMEM
    dma = pltpu.SemaphoreType.DMA
    out, ing, gs, nw, vr = pl.pallas_call(
        functools.partial(block_kernel, n_dev, n_space, slots, n_pos),
        out_shape=(
            grid_shape,
            grid_shape,
            jax.ShapeDtypeStruct((5, IN, EXP), F32),
            jax.ShapeDtypeStruct((5, IN, EXP), F32),
            jax.ShapeDtypeStruct((8, EXP), F32),
        ),
        in_specs=[hbm, hbm] + [vm] * 11,
        out_specs=(hbm, hbm, vm, vm, vm),
        scratch_shapes=[
            vmem((QUADS, slots, ROWS, LANES), F32),
            vmem((QUADS, slots, ROWS, LANES), F32),
            vmem((QUADS, slots, ROWS, LANES), F32),
            vmem((slots, 96, wide), BF16),
            vmem((slots, EXP, wide), F32),
            vmem((slots, EXP, wide), F32),
            vmem((slots, 2 * EXP, wide), BF16),
            vmem((slots, EXP, wide), F32),
            vmem((EXP, wide), F32),
            vmem((slots, IN, wide), F32),
            vmem((slots, slots * REGIONS, wide), BF16),
            vmem((slots, 256, wide), BF16),
            vmem((TAPS + 3, EXP, LANES), F32),
            vmem((2, slots, 8, HALF_W * LANES), F32),
            vmem((REGIONS, slots, 8, HALF_W * LANES), F32),
            vmem((TAPS, EXP, LANES), F32),
            vmem((EXP, 96), BF16),
            vmem((IN, 96), BF16),
            vmem((5, IN, EXP), F32),
            vmem((slots * REGIONS, EXP), F32),
            vmem((slots, REGIONS, EXP), F32),
            vmem((slots, REGIONS, EXP), F32),
            vmem((BULK, 8, LANES), F32),
            vmem((GROUP, BULK // GROUP, 8, LANES), F32),
            vmem((n_dev, BULK // GROUP, 8, LANES), F32),
            vmem((n_dev, 8, LANES), F32),
            vmem((3, n_dev, 4, LANES), F32),
            vmem((GROUP, IN, EXP), F32),
            vmem((IN, LANES), F32),
            dma((QUADS,)),
        ]
        + [dma((QUADS, slots))] * 8
        + [dma((8,)), dma((8,)), dma((4,))],
        compiler_params=pltpu.CompilerParams(
            collective_id=0, has_side_effects=True, vmem_limit_bytes=60 << 20
        ),
    )(
        features.reshape(slot_count, ROWS, LANES),
        cotangent.reshape(slot_count, ROWS, LANES),
        segment_ids, w_expand, w_depth, w_reduce.T, w_excite, w_project.T, prm,
        big_stats, in_stats, sq_stats, tap_stats,
    )
    shape = jax.ShapeDtypeStruct
    ge, gd, gr_t, gx, gp_t, ne, nd, nr_t, nx, np_t, big_new, in_new, sq_new, tap_new = pl.pallas_call(
        finish_kernel,
        out_shape=tuple(
            shape(dims, F32)
            for dims in [(IN, EXP), (TAPS, EXP), (SQZ, EXP), (SQZ, EXP), (IN, EXP)] * 2
            + [(5, EXP, EXP), (2, IN, IN), (2, SQZ, SQZ), (TAPS, TAPS)]
        ),
        in_specs=[vm] * 6,
        out_specs=(vm,) * 14,
    )(gs, nw, big_stats, in_stats, sq_stats, tap_stats)
    vector_grads = jnp.concatenate([vr[i, : cuts[i + 1] - cuts[i]] for i in range(8)])
    moments_new = DECAY * vector_moments + FRESH * vector_grads * vector_grads
    vector_new = vector_params - VECTOR_RATE * vector_grads / (jnp.sqrt(moments_new) + 1e-08)
    return (
        out.reshape(features.shape), ing.reshape(features.shape),
        ge, gd, gr_t.T, gx, gp_t.T, ne, nd, nr_t.T, nx, np_t.T,
        big_new, in_new, sq_new, tap_new, vector_grads, moments_new, vector_new,
    )


def solution(mesh):
    field = P("dp", None, "space", None)
    return jax.shard_map(
        functools.partial(on_device, mesh.shape["dp"] * mesh.shape["space"], mesh.shape["space"]),
        mesh=mesh,
        in_specs=(field, field, P("dp", None)) + (P(),) * 11,
        out_specs=(field, field) + (P(),) * 17,
        check_vma=False,
    )
```

time: 1120 us -> 176 us (0.16)
  blocking collectives: 434 us -> 0 us
  other arithmetic: 313 us -> 0.62 us
  Pallas kernels: 0 us -> 161 us
  matrix products: 151 us -> 0 us
  waiting for transfers between devices: 145 us -> 0 us
  between operations: 24.8 us -> 0.7 us
  starting transfers between devices: 20.5 us -> 0 us
    psum x10 -> x0, blocking collectives: 434 us -> none  [the longest x3 136 us: moments(): lax.psum(jnp.sum(array, axis=axes, keepdims=True), ('dp', 'space'))]
    reduce_sum x15 -> x0, other arithmetic: 223 us -> none  [the longest x3 76.5 us: norm_back(): jnp.sum(upstream, axis=axes, keepdims=True)]
    pallas_call x0 -> x2, Pallas kernels: none -> 161 us  [the longest x1 158 us: on_device(): pl.pallas_call(functools.partial(block_kernel, n_dev, n_space, slots, n_p...]
    dot_general x258 -> x0, matrix products: 151 us -> none  [the longest x242 49.5 us: exact_dot(): return jnp.dot(left, right, precision=PRECISE)]
    psum x3 -> x0, waiting for transfers between devices: 135 us -> none  [the longest x1 73.7 us: on_device(): lax.psum(slot_mask[:, None, None] * inverse_root(mine)[None], 'dp')]
    concatenate x2 -> x0, other arithmetic: 57.9 us -> none  [extend(): return jnp.concatenate([left_edge, tall, right_edge], axis=2)]
    ppermute x8 -> x0, starting transfers between devices: 20.4 us -> none  [passed_along(): lax.ppermute(value, axis, [(source, source + steps) for source in range(l...]
    mul x12 -> x0, other arithmetic: 18.8 us -> none  [the longest x1 6.89 us: on_device(): hidden_one = shaped_one * sigma_one]
  transfers between devices with their start and end apart: 11 -> 0, of which waited for: 6 -> 0; matrix products, arithmetic and copies ran while one was open for 2% -> 0% of each run, Pallas kernels for 0% -> 0%
where the time goes in v1:
time: 176 us; the launch traced here: 175 us
  Pallas kernels  161 us (91%)
  local copies, waits for them, and re-layouts  12.4 us (7%)
    pallas_call x1, Pallas kernels, on_device(): pl.pallas_call(functools.partial(block_kernel, n_dev, n_space, slots, n_p...  158 us
    unnamed x12, local copies, waits for them, and re-layouts  6.8 us

profile of v1, /device:TPU:0, one launch (start us, length us, event | category | flops | bytes accessed | tf_op | source)
XLA Modules:
  0.0 175.1 jit_solution(11159617547145261154)
XLA Ops:
  0.7 0.8 slice.54
  1.4 0.8 fusion.4
  2.3 0.9 fusion.3
  3.2 0.6 stack.35.prm
  3.8 1.3 copy.33.sq_st
  5.1 0.0 copy-start.1
  5.1 0.0 copy-start.3
  5.1 158.4 %shard_map.285 = (f32[32,72,128]{2,1,0:T(8,128)}, f32[32,72,128]{2,1,0:T(8,128)}, f32[5,24,144]{2,1,0:T(8,128)}, f32[5,24,144]{2,1,0:T(8,128)}, f32[8,144]{1,0:T(8,128)}) custom-call(f32[32,72,128]{2,1,0:T(8,128)} %bitcast.29, f32[32,72,128]{2,1,0:T(8,128)} %bitcast.30, s32[32,96]{1,0:T(8,128)} %ids_ref.1, f32[24,144]{1,0:T(8,128)} %w_exp.1, ...), custom_call_target="tpu_custom_call" | custom-call | tf_op jit(solution)/shard_map/pallas_call | solution.py:878
  163.6 0.7 slice_bitcast_fusion
  164.2 0.8 slice_bitcast_fusion.1
  165.0 0.9 fusion.2
  165.9 0.1 concatenate.3
  166.0 0.0 copy-done.1
  166.0 0.0 copy-done.3
  166.0 0.0 copy-start.2
  166.0 0.6 divide_subtract_fusion
  166.6 3.0 %shard_map.286 = (f32[24,144]{1,0:T(8,128)}, f32[9,144]{1,0:T(8,128)}, f32[6,144]{1,0:T(8,128)}, f32[6,144]{1,0:T(8,128)}, f32[24,144]{1,0:T(8,128)}, /*index=5*...) custom-call(f32[5,24,144]{2,1,0:T(8,128)} %get-tuple-element.40.gs, ...), custom_call_target="tpu_custom_call" | custom-call | tf_op jit(solution)/shard_map/pallas_call | solution.py:933
  169.6 1.3 copy.37
  170.9 0.0 copy-start
  170.9 3.2 %copy.40 = f32[32,24,1,384]{3,2,1,0:T(1,128)} copy(f32[32,24,1,384]{3,2,1,0:T(1,128)} %bitcast.32) | data formatting | bytes 2359296
  174.1 0.0 copy-done.2
  174.1 0.0 copy-done
  174.1 1.0 copy.41
  (3 shorter events, 0.0 us)
Async XLA Ops:
  5.1 160.8 %copy-start.1 = (f32[774]{0:T(1024)S(1)}, f32[774]{0:T(1024)}, u32[]{:S(2)}) copy-start(f32[774]{0:T(1024)} %param.22) | copy-start | bytes 9292
  5.1 160.8 %copy-start.3 = (f32[774]{0:T(1024)S(1)}, f32[774]{0:T(1024)}, u32[]{:S(2)}) copy-start(f32[774]{0:T(1024)} %param.23) | copy-start | bytes 9292
  166.0 8.1 %copy-start.2 = (f32[774]{0:T(1024)}, f32[774]{0:T(1024)S(1)}, u32[]{:S(2)}) copy-start(f32[774]{0:T(1024)S(1)} %concatenate.3) | copy-start | bytes 9292
  170.9 3.2 %copy-start = (f32[32,72,128]{2,1,0:T(8,128)S(1)}, f32[32,72,128]{2,1,0:T(8,128)}, u32[]{:S(2)}) copy-start(f32[32,72,128]{2,1,0:T(8,128)} %get-tuple-element.39) | copy-start | bytes 3538948

commit v2 on v1

--- a/solution.py
+++ b/solution.py
@@ -22,6 +22,7 @@
 FRESH = 1.0 - DECAY
 STEP_FRACTION = 0.5
 VECTOR_RATE = 0.15
+PARTS = (EXP, EXP, EXP, EXP, IN, IN, SQZ, EXP)
 
 LANES = 128
 HALF_W = 6
@@ -89,9 +90,9 @@
 
 def block_kernel(
     n_dev, n_space, slots, n_pos,
-    feat, cot, ids_ref, w_exp, w_dep, w_red_t, w_exc, w_pro_t, prm, big, in_st, sq_st, tap_st,
+    feat, cot, ids_ref, w_exp, w_dep, w_red_t, w_exc, w_pro_t, vec, big, in_st, sq_st, tap_st,
     out, ing, gs_out, nw_out, vr_out,
-    xloc, xq, cq, xs, v1, a2, hh, dn2, dh, a3, hot, dcat, tab, msk, reg, acc, w1t, wlow,
+    xloc, xq, cq, xs, x3, c3, v1, a2, hh, dn2, dh, dm, dp, a3, hot, dcat, tab, msk, reg, acc, w1t, wlow, prm,
     small, pooled, gates, dgate, bulk, bulk_in, bulk_all, rb1, rb, nws, fold,
     loc_sem, x_send, x_recv, c_send, c_recv, o_send, o_recv, g_send, g_recv,
     r_send, r_recv, own_sem,
@@ -128,44 +129,6 @@
     own_c = pltpu.make_async_copy(cot.at[pl.ds(slots * space, slots)], cq.at[space], own_sem.at[1])
     own_x.start()
     own_c.start()
-
-    lane = lax.broadcasted_iota(jnp.int32, (8, LANES), 1)
-    low_bin = lax.rem(lane, 8) == 0
-    high_bin = lax.rem(lane, 8) == 7
-    first_row = lane < 8
-    last_row = lane >= LANES - 8
-    zero_tile = jnp.zeros((8, LANES), F32)
-
-    half_lanes = HALF_W * LANES
-    own_ids = ids_ref[pl.ds(pl.multiple_of(slots * space, 8), slots), :].astype(F32)
-    spread = (
-        lax.broadcasted_iota(jnp.int32, (FRAMES, half_lanes), 1) // 8
-        == lax.broadcasted_iota(jnp.int32, (FRAMES, half_lanes), 0)
-    )
-    wide_ids = nn(own_ids.astype(BF16), spread.astype(F32).astype(BF16))
-    wide_lane = lax.broadcasted_iota(jnp.int32, (slots, half_lanes), 1)
-    before = pltpu.roll(wide_ids, 8, 1)
-    after = pltpu.roll(wide_ids, half_lanes - 8, 1)
-    from_ok = jnp.where((before == wide_ids) & (wide_lane >= 8), 1.0, 0.0)
-    to_ok = jnp.where((after == wide_ids) & (wide_lane < half_lanes - 8), 1.0, 0.0)
-    for s in range(slots):
-        msk[0, s] = jnp.broadcast_to(from_ok[s : s + 1], (8, half_lanes))
-        msk[1, s] = jnp.broadcast_to(to_ok[s : s + 1], (8, half_lanes))
-        for r in range(REGIONS):
-            reg[r, s] = jnp.broadcast_to((wide_ids[s : s + 1] == float(r)).astype(F32), (8, half_lanes))
-    row_index = lax.broadcasted_iota(jnp.int32, (slots * REGIONS, half_lanes), 0)
-    row_region = lax.rem(row_index, REGIONS).astype(F32)
-    counts = jnp.zeros((slots * REGIONS, 1), F32)
-    for s in range(slots):
-        row = jnp.where(
-            (lax.div(row_index, REGIONS) == s) & (wide_ids[s : s + 1] == row_region), 1.0, 0.0
-        )
-        counts = counts + 2.0 * jnp.sum(row, axis=1, keepdims=True)
-        hot[s, :, :half_lanes] = row.astype(BF16)
-        hot[s, :, half_lanes:] = row.astype(BF16)
-    taps = w_dep[...]
-    for t in range(TAPS):
-        tab[t] = column(taps, t, EXP)
 
     for load in loads:
         load.wait()
@@ -247,6 +210,55 @@
 
     lax.fori_loop(0, slots, x_start, 0)
 
+    lane = lax.broadcasted_iota(jnp.int32, (8, LANES), 1)
+    low_bin = lax.rem(lane, 8) == 0
+    high_bin = lax.rem(lane, 8) == 7
+    first_row = lane < 8
+    second_row = (lane >= 8) & (lane < 16)
+    last_row = lane >= LANES - 8
+    zero_tile = jnp.zeros((8, LANES), F32)
+
+    half_lanes = HALF_W * LANES
+    own_ids = ids_ref[pl.ds(pl.multiple_of(slots * space, 8), slots), :].astype(F32)
+    spread = (
+        lax.broadcasted_iota(jnp.int32, (FRAMES, half_lanes), 1) // 8
+        == lax.broadcasted_iota(jnp.int32, (FRAMES, half_lanes), 0)
+    )
+    wide_ids = nn(own_ids.astype(BF16), spread.astype(F32).astype(BF16))
+    wide_lane = lax.broadcasted_iota(jnp.int32, (slots, half_lanes), 1)
+    before = pltpu.roll(wide_ids, 8, 1)
+    after = pltpu.roll(wide_ids, half_lanes - 8, 1)
+    from_ok = jnp.where((before == wide_ids) & (wide_lane >= 8), 1.0, 0.0)
+    to_ok = jnp.where((after == wide_ids) & (wide_lane < half_lanes - 8), 1.0, 0.0)
+    def both_halves(rows):
+        turned = [pltpu.roll(rows[:, n * LANES : (n + 1) * LANES], 8, 1) for n in range(HALF_W)]
+        return jnp.concatenate([rows] + turned, axis=1)
+
+    marks = [both_halves(rows) for rows in (from_ok, to_ok)]
+    regions = [both_halves((wide_ids == float(r)).astype(F32)) for r in range(REGIONS)]
+    for s in range(slots):
+        for i in range(2):
+            msk[i, s] = jnp.broadcast_to(marks[i][s : s + 1], (8, WIDE * LANES))
+        for r in range(REGIONS):
+            reg[r, s] = jnp.broadcast_to(regions[r][s : s + 1], (8, WIDE * LANES))
+    row_index = lax.broadcasted_iota(jnp.int32, (slots * REGIONS, WIDE * LANES), 0)
+    counts = jnp.zeros((slots * REGIONS, 1), F32)
+    for s in range(slots):
+        row = jnp.zeros((slots * REGIONS, WIDE * LANES), F32)
+        for r in range(REGIONS):
+            row = jnp.where(row_index == REGIONS * s + r, regions[r][s : s + 1], row)
+        counts = counts + jnp.sum(row, axis=1, keepdims=True)
+        hot[s] = row.astype(BF16)
+    taps = w_dep[...]
+    for t in range(TAPS):
+        tab[t] = column(taps, t, EXP)
+
+    start = 0
+    prm[...] = jnp.zeros((8, EXP), F32)
+    for i, width in enumerate(PARTS):
+        prm[i : i + 1, :width] = vec[:, start : start + width]
+        start = start + width
+
     spread_wait(rb1.at[pl.ds(0, n_dev - 1)], 0)
     gathered = jnp.sum(rb1[...], axis=0)
     means = rb1[:, 6, :]
@@ -277,36 +289,41 @@
     own_x.wait()
     acc[0] = jnp.zeros((EXP, LANES), F32)
 
-    def x_tile(s, n):
-        return xq[tile_quad(n), s, pl.ds(n % 3, IN, stride=3), :]
-
-    def c_tile(s, n):
-        return cq[tile_quad(n), s, pl.ds(n % 3, IN, stride=3), :]
+    def fetch(quads, s, n):
+        tile = quads[tile_quad(n), s, pl.ds(n % 3, IN, stride=3), :]
+        return tile if n < HALF_W else pltpu.roll(tile, 8, 1)
+
+    def place_back(quads, s, n, tile):
+        tile = tile if n < HALF_W else pltpu.roll(tile, LANES - 8, 1)
+        quads[tile_quad(n), s, pl.ds(n % 3, IN, stride=3), :] = tile
 
     def later_bin(low, high):
         return (
-            jnp.where(high_bin, pltpu.roll(high, 7, 1), pltpu.roll(low, LANES - 1, 1)),
+            pltpu.roll(jnp.where(low_bin, high, low), LANES - 1, 1),
             jnp.where(high_bin, 0.0, pltpu.roll(high, LANES - 1, 1)),
         )
 
     def earlier_bin(low, high):
         return (
             jnp.where(low_bin, 0.0, pltpu.roll(low, 1, 1)),
-            jnp.where(low_bin, pltpu.roll(low, LANES - 7, 1), pltpu.roll(high, 1, 1)),
+            pltpu.roll(jnp.where(high_bin, low, high), 1, 1),
         )
 
-    def from_before(tiles, k):
-        return pltpu.roll(jnp.where(last_row, tiles[max(k - 1, 0)], tiles[k]), 8, 1)
-
-    def from_after(tiles, k):
-        return pltpu.roll(jnp.where(first_row, tiles[min(k + 1, HALF_W - 1)], tiles[k]), LANES - 8, 1)
+    def from_before(tiles, k, half):
+        edge = first_row if half else last_row
+        return pltpu.roll(jnp.where(edge, tiles[(k - 1) % HALF_W], tiles[k]), 8, 1)
+
+    def from_after(tiles, k, half):
+        edge = second_row if half else first_row
+        return pltpu.roll(jnp.where(edge, tiles[(k + 1) % HALF_W], tiles[k]), LANES - 8, 1)
 
     def forward_slot(s, carry):
         for step in range(1, QUADS):
             x_copy(step, s).wait_recv()
         for n in range(WIDE):
-            tile = jnp.concatenate([x_tile(s, n) - mean_col, one_rows], axis=0)
-            high, low = halves(tile)
+            tile = fetch(xq, s, n)
+            x3[s, :, on_lane(n)] = tile
+            high, low = halves(jnp.concatenate([tile - mean_col, one_rows], axis=0))
             xs[s, 0:32, on_lane(n)] = high
             xs[s, 32:64, on_lane(n)] = low
             xs[s, 64:96, on_lane(n)] = high
@@ -314,10 +331,9 @@
             c_copy(step, s).start()
         v1[s] = nn(w1t[...], xs[s])
 
-        def taps_step(j, carry):
+        def bins_step(j, carry):
             rows = pl.ds(pl.multiple_of(8 * j, 8), 8)
             wt = [tab[t, rows, :] for t in range(TAPS)]
-            keep = [[[None] * HALF_W for _ in range(2)] for _ in range(3)]
             for k in range(HALF_W):
                 pair = []
                 for half in range(2):
@@ -326,26 +342,32 @@
                 nxt = later_bin(*pair)
                 prv = earlier_bin(*pair)
                 for half in range(2):
-                    for p in range(3):
-                        keep[p][half][k] = (
+                    for p, target in enumerate((dm, dh, dp)):
+                        target[rows, on_lane(half * HALF_W + k)] = (
                             wt[3 * p] * prv[half] + wt[3 * p + 1] * pair[half] + wt[3 * p + 2] * nxt[half]
                         )
+            return carry
+
+        def frames_step(j, carry):
+            rows = pl.ds(pl.multiple_of(8 * j, 8), 8)
             got = zero_tile
-            for k in range(HALF_W):
-                back_ok = msk[0, s, :, on_lane(k)]
-                fore_ok = msk[1, s, :, on_lane(k)]
-                for half in range(2):
+            for half in range(2):
+                prior = [dm[rows, on_lane(half * HALF_W + k)] for k in range(HALF_W)]
+                later = [dp[rows, on_lane(half * HALF_W + k)] for k in range(HALF_W)]
+                for k in range(HALF_W):
+                    where = on_lane(half * HALF_W + k)
                     value = (
-                        keep[1][half][k]
-                        + back_ok * from_before(keep[0][half], k)
-                        + fore_ok * from_after(keep[2][half], k)
+                        dh[rows, where]
+                        + msk[0, s, :, where] * from_before(prior, k, half)
+                        + msk[1, s, :, where] * from_after(later, k, half)
                     )
-                    a2[s, rows, on_lane(half * HALF_W + k)] = value
+                    a2[s, rows, where] = value
                     got = got + value
             acc[0, rows, :] = acc[0, rows, :] + got
             return carry
 
-        lax.fori_loop(0, EXP // 8, taps_step, 0)
+        lax.fori_loop(0, EXP // 8, bins_step, 0, unroll=9)
+        lax.fori_loop(0, EXP // 8, frames_step, 0, unroll=9)
         return carry
 
     lax.fori_loop(0, slots, forward_slot, 0)
@@ -364,7 +386,7 @@
             acc[2, rows, :] = acc[2, rows, :] + got
             return carry
 
-        return lax.fori_loop(0, EXP // 8, tile_step, carry)
+        return lax.fori_loop(0, EXP // 8, tile_step, carry, unroll=3)
 
     lax.fori_loop(0, slots, square_step, 0)
     rb[0, me, 0:2, :] = split_row(lane_sums(acc[0]) * (1.0 / n_loc))
@@ -399,7 +421,7 @@
                 hh[s, low_rows, on_lane(n)] = low
             return carry
 
-        lax.fori_loop(0, EXP // 16, step, 0)
+        lax.fori_loop(0, EXP // 16, step, 0, unroll=3)
         pooled[...] = pooled[...] + nt(hot[s], hh[s, 0:EXP, :]) + nt(hot[s], hh[s, EXP:, :])
         return carry
 
@@ -420,7 +442,7 @@
         return jnp.concatenate([project * rows[r : r + 1] for r in range(REGIONS)], axis=0)
 
     def region_tile(r, s, n):
-        return jnp.concatenate([reg[r, s, :, on_lane(n % HALF_W)]] * (IN // 8), axis=0)
+        return jnp.concatenate([reg[r, s, :, on_lane(n)]] * (IN // 8), axis=0)
 
     def project_slot(s, carry):
         total_a, total_c = carry
@@ -438,7 +460,9 @@
                 )
             a3[s, :, on_lane(n)] = value
             total_a = total_a + value
-            total_c = total_c + c_tile(s, n)
+            upstream = fetch(cq, s, n)
+            c3[s, :, on_lane(n)] = upstream
+            total_c = total_c + upstream
         return total_a, total_c
 
     own_c.wait()
@@ -451,7 +475,7 @@
         for n in range(WIDE):
             off = a3[s, :, on_lane(n)] - center3
             square = square + off * off
-            cross = cross + off * c_tile(s, n)
+            cross = cross + off * c3[s, :, on_lane(n)]
         return square, cross
 
     square3, cross3 = lax.fori_loop(0, slots, third_step, (zero24, zero24))
@@ -498,8 +522,8 @@
     def back_slot(s, carry):
         for n in range(WIDE):
             off = a3[s, :, on_lane(n)] - mean3_c
-            xloc[tile_quad(n), s, pl.ds(n % 3, IN, stride=3), :] = x_tile(s, n) + off * grow3_c + lift3_c
-            grad = grow3_c * c_tile(s, n) - flat3_c - off * lean3_c
+            place_back(xloc, s, n, x3[s, :, on_lane(n)] + off * grow3_c + lift3_c)
+            grad = grow3_c * c3[s, :, on_lane(n)] - flat3_c - off * lean3_c
             high, low = halves(
                 jnp.concatenate(
                     [grad * region_tile(r, s, n) for r in range(REGIONS)], axis=0
@@ -563,7 +587,7 @@
             acc[1, rows, :] = acc[1, rows, :] + cross
             return carry
 
-        lax.fori_loop(0, EXP // 8, step, 0)
+        lax.fori_loop(0, EXP // 8, step, 0, unroll=6)
         return carry
 
     lax.fori_loop(0, slots, second_back_slot, 0)
@@ -594,52 +618,66 @@
     small[2] = jnp.zeros((IN, EXP), F32)
 
     def taps_back_slot(s, carry):
-        def step(j, carry):
+        def frames_step(j, carry):
+            rows = pl.ds(pl.multiple_of(8 * j, 8), 8)
+            k1, k2, k3 = (tab[TAPS + i, rows, :] for i in range(3))
+            for half in range(2):
+                grads = []
+                for k in range(HALF_W):
+                    where = on_lane(half * HALF_W + k)
+                    grads.append(k1 * dn2[s, rows, where] + k2 * a2[s, rows, where] + k3)
+                for k in range(HALF_W):
+                    where = on_lane(half * HALF_W + k)
+                    dn2[s, rows, where] = grads[k]
+                    dm[rows, where] = msk[1, s, :, where] * from_after(grads, k, half)
+                    dp[rows, where] = msk[0, s, :, where] * from_before(grads, k, half)
+            return carry
+
+        def bins_step(j, carry):
             rows = pl.ds(pl.multiple_of(8 * j, 8), 8)
             wt = [tab[t, rows, :] for t in range(TAPS)]
-            k1, k2, k3 = (tab[TAPS + i, rows, :] for i in range(3))
-            grads = [[], []]
-            for half in range(2):
-                for k in range(HALF_W):
+            for k in range(HALF_W):
+                mix = [[], [], []]
+                us, hs = [], []
+                for half in range(2):
                     where = on_lane(half * HALF_W + k)
-                    grads[half].append(k1 * dn2[s, rows, where] + k2 * a2[s, rows, where] + k3)
-            sums = [zero_tile] * TAPS
-            for k in range(HALF_W):
-                back_ok = msk[0, s, :, on_lane(k)]
-                fore_ok = msk[1, s, :, on_lane(k)]
-                vs, us, hs = [], [], []
-                for half in range(2):
-                    v = v1[s, rows, on_lane(half * HALF_W + k)]
+                    moved = [dm[rows, where], dn2[s, rows, where], dp[rows, where]]
+                    for q in range(3):
+                        mix[q].append(wt[q] * moved[0] + wt[3 + q] * moved[1] + wt[6 + q] * moved[2])
+                    v = v1[s, rows, where]
                     u = 1.0 + jnp.tanh(v)
-                    vs.append(v)
                     us.append(u)
                     hs.append(v * u)
-                near = [earlier_bin(*hs), hs, later_bin(*hs)]
-                mix = [[], [], []]
-                for half in range(2):
-                    moved = [
-                        fore_ok * from_after(grads[half], k),
-                        grads[half][k],
-                        back_ok * from_before(grads[half], k),
-                    ]
-                    for q in range(3):
-                        mix[q].append(
-                            wt[q] * moved[0] + wt[3 + q] * moved[1] + wt[6 + q] * moved[2]
-                        )
-                        for p in range(3):
-                            sums[3 * p + q] = sums[3 * p + q] + moved[p] * near[q][half]
                 left = later_bin(*mix[0])
                 right = earlier_bin(*mix[2])
                 for half in range(2):
-                    d = (left[half] + mix[1][half] + right[half]) * (
+                    dh[rows, on_lane(half * HALF_W + k)] = (left[half] + mix[1][half] + right[half]) * (
                         us[half] + hs[half] * (2.0 - us[half])
                     )
-                    dh[rows, on_lane(half * HALF_W + k)] = d
+            return carry
+
+        def taps_step(j, carry):
+            rows = pl.ds(pl.multiple_of(8 * j, 8), 8)
+            sums = [zero_tile] * TAPS
+            for k in range(HALF_W):
+                hs = []
+                for half in range(2):
+                    v = v1[s, rows, on_lane(half * HALF_W + k)]
+                    hs.append(v + v * jnp.tanh(v))
+                near = [earlier_bin(*hs), hs, later_bin(*hs)]
+                for half in range(2):
+                    where = on_lane(half * HALF_W + k)
+                    moved = [dm[rows, where], dn2[s, rows, where], dp[rows, where]]
+                    for q in range(3):
+                        for p in range(3):
+                            sums[3 * p + q] = sums[3 * p + q] + moved[p] * near[q][half]
             for t in range(TAPS):
                 acc[t, rows, :] = acc[t, rows, :] + sums[t]
             return carry
 
-        lax.fori_loop(0, EXP // 8, step, 0)
+        lax.fori_loop(0, EXP // 8, frames_step, 0, unroll=9)
+        lax.fori_loop(0, EXP // 8, bins_step, 0, unroll=9)
+        lax.fori_loop(0, EXP // 8, taps_step, 0, unroll=6)
 
         def pack(j, carry):
             rows = pl.ds(pl.multiple_of(16 * j, 16), 16)
@@ -650,7 +688,7 @@
                 hh[s, low_rows, on_lane(n)] = low
             return carry
 
-        lax.fori_loop(0, EXP // 16, pack, 0)
+        lax.fori_loop(0, EXP // 16, pack, 0, unroll=3)
         main = nt(xs[s, 0:64, :], hh[s, 0:EXP, :])
         main = main[0:32] + main[32:64] + nt(xs[s, 0:32, :], hh[s, EXP:, :])
         small[1] = small[1] + main[0:IN]
@@ -659,7 +697,10 @@
 
     lax.fori_loop(0, slots, taps_back_slot, 0)
 
-    stacked = [small[0], small[1], small[2, 0:8, :]]
+    stacked = [small[0], small[1]]
+    cross1 = jnp.sum(small[1] * weight, axis=0, keepdims=True)
+    rb[3, me, 0:2, :] = split_row(small[2, 0:1, :])
+    rb[3, me, 2:4, :] = split_row(cross1)
     tail = [lane_sums(acc[t]) for t in range(TAPS)]
     tail.append(excite_bias_grad)
     tail.append(jnp.concatenate([reduce_bias_grad, jnp.zeros((1, EXP - SQZ), F32)], axis=1))
@@ -668,7 +709,7 @@
     for part in (excite_grad, reduce_grad):
         stacked.append(jnp.concatenate([part, jnp.zeros((8 - SQZ, EXP), F32)], axis=0))
     stacked = jnp.concatenate(stacked, axis=0)
-    n_heads = 11
+    n_heads = 10
     for i in range(n_heads):
         bulk[i] = stacked[8 * i : 8 * i + 8, :LANES]
     ends = [stacked[8 * i : 8 * i + 8, LANES:] for i in range(n_heads)]
@@ -690,11 +731,48 @@
         other = lax.rem(place + step, GROUP)
         group_copy(bulk.at[pl.ds(each * other, each)], bulk_in.at[place], 4, step).start()
     bulk_in[place] = bulk[pl.ds(each * place, each)]
+    spread_start(rb.at[3, me], rb.at[3, me], 7)
     done = group_copy(bulk_in.at[pl.ds(0, GROUP - 1)], bulk_in.at[pl.ds(0, GROUP - 1)], 4, 1)
     done.wait_send()
     done.wait_recv()
     bulk_all[me] = jnp.sum(bulk_in[...], axis=0)
     spread_start(bulk_all.at[me], bulk_all.at[me], 5)
+    spread_wait(rb.at[3, pl.ds(0, n_dev - 1)], 7)
+    sums = jnp.sum(rb[3], axis=0)
+    bias1_grad = join_row(sums[0:2])
+    gain1_grad = scale1 * join_row(sums[2:4])
+    lean1 = scale1 * gain1_grad * (1.0 / total)
+
+    for step in range(1, QUADS):
+        def o_done(s, carry, step=step):
+            o_copy(step, s).wait_send()
+            x_copy(step, s).wait_send()
+            c_copy(step, s).wait_send()
+            return carry
+
+        lax.fori_loop(0, slots, o_done, 0)
+    grown = weight * grow1
+    grown_high = grown.astype(BF16)
+    grown_both = jnp.concatenate([grown_high.astype(F32), grown - grown_high.astype(F32)], axis=0).astype(BF16)
+    lean_map = -nt(grown * lean1, weight, FULL)
+    flat_col = -jnp.sum(grown * (bias1_grad * (1.0 / total)), axis=1, keepdims=True)
+    side = jnp.concatenate([lean_map, flat_col, jnp.zeros((IN, 7), F32)], axis=1)
+    side_high = side.astype(BF16).astype(F32)
+    wlow[...] = jnp.concatenate([side_high, side_high, side - side_high], axis=1).astype(BF16)
+
+    def last_slot(s, carry):
+        main = nn(grown_both, hh[s, 0:EXP, :])
+        main = main[:IN] + main[IN:] + nn(grown_high, hh[s, EXP:, :]) + nn(wlow[...], xs[s])
+        for n in range(WIDE):
+            place_back(xq, s, n, c3[s, :, on_lane(n)] + main[:, n * LANES : (n + 1) * LANES])
+        for step in range(1, QUADS):
+            g_copy(step, s).start()
+        return carry
+
+    lax.fori_loop(0, slots, last_slot, 0)
+    own_g = pltpu.make_async_copy(xq.at[space], ing.at[pl.ds(slots * space, slots)], own_sem.at[3])
+    own_g.start()
+
     spread_wait(bulk_all.at[pl.ds(0, n_dev - 1)], 5)
     summed = []
     for i in range(n_heads + 2):
@@ -709,13 +787,9 @@
 
     project_grad = jnp.concatenate([row_tile(i) for i in range(3)], axis=0)
     expand_cross = jnp.concatenate([row_tile(i) for i in range(3, 6)], axis=0)
-    bias1_grad = row_tile(6)[0:1]
-    depth_tiles = jnp.concatenate([row_tile(7), row_tile(8)], axis=0)
-    excite_tile = row_tile(9)
-    reduce_tile = row_tile(10)
-    cross1 = jnp.sum(expand_cross * weight, axis=0, keepdims=True)
-    gain1_grad = scale1 * cross1
-    lean1 = scale1 * gain1_grad * (1.0 / total)
+    depth_tiles = jnp.concatenate([row_tile(6), row_tile(7)], axis=0)
+    excite_tile = row_tile(8)
+    reduce_tile = row_tile(9)
     expand_grad = grow1 * (expand_cross - lean1 * moment_w)
     zero_rows = jnp.zeros((16, EXP), F32)
     gs_out[0] = expand_grad
@@ -738,46 +812,14 @@
         axis=0,
     )
 
-    for step in range(1, QUADS):
-        def o_done(s, carry, step=step):
-            o_copy(step, s).wait_send()
-            x_copy(step, s).wait_send()
-            c_copy(step, s).wait_send()
-            return carry
-
-        lax.fori_loop(0, slots, o_done, 0)
-    grown = weight * grow1
-    grown_high = grown.astype(BF16)
-    grown_both = jnp.concatenate([grown_high.astype(F32), grown - grown_high.astype(F32)], axis=0).astype(BF16)
-    lean_map = -nt(grown * lean1, weight, FULL)
-    flat_col = -jnp.sum(grown * (bias1_grad * (1.0 / total)), axis=1, keepdims=True)
-    side = jnp.concatenate([lean_map, flat_col, jnp.zeros((IN, 7), F32)], axis=1)
-    side_high = side.astype(BF16).astype(F32)
-    wlow[...] = jnp.concatenate([side_high, side_high, side - side_high], axis=1).astype(BF16)
-
-    def last_slot(s, carry):
-        main = nn(grown_both, hh[s, 0:EXP, :])
-        main = main[:IN] + main[IN:] + nn(grown_high, hh[s, EXP:, :]) + nn(wlow[...], xs[s])
-        for n in range(WIDE):
-            xq[tile_quad(n), s, pl.ds(n % 3, IN, stride=3), :] = (
-                c_tile(s, n) + main[:, n * LANES : (n + 1) * LANES]
-            )
-        for step in range(1, QUADS):
-            g_copy(step, s).start()
-        return carry
-
-    lax.fori_loop(0, slots, last_slot, 0)
-    own_g = pltpu.make_async_copy(xq.at[space], ing.at[pl.ds(slots * space, slots)], own_sem.at[3])
-    own_g.start()
-
     mine = jnp.minimum(place, 4)
     grad = gs_out[mine]
     turned = (mine == 1) | (mine == 2)
     small[...] = jnp.zeros(small.shape, F32)
     small[0, :, :IN] = in_st[0]
     small[1, :, :IN] = jnp.transpose(in_st[1])
-    small[2, :SQZ, :SQZ] = jnp.transpose(sq_st[0])
-    small[3, :SQZ, :SQZ] = sq_st[1]
+    small[2, :SQZ, :SQZ] = jnp.transpose(sq_st[:, 0, :])
+    small[3, :SQZ, :SQZ] = sq_st[:, 1, :]
     small[4, :TAPS, :TAPS] = tap_st[...]
     old_big = big[mine]
     old_big = jnp.where(turned, jnp.transpose(old_big), old_big)
@@ -798,13 +840,13 @@
         big_m, small_m, direction, small_h = carry
         big_k = 1.25 * big_eye - 0.25 * big_m
         small_k = 1.25 * small_eye - 0.25 * small_m
-        direction = nn(direction, big_k, FULL)
-        small_h = nn(small_h, small_k, FULL)
-        big_k = nn(big_k, big_k, FULL)
-        small_k = nn(small_k, small_k, FULL)
-        big_k = nn(big_k, big_k, FULL)
-        small_k = nn(small_k, small_k, FULL)
-        return nn(big_k, big_m, FULL), nn(small_k, small_m, FULL), direction, small_h
+        direction = nn(direction, big_k, MID)
+        small_h = nn(small_h, small_k, MID)
+        big_k = nn(big_k, big_k, MID)
+        small_k = nn(small_k, small_k, MID)
+        big_k = nn(big_k, big_k, MID)
+        small_k = nn(small_k, small_k, MID)
+        return nn(big_k, big_m, MID), nn(small_k, small_m, MID), direction, small_h
 
     _, _, direction, small_h = lax.fori_loop(
         0, ROOT_ITERS, root_step, (big_m, small_m, direction, small_h)
@@ -840,11 +882,27 @@
 
 
 def finish_kernel(
-    gs, nw, big, in_st, sq_st, tap_st,
-    ge, gd, gr_t, gx, gp_t, ne, nd, nr_t, nx, np_t, big_new, in_new, sq_new, tap_new,
+    gs, nw, vr, big, in_st, sq_st, tap_st, vec, vec_m, field_a, field_b,
+    out, ing, ge, gd, gr_t, gx, gp_t, ne, nd, nr_t, nx, np_t, big_new, in_new, sq_new, tap_new, vg, vm, vn, held, sem,
 ):
+    fields = ((field_a, out), (field_b, ing))
+    loads = [pltpu.make_async_copy(source, held.at[i], sem.at[i]) for i, (source, _) in enumerate(fields)]
+    stores = [pltpu.make_async_copy(held.at[i], target, sem.at[i]) for i, (_, target) in enumerate(fields)]
+    for load in loads:
+        load.start()
     ge[...], gp_t[...], gr_t[...], gx[...], gd[...] = gs[0], gs[1], gs[2, :SQZ], gs[3, :SQZ], gs[4, :TAPS]
     ne[...], np_t[...], nr_t[...], nx[...], nd[...] = nw[0], nw[1], nw[2, :SQZ], nw[3, :SQZ], nw[4, :TAPS]
+    start = 0
+    for i, width in enumerate(PARTS):
+        vg[:, start : start + width] = vr[i : i + 1, :width]
+        start = start + width
+    grads = vg[...]
+    moments = DECAY * vec_m[...] + FRESH * grads * grads
+    vm[...] = moments
+    vn[...] = vec[...] - VECTOR_RATE * grads / (jnp.sqrt(moments) + 1e-08)
+    for load, store in zip(loads, stores):
+        load.wait()
+        store.start()
     for i in range(5):
         grad = gs[i]
         big_new[i] = DECAY * big[i] + FRESH * tn(grad, grad, FULL)
@@ -852,9 +910,11 @@
         if i < 2:
             in_new[i] = DECAY * in_st[i] + inner
         elif i < 4:
-            sq_new[i - 2] = DECAY * sq_st[i - 2] + inner[:SQZ, :SQZ]
+            sq_new[:, i - 2, :] = DECAY * sq_st[:, i - 2, :] + inner[:SQZ, :SQZ]
         else:
             tap_new[...] = DECAY * tap_st[...] + inner[:TAPS, :TAPS]
+    for store in stores:
+        store.wait()
 
 
 def on_device(
@@ -865,11 +925,9 @@
     slot_count = features.shape[0]
     slots = slot_count // QUADS
     n_pos = slot_count * (n_dev // n_space) * FRAMES * BINS
-    cuts = [0, EXP, 2 * EXP, 3 * EXP, 4 * EXP, 4 * EXP + IN, 4 * EXP + 2 * IN, 4 * EXP + 2 * IN + SQZ]
-    cuts.append(cuts[-1] + EXP)
-    pieces = [vector_params[a:b] for a, b in zip(cuts[:-1], cuts[1:])]
-    prm = jnp.stack([jnp.pad(piece, (0, EXP - piece.shape[0])) for piece in pieces])
     vm = pl.BlockSpec(memory_space=pltpu.VMEM)
+    vec = vector_params.reshape(1, -1)
+    sq_rows = sq_stats.transpose(1, 0, 2)
     hbm = pl.BlockSpec(memory_space=pl.ANY)
     grid_shape = jax.ShapeDtypeStruct((slot_count, ROWS, LANES), F32)
     wide = WIDE * LANES
@@ -891,20 +949,25 @@
             vmem((QUADS, slots, ROWS, LANES), F32),
             vmem((QUADS, slots, ROWS, LANES), F32),
             vmem((slots, 96, wide), BF16),
+            vmem((slots, IN, wide), F32),
+            vmem((slots, IN, wide), F32),
             vmem((slots, EXP, wide), F32),
             vmem((slots, EXP, wide), F32),
             vmem((slots, 2 * EXP, wide), BF16),
             vmem((slots, EXP, wide), F32),
             vmem((EXP, wide), F32),
+            vmem((EXP, wide), F32),
+            vmem((EXP, wide), F32),
             vmem((slots, IN, wide), F32),
             vmem((slots, slots * REGIONS, wide), BF16),
             vmem((slots, 256, wide), BF16),
             vmem((TAPS + 3, EXP, LANES), F32),
-            vmem((2, slots, 8, HALF_W * LANES), F32),
-            vmem((REGIONS, slots, 8, HALF_W * LANES), F32),
+            vmem((2, slots, 8, wide), F32),
+            vmem((REGIONS, slots, 8, wide), F32),
             vmem((TAPS, EXP, LANES), F32),
             vmem((EXP, 96), BF16),
             vmem((IN, 96), BF16),
+            vmem((8, EXP), F32),
             vmem((5, IN, EXP), F32),
             vmem((slots * REGIONS, EXP), F32),
             vmem((slots, REGIONS, EXP), F32),
@@ -913,7 +976,7 @@
             vmem((GROUP, BULK // GROUP, 8, LANES), F32),
             vmem((n_dev, BULK // GROUP, 8, LANES), F32),
             vmem((n_dev, 8, LANES), F32),
-            vmem((3, n_dev, 4, LANES), F32),
+            vmem((4, n_dev, 4, LANES), F32),
             vmem((GROUP, IN, EXP), F32),
             vmem((IN, LANES), F32),
             dma((QUADS,)),
@@ -926,27 +989,29 @@
     )(
         features.reshape(slot_count, ROWS, LANES),
         cotangent.reshape(slot_count, ROWS, LANES),
-        segment_ids, w_expand, w_depth, w_reduce.T, w_excite, w_project.T, prm,
-        big_stats, in_stats, sq_stats, tap_stats,
+        segment_ids, w_expand, w_depth, w_reduce.T, w_excite, w_project.T, vec,
+        big_stats, in_stats, sq_rows, tap_stats,
     )
     shape = jax.ShapeDtypeStruct
-    ge, gd, gr_t, gx, gp_t, ne, nd, nr_t, nx, np_t, big_new, in_new, sq_new, tap_new = pl.pallas_call(
+    (
+        out, ing, ge, gd, gr_t, gx, gp_t, ne, nd, nr_t, nx, np_t, big_new, in_new, sq_new, tap_new, vg, vm_new, vn
+    ) = pl.pallas_call(
         finish_kernel,
-        out_shape=tuple(
+        out_shape=(grid_shape, grid_shape) + tuple(
             shape(dims, F32)
             for dims in [(IN, EXP), (TAPS, EXP), (SQZ, EXP), (SQZ, EXP), (IN, EXP)] * 2
-            + [(5, EXP, EXP), (2, IN, IN), (2, SQZ, SQZ), (TAPS, TAPS)]
+            + [(5, EXP, EXP), (2, IN, IN), (SQZ, 2, SQZ), (TAPS, TAPS)]
+            + [vec.shape] * 3
         ),
-        in_specs=[vm] * 6,
-        out_specs=(vm,) * 14,
-    )(gs, nw, big_stats, in_stats, sq_stats, tap_stats)
-    vector_grads = jnp.concatenate([vr[i, : cuts[i + 1] - cuts[i]] for i in range(8)])
-    moments_new = DECAY * vector_moments + FRESH * vector_grads * vector_grads
-    vector_new = vector_params - VECTOR_RATE * vector_grads / (jnp.sqrt(moments_new) + 1e-08)
+        in_specs=[vm] * 9 + [hbm] * 2,
+        out_specs=(hbm, hbm) + (vm,) * 17,
+        scratch_shapes=[vmem((2,) + grid_shape.shape, F32), dma((2,))],
+        compiler_params=pltpu.CompilerParams(vmem_limit_bytes=32 << 20),
+    )(gs, nw, vr, big_stats, in_stats, sq_rows, tap_stats, vec, vector_moments.reshape(1, -1), out, ing)
     return (
         out.reshape(features.shape), ing.reshape(features.shape),
         ge, gd, gr_t.T, gx, gp_t.T, ne, nd, nr_t.T, nx, np_t.T,
-        big_new, in_new, sq_new, tap_new, vector_grads, moments_new, vector_new,
+        big_new, in_new, sq_new.transpose(1, 0, 2), tap_new, vg.reshape(-1), vm_new.reshape(-1), vn.reshape(-1),
     )
 
 

time: 176 us -> 134 us (0.76)
  Pallas kernels: 161 us -> 124 us
  local copies, waits for them, and re-layouts: 12.4 us -> 7.01 us
    pallas_call x1, Pallas kernels: 158 us -> 121 us  [on_device(): pl.pallas_call(functools.partial(block_kernel, n_dev, n_space, slots, n_p...]
    slice x4 -> x0, local copies, waits for them, and re-layouts: 3.42 us -> none  [the longest x3 2.54 us: on_device(): pieces = [vector_params[a:b] for a, b in zip(cuts[:-1], cuts[1:])]]
    reshape x0 -> x2, local copies, waits for them, and re-layouts: none -> 1.96 us  [the longest x1 1.27 us: on_device(): vec = vector_params.reshape(1, -1)]
    pallas_call x0 -> x3, other arithmetic: none -> 1.82 us  [on_device(): pl.pallas_call(finish_kernel, out_shape=(grid_shape, grid_shape) + tuple(...]
    unnamed x12 -> x20, local copies, waits for them, and re-layouts: 6.8 us -> 5.06 us
where the time goes in v2:
time: 134 us
  Pallas kernels  124 us (93%)
  local copies, waits for them, and re-layouts  7.01 us (5%)
  other arithmetic  1.82 us (1%)
    pallas_call x1, Pallas kernels, on_device(): pl.pallas_call(functools.partial(block_kernel, n_dev, n_space, slots, n_p...  121 us
    unnamed x20, local copies, waits for them, and re-layouts  5.06 us
    pallas_call x1, Pallas kernels, on_device(): pl.pallas_call(finish_kernel, out_shape=(grid_shape, grid_shape) + tuple(...  3.23 us

profile of v2, /device:TPU:0, one launch (start us, length us, event | category | flops | bytes accessed | tf_op | source)
XLA Modules:
  0.0 133.9 jit_solution(5864135248795276805)
XLA Ops:
  0.7 1.3 reshape.67.vec
  1.9 0.7 reshape.68.vec_m
  2.6 0.0 copy-start
  2.6 0.0 copy-start.5
  2.6 0.0 copy-start.6
  2.6 0.0 copy-start.7
  2.6 0.0 copy-start.8
  2.6 121.1 %shard_map.285 = (f32[32,72,128]{2,1,0:T(8,128)}, f32[32,72,128]{2,1,0:T(8,128)}, f32[5,24,144]{2,1,0:T(8,128)}, f32[5,24,144]{2,1,0:T(8,128)}, f32[8,144]{1,0:T(8,128)}) custom-call(f32[32,72,128]{2,1,0:T(8,128)} %bitcast.14, f32[32,72,128]{2,1,0:T(8,128)} %bitcast.15, s32[32,96]{1,0:T(8,128)} %ids_ref.1, f32[24,144]{1,0:T(8,128)} %w_exp.1, ...), custom_call_target="tpu_custom_call" | custom-call | tf_op jit(solution)/shard_map/pallas_call | solution.py:936
  123.7 0.0 copy-done
  123.7 0.0 copy-done.5
  123.7 0.0 copy-done.6
  123.7 0.0 copy-done.7
  123.7 0.0 copy-done.8
  123.8 0.0 copy-start.1
  123.8 1.3 copy-done.1
  125.0 0.0 copy-start.2
  125.0 1.3 copy-done.2
  126.3 0.0 copy-start.3
  126.3 0.9 copy-done.3
  127.2 0.0 copy-start.4
  127.2 0.9 copy-done.4
  128.1 0.0 copy-start.9
  128.1 0.7 copy-done.9
  128.8 3.2 %shard_map.286 = (f32[32,72,128]{2,1,0:T(8,128)}, f32[32,72,128]{2,1,0:T(8,128)}, f32[24,144]{1,0:T(8,128)}, f32[9,144]{1,0:T(8,128)}, f32[6,144]{1,0:T(8,128)},...) custom-call(f32[5,24,144]{2,1,0:T(8,128)S(1)} %copy-done.3, ...), custom_call_target="tpu_custom_call" | custom-call | tf_op jit(solution)/shard_map/pallas_call | solution.py:998
  132.0 0.6 reduce
  132.6 0.6 reduce.1
  133.3 0.6 reduce.2
Async XLA Ops:
  2.6 121.1 %copy-start = (f32[5,144,144]{2,1,0:T(8,128)S(1)}, f32[5,144,144]{2,1,0:T(8,128)}, u32[]{:S(2)}) copy-start(f32[5,144,144]{2,1,0:T(8,128)} %big.3) | copy-start | bytes 1244164
  2.6 121.1 %copy-start.5 = (f32[2,24,24]{2,1,0:T(8,128)S(1)}, f32[2,24,24]{2,1,0:T(8,128)}, u32[]{:S(2)}) copy-start(f32[2,24,24]{2,1,0:T(8,128)} %in_st.3) | copy-start | bytes 13828
  2.6 121.1 %copy-start.6 = (f32[9,9]{1,0:T(8,128)S(1)}, f32[9,9]{1,0:T(8,128)}, u32[]{:S(2)}) copy-start(f32[9,9]{1,0:T(8,128)} %tap_st.3) | copy-start | bytes 976
  2.6 121.1 %copy-start.7 = (f32[1,774]{1,0:T(1,128)S(1)}, f32[1,774]{1,0:T(1,128)}, u32[]{:S(2)}) copy-start(f32[1,774]{1,0:T(1,128)} %reshape.67.vec) | copy-start | bytes 9292
  2.6 121.1 %copy-start.8 = (f32[2,6,6]{2,0,1:T(2,128)S(1)}, f32[2,6,6]{2,0,1:T(2,128)}, u32[]{:S(2)}) copy-start(f32[2,6,6]{2,0,1:T(2,128)} %param.26) | copy-start | bytes 868
  123.8 1.3 copy-start.1
  125.0 1.3 copy-start.2
  126.3 0.9 copy-start.3
  127.2 0.9 copy-start.4
  128.1 0.7 copy-start.9

commit v3 on v2

--- a/solution.py
+++ b/solution.py
@@ -148,7 +148,7 @@
         both = jnp.concatenate([high, low], axis=0)
         return gram + nt(both, both)
 
-    gram = lax.fori_loop(0, slots, gram_step, jnp.zeros((64, 64), F32))
+    gram = lax.fori_loop(0, slots, gram_step, jnp.zeros((64, 64), F32), unroll=True)
     gram = gram[:32, :32] + gram[32:, :32] + gram[:32, 32:] + gram[32:, 32:]
     off_row = gram[IN : IN + 1, :IN] * (1.0 / n_loc)
     off_col = gram[:IN, IN : IN + 1] * (1.0 / n_loc)
@@ -256,7 +256,7 @@
     start = 0
     prm[...] = jnp.zeros((8, EXP), F32)
     for i, width in enumerate(PARTS):
-        prm[i : i + 1, :width] = vec[:, start : start + width]
+        prm[i : i + 1, :width] = vec[pl.ds(start, width)].reshape(1, width)
         start = start + width
 
     spread_wait(rb1.at[pl.ds(0, n_dev - 1)], 0)
@@ -317,9 +317,10 @@
         edge = second_row if half else first_row
         return pltpu.roll(jnp.where(edge, tiles[(k + 1) % HALF_W], tiles[k]), LANES - 8, 1)
 
-    def forward_slot(s, carry):
-        for step in range(1, QUADS):
-            x_copy(step, s).wait_recv()
+    def tile_rows(j, height=8):
+        return pl.ds(height * j, height) if isinstance(j, int) else pl.ds(pl.multiple_of(height * j, height), height)
+
+    def expand_slot(s):
         for n in range(WIDE):
             tile = fetch(xq, s, n)
             x3[s, :, on_lane(n)] = tile
@@ -327,9 +328,15 @@
             xs[s, 0:32, on_lane(n)] = high
             xs[s, 32:64, on_lane(n)] = low
             xs[s, 64:96, on_lane(n)] = high
+        v1[s] = nn(w1t[...], xs[s])
+
+    def x_arrived(s):
+        for step in range(1, QUADS):
+            x_copy(step, s).wait_recv()
+
+    def forward_slot(s, carry):
         for step in range(1, QUADS):
             c_copy(step, s).start()
-        v1[s] = nn(w1t[...], xs[s])
 
         def bins_step(j, carry):
             rows = pl.ds(pl.multiple_of(8 * j, 8), 8)
@@ -349,7 +356,7 @@
             return carry
 
         def frames_step(j, carry):
-            rows = pl.ds(pl.multiple_of(8 * j, 8), 8)
+            rows = tile_rows(j)
             got = zero_tile
             for half in range(2):
                 prior = [dm[rows, on_lane(half * HALF_W + k)] for k in range(HALF_W)]
@@ -367,8 +374,18 @@
             return carry
 
         lax.fori_loop(0, EXP // 8, bins_step, 0, unroll=9)
-        lax.fori_loop(0, EXP // 8, frames_step, 0, unroll=9)
+
+        @pl.when(s < slots - 1)
+        def _():
+            x_arrived(s + 1)
+
+        expand_slot(jnp.minimum(s + 1, slots - 1))
+        for j in range(EXP // 8):
+            frames_step(j, 0)
         return carry
+
+    x_arrived(0)
+    expand_slot(0)
 
     lax.fori_loop(0, slots, forward_slot, 0)
 
@@ -407,10 +424,9 @@
 
     pooled[...] = jnp.zeros((slots * REGIONS, EXP), F32)
 
-    def activate_slot(s, carry):
-        def step(j, carry):
-            rows = pl.ds(pl.multiple_of(16 * j, 16), 16)
-            low_rows = pl.ds(pl.multiple_of(EXP + 16 * j, 16), 16)
+    def activate(s):
+        for j in range(EXP // 16):
+            rows, low_rows = pl.ds(16 * j, 16), pl.ds(EXP + 16 * j, 16)
             center, grow, lift = (tab[TAPS + i, rows, :] for i in range(3))
             for n in range(WIDE):
                 off = a2[s, rows, on_lane(n)] - center
@@ -419,13 +435,18 @@
                 high, low = halves(v + v * jnp.tanh(v))
                 hh[s, rows, on_lane(n)] = high
                 hh[s, low_rows, on_lane(n)] = low
-            return carry
-
-        lax.fori_loop(0, EXP // 16, step, 0, unroll=3)
+
+    def pool(s):
         pooled[...] = pooled[...] + nt(hot[s], hh[s, 0:EXP, :]) + nt(hot[s], hh[s, EXP:, :])
+
+    def activate_slot(s, carry):
+        pool(s - 1)
+        activate(s)
         return carry
 
-    lax.fori_loop(0, slots, activate_slot, 0)
+    activate(0)
+    lax.fori_loop(1, slots, activate_slot, 0)
+    pool(slots - 1)
 
     per_count = 1.0 / counts
     mean_pool = pooled[...] * per_count
@@ -519,7 +540,7 @@
 
     small[0] = jnp.zeros((IN, EXP), F32)
 
-    def back_slot(s, carry):
+    def project_back(s):
         for n in range(WIDE):
             off = a3[s, :, on_lane(n)] - mean3_c
             place_back(xloc, s, n, x3[s, :, on_lane(n)] + off * grow3_c + lift3_c)
@@ -535,6 +556,8 @@
         dcat[s, 224:256, :] = hot[s]
         for step in range(1, QUADS):
             o_copy(step, s).start()
+
+    def gate_back(s):
         main = nt(dcat[s, 0:224, :], hh[s, 0:EXP, :])
         main = main[0:96] + main[128:224] + nt(dcat[s, 0:96, :], hh[s, EXP:, :])
         project = w_pro_t[...]
@@ -545,9 +568,15 @@
             dgate[s, r : r + 1, :] = jnp.sum(part * project, axis=0, keepdims=True)
             gp = gp + part * rows[r : r + 1]
         small[0] = gp
+
+    def back_slot(s, carry):
+        gate_back(s - 1)
+        project_back(s)
         return carry
 
-    lax.fori_loop(0, slots, back_slot, 0)
+    project_back(0)
+    lax.fori_loop(1, slots, back_slot, 0)
+    gate_back(slots - 1)
     own_o = pltpu.make_async_copy(xloc.at[space], out.at[pl.ds(slots * space, slots)], own_sem.at[2])
     own_o.start()
 
@@ -565,32 +594,38 @@
     acc[0] = jnp.zeros((EXP, LANES), F32)
     acc[1] = jnp.zeros((EXP, LANES), F32)
 
-    def second_back_slot(s, carry):
+    def activation_back(s, target):
         high, low = halves(0.5 * gated_weights(s))
         pool_high, pool_low = halves(pooled[...])
         left = jnp.concatenate([high, pool_high, high, pool_low], axis=0)
-        dh[...] = tn(left, dcat[s]) + tn(low, dcat[s, 0:96, :])
-
-        def step(j, carry):
-            rows = pl.ds(pl.multiple_of(8 * j, 8), 8)
+        target[...] = tn(left, dcat[s]) + tn(low, dcat[s, 0:96, :])
+
+    def norm_back(s, source):
+        for j in range(EXP // 8):
+            rows = tile_rows(j)
             grow, lift = (tab[TAPS + i, rows, :] for i in (1, 2))
             plain, cross = zero_tile, zero_tile
             for n in range(WIDE):
                 off = a2[s, rows, on_lane(n)]
                 v = off * grow + lift
                 u = 1.0 + jnp.tanh(v)
-                d = dh[rows, on_lane(n)] * (u + (v * u) * (2.0 - u))
+                d = source[rows, on_lane(n)] * (u + (v * u) * (2.0 - u))
                 dn2[s, rows, on_lane(n)] = d
                 plain = plain + d
                 cross = cross + d * off
             acc[0, rows, :] = acc[0, rows, :] + plain
             acc[1, rows, :] = acc[1, rows, :] + cross
-            return carry
-
-        lax.fori_loop(0, EXP // 8, step, 0, unroll=6)
+
+    def second_back_pair(i, carry):
+        s = 2 * i
+        activation_back(s + 1, dm)
+        norm_back(s, dh)
+        activation_back(jnp.minimum(s + 2, slots - 1), dh)
+        norm_back(s + 1, dm)
         return carry
 
-    lax.fori_loop(0, slots, second_back_slot, 0)
+    activation_back(0, dh)
+    lax.fori_loop(0, slots // 2, second_back_pair, 0)
     rb[2, me, 0:2, :] = split_row(lane_sums(acc[0]))
     rb[2, me, 2:4, :] = split_row(lane_sums(acc[1]))
     spread_start(rb.at[2, me], rb.at[2, me], 3)
@@ -633,8 +668,9 @@
                     dp[rows, where] = msk[0, s, :, where] * from_before(grads, k, half)
             return carry
 
-        def bins_step(j, carry):
+        def bins_tile(j):
             rows = pl.ds(pl.multiple_of(8 * j, 8), 8)
+            out = [None] * WIDE
             wt = [tab[t, rows, :] for t in range(TAPS)]
             for k in range(HALF_W):
                 mix = [[], [], []]
@@ -651,13 +687,22 @@
                 left = later_bin(*mix[0])
                 right = earlier_bin(*mix[2])
                 for half in range(2):
-                    dh[rows, on_lane(half * HALF_W + k)] = (left[half] + mix[1][half] + right[half]) * (
+                    out[half * HALF_W + k] = (left[half] + mix[1][half] + right[half]) * (
                         us[half] + hs[half] * (2.0 - us[half])
                     )
+            return out
+
+        def bins_step(j, carry):
+            rows = pl.ds(pl.multiple_of(16 * j, 16), 16)
+            low_rows = pl.ds(pl.multiple_of(EXP + 16 * j, 16), 16)
+            for n, pair in enumerate(zip(bins_tile(2 * j), bins_tile(2 * j + 1))):
+                high, low = halves(jnp.concatenate(pair, axis=0))
+                hh[s, rows, on_lane(n)] = high
+                hh[s, low_rows, on_lane(n)] = low
             return carry
 
         def taps_step(j, carry):
-            rows = pl.ds(pl.multiple_of(8 * j, 8), 8)
+            rows = tile_rows(j)
             sums = [zero_tile] * TAPS
             for k in range(HALF_W):
                 hs = []
@@ -676,23 +721,13 @@
             return carry
 
         lax.fori_loop(0, EXP // 8, frames_step, 0, unroll=9)
-        lax.fori_loop(0, EXP // 8, bins_step, 0, unroll=9)
-        lax.fori_loop(0, EXP // 8, taps_step, 0, unroll=6)
-
-        def pack(j, carry):
-            rows = pl.ds(pl.multiple_of(16 * j, 16), 16)
-            low_rows = pl.ds(pl.multiple_of(EXP + 16 * j, 16), 16)
-            for n in range(WIDE):
-                high, low = halves(0.5 * dh[rows, on_lane(n)])
-                hh[s, rows, on_lane(n)] = high
-                hh[s, low_rows, on_lane(n)] = low
-            return carry
-
-        lax.fori_loop(0, EXP // 16, pack, 0, unroll=3)
+        lax.fori_loop(0, EXP // 16, bins_step, 0, unroll=True)
+        for j in range(EXP // 8):
+            taps_step(j, 0)
         main = nt(xs[s, 0:64, :], hh[s, 0:EXP, :])
         main = main[0:32] + main[32:64] + nt(xs[s, 0:32, :], hh[s, EXP:, :])
-        small[1] = small[1] + main[0:IN]
-        small[2, 0:8, :] = small[2, 0:8, :] + main[IN:32]
+        small[1] = small[1] + 0.5 * main[0:IN]
+        small[2, 0:8, :] = small[2, 0:8, :] + 0.5 * main[IN:32]
         return carry
 
     lax.fori_loop(0, slots, taps_back_slot, 0)
@@ -751,11 +786,11 @@
             return carry
 
         lax.fori_loop(0, slots, o_done, 0)
-    grown = weight * grow1
+    grown = 0.5 * weight * grow1
     grown_high = grown.astype(BF16)
     grown_both = jnp.concatenate([grown_high.astype(F32), grown - grown_high.astype(F32)], axis=0).astype(BF16)
-    lean_map = -nt(grown * lean1, weight, FULL)
-    flat_col = -jnp.sum(grown * (bias1_grad * (1.0 / total)), axis=1, keepdims=True)
+    lean_map = -2.0 * nt(grown * lean1, weight, FULL)
+    flat_col = -2.0 * jnp.sum(grown * (bias1_grad * (1.0 / total)), axis=1, keepdims=True)
     side = jnp.concatenate([lean_map, flat_col, jnp.zeros((IN, 7), F32)], axis=1)
     side_high = side.astype(BF16).astype(F32)
     wlow[...] = jnp.concatenate([side_high, side_high, side - side_high], axis=1).astype(BF16)
@@ -894,7 +929,7 @@
     ne[...], np_t[...], nr_t[...], nx[...], nd[...] = nw[0], nw[1], nw[2, :SQZ], nw[3, :SQZ], nw[4, :TAPS]
     start = 0
     for i, width in enumerate(PARTS):
-        vg[:, start : start + width] = vr[i : i + 1, :width]
+        vg[pl.ds(start, width)] = vr[i : i + 1, :width].reshape(width)
         start = start + width
     grads = vg[...]
     moments = DECAY * vec_m[...] + FRESH * grads * grads
@@ -926,7 +961,6 @@
     slots = slot_count // QUADS
     n_pos = slot_count * (n_dev // n_space) * FRAMES * BINS
     vm = pl.BlockSpec(memory_space=pltpu.VMEM)
-    vec = vector_params.reshape(1, -1)
     sq_rows = sq_stats.transpose(1, 0, 2)
     hbm = pl.BlockSpec(memory_space=pl.ANY)
     grid_shape = jax.ShapeDtypeStruct((slot_count, ROWS, LANES), F32)
@@ -989,7 +1023,7 @@
     )(
         features.reshape(slot_count, ROWS, LANES),
         cotangent.reshape(slot_count, ROWS, LANES),
-        segment_ids, w_expand, w_depth, w_reduce.T, w_excite, w_project.T, vec,
+        segment_ids, w_expand, w_depth, w_reduce.T, w_excite, w_project.T, vector_params,
         big_stats, in_stats, sq_rows, tap_stats,
     )
     shape = jax.ShapeDtypeStruct
@@ -1001,17 +1035,17 @@
             shape(dims, F32)
             for dims in [(IN, EXP), (TAPS, EXP), (SQZ, EXP), (SQZ, EXP), (IN, EXP)] * 2
             + [(5, EXP, EXP), (2, IN, IN), (SQZ, 2, SQZ), (TAPS, TAPS)]
-            + [vec.shape] * 3
+            + [vector_params.shape] * 3
         ),
         in_specs=[vm] * 9 + [hbm] * 2,
         out_specs=(hbm, hbm) + (vm,) * 17,
         scratch_shapes=[vmem((2,) + grid_shape.shape, F32), dma((2,))],
-        compiler_params=pltpu.CompilerParams(vmem_limit_bytes=32 << 20),
-    )(gs, nw, vr, big_stats, in_stats, sq_rows, tap_stats, vec, vector_moments.reshape(1, -1), out, ing)
+        compiler_params=pltpu.CompilerParams(vmem_limit_bytes=60 << 20),
+    )(gs, nw, vr, big_stats, in_stats, sq_rows, tap_stats, vector_params, vector_moments, out, ing)
     return (
         out.reshape(features.shape), ing.reshape(features.shape),
         ge, gd, gr_t.T, gx, gp_t.T, ne, nd, nr_t.T, nx, np_t.T,
-        big_new, in_new, sq_new.transpose(1, 0, 2), tap_new, vg.reshape(-1), vm_new.reshape(-1), vn.reshape(-1),
+        big_new, in_new, sq_new.transpose(1, 0, 2), tap_new, vg, vm_new, vn,
     )
 
 

time: 134 us -> 119 us (0.89)
  local copies, waits for them, and re-layouts: 7.01 us -> 0 us
  Pallas kernels: 124 us -> 118 us
  other arithmetic: 1.82 us -> 0 us
    pallas_call x1, Pallas kernels: 121 us -> 113 us  [on_device(): pl.pallas_call(functools.partial(block_kernel, n_dev, n_space, slots, n_p...]
    unnamed x20 -> x0, local copies, waits for them, and re-layouts: 5.06 us -> none
    reshape x2 -> x0, local copies, waits for them, and re-layouts: 1.96 us -> none  [the longest x1 1.27 us: on_device(): vec = vector_params.reshape(1, -1)]
    pallas_call x3 -> x0, other arithmetic: 1.82 us -> none  [on_device(): pl.pallas_call(finish_kernel, out_shape=(grid_shape, grid_shape) + tuple(...]
    pallas_call x1, Pallas kernels: 3.23 us -> 4.94 us  [on_device(): pl.pallas_call(finish_kernel, out_shape=(grid_shape, grid_shape) + tuple(...]
where the time goes in v3:
time: 119 us
  Pallas kernels  118 us (99%)
    pallas_call x1, Pallas kernels, on_device(): pl.pallas_call(functools.partial(block_kernel, n_dev, n_space, slots, n_p...  113 us
    pallas_call x1, Pallas kernels, on_device(): pl.pallas_call(finish_kernel, out_shape=(grid_shape, grid_shape) + tuple(...  4.94 us

profile of v3, /device:TPU:0, one launch (start us, length us, event | category | flops | bytes accessed | tf_op | source)
XLA Modules:
  0.0 118.5 jit_solution(1829128869213486382)
XLA Ops:
  0.7 112.9 %shard_map.285 = (f32[32,72,128]{2,1,0:T(8,128)}, f32[32,72,128]{2,1,0:T(8,128)}, f32[5,24,144]{2,1,0:T(8,128)}, f32[5,24,144]{2,1,0:T(8,128)}, f32[8,144]{1,0:T(8,128)}) custom-call(f32[32,72,128]{2,1,0:T(8,128)} %bitcast.12, f32[32,72,128]{2,1,0:T(8,128)} %bitcast.13, s32[32,96]{1,0:T(8,128)} %ids_ref.1, f32[24,144]{1,0:T(8,128)} %w_exp.1, ...), custom_call_target="tpu_custom_call" | custom-call | tf_op jit(solution)/shard_map/pallas_call | solution.py:970
  113.6 4.9 %shard_map.286 = (f32[32,72,128]{2,1,0:T(8,128)}, f32[32,72,128]{2,1,0:T(8,128)}, f32[24,144]{1,0:T(8,128)}, f32[9,144]{1,0:T(8,128)}, f32[6,144]{1,0:T(8,128)},...) custom-call(f32[5,24,144]{2,1,0:T(8,128)} %get-tuple-element.43.gs, ...), custom_call_target="tpu_custom_call" | custom-call | tf_op jit(solution)/shard_map/pallas_call | solution.py:1032

commit v4 on v3

--- a/solution.py
+++ b/solution.py
@@ -29,7 +29,6 @@
 WIDE = 2 * HALF_W
 ROWS = IN * 3
 GROUP = 8
-BULK = 16
 
 F32 = jnp.float32
 BF16 = jnp.bfloat16
@@ -92,8 +91,8 @@
     n_dev, n_space, slots, n_pos,
     feat, cot, ids_ref, w_exp, w_dep, w_red_t, w_exc, w_pro_t, vec, big, in_st, sq_st, tap_st,
     out, ing, gs_out, nw_out, vr_out,
-    xloc, xq, cq, xs, x3, c3, v1, a2, hh, dn2, dh, dm, dp, a3, hot, dcat, tab, msk, reg, acc, w1t, wlow, prm,
-    small, pooled, gates, dgate, bulk, bulk_in, bulk_all, rb1, rb, nws, fold,
+    xloc, xq, xs, v1, a2, hh, dn2, dh, dm, dp, a3, hot, dcat, prods, tab, msk, reg, acc, w1t, wlow, prm,
+    small, pooled, gates, bulk, bulk_in, bulk_all, rb1, rb, nws, fold,
     loc_sem, x_send, x_recv, c_send, c_recv, o_send, o_recv, g_send, g_recv,
     r_send, r_recv, own_sem,
 ):
@@ -126,9 +125,8 @@
     for load in loads:
         load.start()
     own_x = pltpu.make_async_copy(feat.at[pl.ds(slots * space, slots)], xq.at[space], own_sem.at[0])
-    own_c = pltpu.make_async_copy(cot.at[pl.ds(slots * space, slots)], cq.at[space], own_sem.at[1])
+    own_c = pltpu.make_async_copy(cot.at[pl.ds(slots * space, slots)], xloc.at[space], own_sem.at[1])
     own_x.start()
-    own_c.start()
 
     for load in loads:
         load.wait()
@@ -193,13 +191,55 @@
         return quad_copy(feat.at[slots * peer(step) + s], xq.at[space, s], x_send, x_recv, step, s)
 
     def c_copy(step, s):
-        return quad_copy(cot.at[slots * peer(step) + s], cq.at[space, s], c_send, c_recv, step, s)
+        return quad_copy(cot.at[slots * peer(step) + s], xloc.at[space, s], c_send, c_recv, step, s)
 
     def o_copy(step, s):
-        return quad_copy(xloc.at[peer(step), s], out.at[slots * space + s], o_send, o_recv, step, s)
+        return quad_copy(xq.at[peer(step), s], out.at[slots * space + s], o_send, o_recv, step, s)
 
     def g_copy(step, s):
-        return quad_copy(xq.at[peer(step), s], ing.at[slots * space + s], g_send, g_recv, step, s)
+        return quad_copy(xloc.at[peer(step), s], ing.at[slots * space + s], g_send, g_recv, step, s)
+
+    base = lax.div(me, GROUP) * GROUP
+    place = lax.rem(me, GROUP)
+
+    def group_copy(source, target, index, step):
+        return pltpu.make_async_remote_copy(
+            src_ref=source, dst_ref=target, send_sem=r_send.at[index], recv_sem=r_recv.at[index],
+            device_id=device(base + lax.rem(place + step, GROUP)), device_id_type=MESH,
+        )
+
+    def bulk_scatter(which, heads, index):
+        for i in range(GROUP):
+            bulk[which, i] = heads[i][:, :LANES] if i < len(heads) else jnp.zeros((8, LANES), F32)
+        ends = [head[:, LANES:] for head in heads]
+        rest = jnp.zeros((8, LANES - (EXP - LANES) * len(heads)), F32)
+        bulk[which, len(heads)] = jnp.concatenate(ends + [rest], axis=1)
+        for step in range(1, GROUP):
+            other = lax.rem(place + step, GROUP)
+            group_copy(bulk.at[which, other], bulk_in.at[which, place], index, step).start()
+        bulk_in[which, place] = bulk[which, place]
+
+    def bulk_gather(which, index, out_index):
+        window = bulk_in.at[which, pl.ds(0, GROUP - 1)]
+        done = group_copy(window, window, index, 1)
+        done.wait_send()
+        done.wait_recv()
+        bulk_all[which, me] = jnp.sum(bulk_in[which], axis=0)
+        spread_start(bulk_all.at[which, me], bulk_all.at[which, me], out_index)
+
+    def bulk_tiles(which, count, out_index):
+        spread_wait(bulk_all.at[which, pl.ds(0, n_dev - 1)], out_index)
+        summed = []
+        for i in range(count + 1):
+            tile = bulk_all[which, i]
+            for g in range(1, n_dev // GROUP):
+                tile = tile + bulk_all[which, g * GROUP + i]
+            summed.append(tile)
+        width = EXP - LANES
+        return [
+            jnp.concatenate([summed[i], summed[count][:, width * i : width * (i + 1)]], axis=1)
+            for i in range(count)
+        ]
 
     spread_start(rb1.at[me], rb1.at[me], 0)
 
@@ -236,11 +276,11 @@
 
     marks = [both_halves(rows) for rows in (from_ok, to_ok)]
     regions = [both_halves((wide_ids == float(r)).astype(F32)) for r in range(REGIONS)]
+    region_ids = both_halves(wide_ids)
     for s in range(slots):
         for i in range(2):
             msk[i, s] = jnp.broadcast_to(marks[i][s : s + 1], (8, WIDE * LANES))
-        for r in range(REGIONS):
-            reg[r, s] = jnp.broadcast_to(regions[r][s : s + 1], (8, WIDE * LANES))
+        reg[s] = jnp.broadcast_to(region_ids[s : s + 1], (8, WIDE * LANES)).astype(jnp.int32)
     row_index = lax.broadcasted_iota(jnp.int32, (slots * REGIONS, WIDE * LANES), 0)
     counts = jnp.zeros((slots * REGIONS, 1), F32)
     for s in range(slots):
@@ -287,15 +327,17 @@
     ).astype(BF16)
 
     own_x.wait()
-    acc[0] = jnp.zeros((EXP, LANES), F32)
+    for i in (0, 2, 3):
+        acc[i] = jnp.zeros((EXP, LANES), F32)
 
     def fetch(quads, s, n):
         tile = quads[tile_quad(n), s, pl.ds(n % 3, IN, stride=3), :]
         return tile if n < HALF_W else pltpu.roll(tile, 8, 1)
 
-    def place_back(quads, s, n, tile):
+    def add_to(quads, s, n, tile):
         tile = tile if n < HALF_W else pltpu.roll(tile, LANES - 8, 1)
-        quads[tile_quad(n), s, pl.ds(n % 3, IN, stride=3), :] = tile
+        where = pl.ds(n % 3, IN, stride=3)
+        quads[tile_quad(n), s, where, :] = quads[tile_quad(n), s, where, :] + tile
 
     def later_bin(low, high):
         return (
@@ -323,7 +365,6 @@
     def expand_slot(s):
         for n in range(WIDE):
             tile = fetch(xq, s, n)
-            x3[s, :, on_lane(n)] = tile
             high, low = halves(jnp.concatenate([tile - mean_col, one_rows], axis=0))
             xs[s, 0:32, on_lane(n)] = high
             xs[s, 32:64, on_lane(n)] = low
@@ -335,9 +376,6 @@
             x_copy(step, s).wait_recv()
 
     def forward_slot(s, carry):
-        for step in range(1, QUADS):
-            c_copy(step, s).start()
-
         def bins_step(j, carry):
             rows = pl.ds(pl.multiple_of(8 * j, 8), 8)
             wt = [tab[t, rows, :] for t in range(TAPS)]
@@ -357,7 +395,8 @@
 
         def frames_step(j, carry):
             rows = tile_rows(j)
-            got = zero_tile
+            center = acc[3, rows, :]
+            got, square = zero_tile, zero_tile
             for half in range(2):
                 prior = [dm[rows, on_lane(half * HALF_W + k)] for k in range(HALF_W)]
                 later = [dp[rows, on_lane(half * HALF_W + k)] for k in range(HALF_W)]
@@ -369,8 +408,11 @@
                         + msk[1, s, :, where] * from_after(later, k, half)
                     )
                     a2[s, rows, where] = value
-                    got = got + value
+                    off = value - center
+                    got = got + off
+                    square = square + off * off
             acc[0, rows, :] = acc[0, rows, :] + got
+            acc[2, rows, :] = acc[2, rows, :] + square
             return carry
 
         lax.fori_loop(0, EXP // 8, bins_step, 0, unroll=9)
@@ -382,6 +424,25 @@
         expand_slot(jnp.minimum(s + 1, slots - 1))
         for j in range(EXP // 8):
             frames_step(j, 0)
+
+        @pl.when(s == 0)
+        def _():
+            acc[3] = nn(acc[0], jnp.ones((LANES, LANES), F32), FULL) * (1.0 / (FRAMES * BINS))
+
+            def again(j, carry):
+                rows = tile_rows(j)
+                center = acc[3, rows, :]
+                got, square = zero_tile, zero_tile
+                for n in range(WIDE):
+                    off = a2[0, rows, on_lane(n)] - center
+                    got = got + off
+                    square = square + off * off
+                acc[0, rows, :] = got
+                acc[2, rows, :] = square
+                return carry
+
+            lax.fori_loop(0, EXP // 8, again, 0, unroll=3)
+
         return carry
 
     x_arrived(0)
@@ -389,26 +450,17 @@
 
     lax.fori_loop(0, slots, forward_slot, 0)
 
-    acc[1] = nn(acc[0], jnp.ones((LANES, LANES), F32), FULL) * (1.0 / n_loc)
-    acc[2] = jnp.zeros((EXP, LANES), F32)
-
-    def square_step(s, carry):
-        def tile_step(j, carry):
-            rows = pl.ds(pl.multiple_of(8 * j, 8), 8)
-            center = acc[1, rows, :]
-            got = zero_tile
-            for n in range(WIDE):
-                off = a2[s, rows, on_lane(n)] - center
-                got = got + off * off
-            acc[2, rows, :] = acc[2, rows, :] + got
-            return carry
-
-        return lax.fori_loop(0, EXP // 8, tile_step, carry, unroll=3)
-
-    lax.fori_loop(0, slots, square_step, 0)
-    rb[0, me, 0:2, :] = split_row(lane_sums(acc[0]) * (1.0 / n_loc))
-    rb[0, me, 2:4, :] = split_row(lane_sums(acc[2]))
+    drift = lane_sums(acc[0]) * (1.0 / n_loc)
+    rb[0, me, 0:2, :] = split_row(lane_sums(acc[3]) * (1.0 / LANES) + drift)
+    rb[0, me, 2:4, :] = split_row(lane_sums(acc[2]) - n_loc * drift * drift)
     spread_start(rb.at[0, me], rb.at[0, me], 1)
+    def c_start(t, carry):
+        for step in range(1, QUADS):
+            c_copy(step, t).start()
+        return carry
+
+    lax.fori_loop(0, slots, c_start, 0)
+    own_c.start()
     spread_wait(rb.at[0, pl.ds(0, n_dev - 1)], 1)
     sums = jnp.sum(rb[0], axis=0)
     mean2 = sums[0:2] * (1.0 / n_dev)
@@ -462,8 +514,8 @@
         rows = gates[s]
         return jnp.concatenate([project * rows[r : r + 1] for r in range(REGIONS)], axis=0)
 
-    def region_tile(r, s, n):
-        return jnp.concatenate([reg[r, s, :, on_lane(n)]] * (IN // 8), axis=0)
+    def region_tile(s, n):
+        return jnp.concatenate([reg[s, :, on_lane(n)]] * (IN // 8), axis=0)
 
     def project_slot(s, carry):
         total_a, total_c = carry
@@ -474,15 +526,12 @@
             c_copy(step, s).wait_recv()
         for n in range(WIDE):
             value = jnp.zeros((IN, LANES), F32)
+            ids = region_tile(s, n)
             for r in range(REGIONS):
-                value = value + (
-                    body[IN * r : IN * (r + 1), n * LANES : (n + 1) * LANES]
-                    * region_tile(r, s, n)
-                )
+                value = jnp.where(ids == r, body[IN * r : IN * (r + 1), n * LANES : (n + 1) * LANES], value)
             a3[s, :, on_lane(n)] = value
             total_a = total_a + value
-            upstream = fetch(cq, s, n)
-            c3[s, :, on_lane(n)] = upstream
+            upstream = fetch(xloc, s, n)
             total_c = total_c + upstream
         return total_a, total_c
 
@@ -496,7 +545,7 @@
         for n in range(WIDE):
             off = a3[s, :, on_lane(n)] - center3
             square = square + off * off
-            cross = cross + off * c3[s, :, on_lane(n)]
+            cross = cross + off * fetch(xloc, s, n)
         return square, cross
 
     square3, cross3 = lax.fori_loop(0, slots, third_step, (zero24, zero24))
@@ -514,6 +563,37 @@
         axis=0,
     )
     spread_start(rb.at[1, me], rb.at[1, me], 2)
+
+    def region_parts(s):
+        for n in range(WIDE):
+            where = on_lane(n)
+            ids = region_tile(s, n)
+            masks = [ids == r for r in range(REGIONS)]
+            upstream = fetch(xloc, s, n)
+            off = a3[s, :, where] - center3
+            high, low = halves(jnp.concatenate([jnp.where(mask, upstream, 0.0) for mask in masks], axis=0))
+            dcat[s, 0:96, where] = high
+            dcat[s, 128:224, where] = low
+            high, low = halves(jnp.concatenate([jnp.where(mask, off, 0.0) for mask in masks], axis=0))
+            dcat[s, 256:352, where] = high
+            dcat[s, 352:448, where] = low
+        dcat[s, 96:128, :] = hot[s]
+        dcat[s, 224:256, :] = hot[s]
+
+    def region_products(s):
+        main = nt(dcat[s], hh[s, 0:EXP, :])
+        rest = nt(jnp.concatenate([dcat[s, 0:96, :], dcat[s, 256:352, :]], axis=0), hh[s, EXP:, :])
+        prods[0, s] = main[0:96] + main[128:224] + rest[:96]
+        prods[1, s] = main[256:352] + main[352:448] + rest[96:]
+
+    def region_slot(s, carry):
+        region_products(s - 1)
+        region_parts(s)
+        return carry
+
+    region_parts(0)
+    lax.fori_loop(1, slots, region_slot, 0)
+    region_products(slots - 1)
     spread_wait(rb.at[1, pl.ds(0, n_dev - 1)], 2)
     third = rb[1]
     sums = jnp.sum(third, axis=0)
@@ -537,50 +617,29 @@
         axis=0,
     )
     mean3_c, grow3_c, lift3_c, flat3_c, lean3_c = (column(rows8, i, IN) for i in range(5))
-
+    flat3_c = -flat3_c - (center3 - mean3_c) * lean3_c
+
+    grow3_w, lean3_w, flat3_w = (
+        jnp.concatenate([tile, tile[:, : EXP - LANES]], axis=1) for tile in (grow3_c, lean3_c, flat3_c)
+    )
+    project = w_pro_t[...]
+    sums_of_h = pooled[...]
     small[0] = jnp.zeros((IN, EXP), F32)
-
-    def project_back(s):
-        for n in range(WIDE):
-            off = a3[s, :, on_lane(n)] - mean3_c
-            place_back(xloc, s, n, x3[s, :, on_lane(n)] + off * grow3_c + lift3_c)
-            grad = grow3_c * c3[s, :, on_lane(n)] - flat3_c - off * lean3_c
-            high, low = halves(
-                jnp.concatenate(
-                    [grad * region_tile(r, s, n) for r in range(REGIONS)], axis=0
-                )
+    gate_rows = []
+    for s in range(slots):
+        gp = small[0]
+        for r in range(REGIONS):
+            q = REGIONS * s + r
+            part = (
+                grow3_w * prods[0, s, IN * r : IN * (r + 1), :]
+                - lean3_w * prods[1, s, IN * r : IN * (r + 1), :]
+                + flat3_w * sums_of_h[q : q + 1]
             )
-            dcat[s, 0:96, on_lane(n)] = high
-            dcat[s, 128:224, on_lane(n)] = low
-        dcat[s, 96:128, :] = hot[s]
-        dcat[s, 224:256, :] = hot[s]
-        for step in range(1, QUADS):
-            o_copy(step, s).start()
-
-    def gate_back(s):
-        main = nt(dcat[s, 0:224, :], hh[s, 0:EXP, :])
-        main = main[0:96] + main[128:224] + nt(dcat[s, 0:96, :], hh[s, EXP:, :])
-        project = w_pro_t[...]
-        gp = small[0]
-        rows = gates[s]
-        for r in range(REGIONS):
-            part = main[IN * r : IN * (r + 1)]
-            dgate[s, r : r + 1, :] = jnp.sum(part * project, axis=0, keepdims=True)
-            gp = gp + part * rows[r : r + 1]
+            gate_rows.append(jnp.sum(part * project, axis=0, keepdims=True))
+            gp = gp + part * gate[q : q + 1]
         small[0] = gp
-
-    def back_slot(s, carry):
-        gate_back(s - 1)
-        project_back(s)
-        return carry
-
-    project_back(0)
-    lax.fori_loop(1, slots, back_slot, 0)
-    gate_back(slots - 1)
-    own_o = pltpu.make_async_copy(xloc.at[space], out.at[pl.ds(slots * space, slots)], own_sem.at[2])
-    own_o.start()
-
-    dgate_rows = jnp.concatenate([dgate[s] for s in range(slots)], axis=0)
+    dgate_rows = jnp.concatenate(gate_rows, axis=0)
+
     dpre_x = dgate_rows * gate * (1.0 - gate)
     excite_grad = tn(squeezed, dpre_x, FULL)
     excite_bias_grad = jnp.sum(dpre_x, axis=0, keepdims=True)
@@ -589,16 +648,41 @@
     reduce_grad = tn(dpre_r, mean_pool, FULL)
     reduce_bias_grad = jnp.sum(dpre_r, axis=0, keepdims=True)
     dpool = nn(dpre_r, w_red_t[...], FULL) * per_count
-    pooled[...] = 0.5 * dpool
+    pooled[...] = 0.5 * dpool + 0.5 * gate * jnp.sum(project * flat3_w, axis=0, keepdims=True)
+
+    side_rows = jnp.concatenate(
+        [excite_bias_grad, jnp.concatenate([reduce_bias_grad, jnp.zeros((1, EXP - SQZ), F32)], axis=1)], axis=0
+    )
+    early = [small[0, 8 * i : 8 * i + 8, :] for i in range(3)] + [
+        jnp.concatenate([part, jnp.zeros((8 - part.shape[0], EXP), F32)], axis=0)
+        for part in (excite_grad, reduce_grad, side_rows)
+    ]
+    bulk_scatter(0, early, 4)
 
     acc[0] = jnp.zeros((EXP, LANES), F32)
     acc[1] = jnp.zeros((EXP, LANES), F32)
 
+    grown_project = 0.5 * project * grow3_w
+    lean_project = -0.5 * project * lean3_w
+
     def activation_back(s, target):
-        high, low = halves(0.5 * gated_weights(s))
+        rows = gates[s]
+        high, low = halves(jnp.concatenate([grown_project * rows[r : r + 1] for r in range(REGIONS)], axis=0))
+        lean_high, lean_low = halves(
+            jnp.concatenate([lean_project * rows[r : r + 1] for r in range(REGIONS)], axis=0)
+        )
         pool_high, pool_low = halves(pooled[...])
         left = jnp.concatenate([high, pool_high, high, pool_low], axis=0)
-        target[...] = tn(left, dcat[s]) + tn(low, dcat[s, 0:96, :])
+        target[...] = (
+            tn(left, dcat[s, 0:256, :])
+            + tn(jnp.concatenate([lean_high, lean_high], axis=0), dcat[s, 256:448, :])
+            + tn(jnp.concatenate([low, lean_low], axis=0), jnp.concatenate([dcat[s, 0:96, :], dcat[s, 256:352, :]], axis=0))
+        )
+
+    def leave(s):
+        for n in range(WIDE):
+            off = a3[s, :, on_lane(n)] - mean3_c
+            add_to(xq, s, n, off * grow3_c + lift3_c)
 
     def norm_back(s, source):
         for j in range(EXP // 8):
@@ -620,8 +704,10 @@
         s = 2 * i
         activation_back(s + 1, dm)
         norm_back(s, dh)
+        leave(s)
         activation_back(jnp.minimum(s + 2, slots - 1), dh)
         norm_back(s + 1, dm)
+        leave(s + 1)
         return carry
 
     activation_back(0, dh)
@@ -629,7 +715,17 @@
     rb[2, me, 0:2, :] = split_row(lane_sums(acc[0]))
     rb[2, me, 2:4, :] = split_row(lane_sums(acc[1]))
     spread_start(rb.at[2, me], rb.at[2, me], 3)
+
+    def o_start(s, carry):
+        for step in range(1, QUADS):
+            o_copy(step, s).start()
+        return carry
+
+    lax.fori_loop(0, slots, o_start, 0)
+    own_o = pltpu.make_async_copy(xq.at[space], out.at[pl.ds(slots * space, slots)], own_sem.at[2])
+    own_o.start()
     spread_wait(rb.at[2, pl.ds(0, n_dev - 1)], 3)
+    bulk_gather(0, 4, 5)
     sums = jnp.sum(rb[2], axis=0)
     bias2_grad = join_row(sums[0:2])
     cross2 = join_row(sums[2:4])
@@ -732,46 +828,16 @@
 
     lax.fori_loop(0, slots, taps_back_slot, 0)
 
-    stacked = [small[0], small[1]]
     cross1 = jnp.sum(small[1] * weight, axis=0, keepdims=True)
     rb[3, me, 0:2, :] = split_row(small[2, 0:1, :])
     rb[3, me, 2:4, :] = split_row(cross1)
-    tail = [lane_sums(acc[t]) for t in range(TAPS)]
-    tail.append(excite_bias_grad)
-    tail.append(jnp.concatenate([reduce_bias_grad, jnp.zeros((1, EXP - SQZ), F32)], axis=1))
-    tail.append(jnp.zeros((5, EXP), F32))
-    stacked.append(jnp.concatenate(tail, axis=0))
-    for part in (excite_grad, reduce_grad):
-        stacked.append(jnp.concatenate([part, jnp.zeros((8 - SQZ, EXP), F32)], axis=0))
-    stacked = jnp.concatenate(stacked, axis=0)
-    n_heads = 10
-    for i in range(n_heads):
-        bulk[i] = stacked[8 * i : 8 * i + 8, :LANES]
-    ends = [stacked[8 * i : 8 * i + 8, LANES:] for i in range(n_heads)]
-    bulk[n_heads] = jnp.concatenate(ends[:8], axis=1)
-    bulk[n_heads + 1] = jnp.concatenate(ends[8:] + [jnp.zeros((8, LANES - 16 * (n_heads - 8)), F32)], axis=1)
-    for i in range(n_heads + 2, BULK):
-        bulk[i] = zero_tile
-    each = BULK // GROUP
-    base = lax.div(me, GROUP) * GROUP
-    place = lax.rem(me, GROUP)
-
-    def group_copy(source, target, index, step):
-        return pltpu.make_async_remote_copy(
-            src_ref=source, dst_ref=target, send_sem=r_send.at[index], recv_sem=r_recv.at[index],
-            device_id=device(base + lax.rem(place + step, GROUP)), device_id_type=MESH,
-        )
-
-    for step in range(1, GROUP):
-        other = lax.rem(place + step, GROUP)
-        group_copy(bulk.at[pl.ds(each * other, each)], bulk_in.at[place], 4, step).start()
-    bulk_in[place] = bulk[pl.ds(each * place, each)]
+    tap_rows = [lane_sums(acc[t]) for t in range(TAPS)]
+    late = [small[1, 8 * i : 8 * i + 8, :] for i in range(3)]
+    late.append(jnp.concatenate(tap_rows[:8], axis=0))
+    late.append(jnp.concatenate([tap_rows[8], jnp.zeros((7, EXP), F32)], axis=0))
+    bulk_scatter(1, late, 8)
     spread_start(rb.at[3, me], rb.at[3, me], 7)
-    done = group_copy(bulk_in.at[pl.ds(0, GROUP - 1)], bulk_in.at[pl.ds(0, GROUP - 1)], 4, 1)
-    done.wait_send()
-    done.wait_recv()
-    bulk_all[me] = jnp.sum(bulk_in[...], axis=0)
-    spread_start(bulk_all.at[me], bulk_all.at[me], 5)
+    bulk_gather(1, 8, 9)
     spread_wait(rb.at[3, pl.ds(0, n_dev - 1)], 7)
     sums = jnp.sum(rb[3], axis=0)
     bias1_grad = join_row(sums[0:2])
@@ -799,40 +865,28 @@
         main = nn(grown_both, hh[s, 0:EXP, :])
         main = main[:IN] + main[IN:] + nn(grown_high, hh[s, EXP:, :]) + nn(wlow[...], xs[s])
         for n in range(WIDE):
-            place_back(xq, s, n, c3[s, :, on_lane(n)] + main[:, n * LANES : (n + 1) * LANES])
+            add_to(xloc, s, n, main[:, n * LANES : (n + 1) * LANES])
         for step in range(1, QUADS):
             g_copy(step, s).start()
         return carry
 
     lax.fori_loop(0, slots, last_slot, 0)
-    own_g = pltpu.make_async_copy(xq.at[space], ing.at[pl.ds(slots * space, slots)], own_sem.at[3])
+    own_g = pltpu.make_async_copy(xloc.at[space], ing.at[pl.ds(slots * space, slots)], own_sem.at[3])
     own_g.start()
 
-    spread_wait(bulk_all.at[pl.ds(0, n_dev - 1)], 5)
-    summed = []
-    for i in range(n_heads + 2):
-        tile = zero_tile
-        for g in range(n_dev // GROUP):
-            tile = tile + bulk_all[g * GROUP + i // each, i % each]
-        summed.append(tile)
-
-    def row_tile(i):
-        rest = summed[n_heads + i // 8][:, 16 * (i % 8) : 16 * (i % 8) + 16]
-        return jnp.concatenate([summed[i], rest], axis=1)
-
-    project_grad = jnp.concatenate([row_tile(i) for i in range(3)], axis=0)
-    expand_cross = jnp.concatenate([row_tile(i) for i in range(3, 6)], axis=0)
-    depth_tiles = jnp.concatenate([row_tile(6), row_tile(7)], axis=0)
-    excite_tile = row_tile(8)
-    reduce_tile = row_tile(9)
+    early = bulk_tiles(0, 6, 5)
+    late = bulk_tiles(1, 5, 9)
+    project_grad = jnp.concatenate(early[:3], axis=0)
+    excite_tile, reduce_tile, side_tile = early[3:]
+    expand_cross = jnp.concatenate(late[:3], axis=0)
+    depth_tiles = jnp.concatenate(late[3:], axis=0)
     expand_grad = grow1 * (expand_cross - lean1 * moment_w)
     zero_rows = jnp.zeros((16, EXP), F32)
     gs_out[0] = expand_grad
     gs_out[1] = project_grad
     gs_out[2] = jnp.concatenate([reduce_tile, zero_rows], axis=0)
     gs_out[3] = jnp.concatenate([excite_tile, zero_rows], axis=0)
-    row16 = lax.broadcasted_iota(jnp.int32, (16, EXP), 0)
-    gs_out[4] = jnp.concatenate([jnp.where(row16 < TAPS, depth_tiles, 0.0), zero_rows[:8]], axis=0)
+    gs_out[4] = jnp.concatenate([depth_tiles, zero_rows[:8]], axis=0)
     vr_out[...] = jnp.concatenate(
         [
             gain1_grad,
@@ -841,8 +895,8 @@
             bias2_grad,
             jnp.concatenate([gain3_grad, jnp.zeros((1, EXP - LANES), F32)], axis=1),
             jnp.concatenate([bias3_grad, jnp.zeros((1, EXP - LANES), F32)], axis=1),
-            depth_tiles[TAPS + 1 : TAPS + 2],
-            depth_tiles[TAPS : TAPS + 1],
+            side_tile[1:2],
+            side_tile[0:1],
         ],
         axis=0,
     )
@@ -981,10 +1035,7 @@
         scratch_shapes=[
             vmem((QUADS, slots, ROWS, LANES), F32),
             vmem((QUADS, slots, ROWS, LANES), F32),
-            vmem((QUADS, slots, ROWS, LANES), F32),
             vmem((slots, 96, wide), BF16),
-            vmem((slots, IN, wide), F32),
-            vmem((slots, IN, wide), F32),
             vmem((slots, EXP, wide), F32),
             vmem((slots, EXP, wide), F32),
             vmem((slots, 2 * EXP, wide), BF16),
@@ -994,10 +1045,11 @@
             vmem((EXP, wide), F32),
             vmem((slots, IN, wide), F32),
             vmem((slots, slots * REGIONS, wide), BF16),
-            vmem((slots, 256, wide), BF16),
+            vmem((slots, 448, wide), BF16),
+            vmem((2, slots, 96, EXP), F32),
             vmem((TAPS + 3, EXP, LANES), F32),
             vmem((2, slots, 8, wide), F32),
-            vmem((REGIONS, slots, 8, wide), F32),
+            vmem((slots, 8, wide), jnp.int32),
             vmem((TAPS, EXP, LANES), F32),
             vmem((EXP, 96), BF16),
             vmem((IN, 96), BF16),
@@ -1005,10 +1057,9 @@
             vmem((5, IN, EXP), F32),
             vmem((slots * REGIONS, EXP), F32),
             vmem((slots, REGIONS, EXP), F32),
-            vmem((slots, REGIONS, EXP), F32),
-            vmem((BULK, 8, LANES), F32),
-            vmem((GROUP, BULK // GROUP, 8, LANES), F32),
-            vmem((n_dev, BULK // GROUP, 8, LANES), F32),
+            vmem((2, GROUP, 8, LANES), F32),
+            vmem((2, GROUP, 8, LANES), F32),
+            vmem((2, n_dev, 8, LANES), F32),
             vmem((n_dev, 8, LANES), F32),
             vmem((4, n_dev, 4, LANES), F32),
             vmem((GROUP, IN, EXP), F32),
@@ -1016,9 +1067,9 @@
             dma((QUADS,)),
         ]
         + [dma((QUADS, slots))] * 8
-        + [dma((8,)), dma((8,)), dma((4,))],
+        + [dma((10,)), dma((10,)), dma((4,))],
         compiler_params=pltpu.CompilerParams(
-            collective_id=0, has_side_effects=True, vmem_limit_bytes=60 << 20
+            collective_id=0, has_side_effects=True, vmem_limit_bytes=62 << 20
         ),
     )(
         features.reshape(slot_count, ROWS, LANES),
@@ -1040,7 +1091,7 @@
         in_specs=[vm] * 9 + [hbm] * 2,
         out_specs=(hbm, hbm) + (vm,) * 17,
         scratch_shapes=[vmem((2,) + grid_shape.shape, F32), dma((2,))],
-        compiler_params=pltpu.CompilerParams(vmem_limit_bytes=60 << 20),
+        compiler_params=pltpu.CompilerParams(vmem_limit_bytes=62 << 20),
     )(gs, nw, vr, big_stats, in_stats, sq_rows, tap_stats, vector_params, vector_moments, out, ing)
     return (
         out.reshape(features.shape), ing.reshape(features.shape),

time: 119 us -> 114 us (0.958)
  Pallas kernels: 118 us -> 113 us
    pallas_call x1, Pallas kernels: 113 us -> 108 us  [on_device(): pl.pallas_call(functools.partial(block_kernel, n_dev, n_space, slots, n_p...]
where the time goes in v4:
time: 114 us
  Pallas kernels  113 us (99%)
    pallas_call x1, Pallas kernels, on_device(): pl.pallas_call(functools.partial(block_kernel, n_dev, n_space, slots, n_p...  108 us
    pallas_call x1, Pallas kernels, on_device(): pl.pallas_call(finish_kernel, out_shape=(grid_shape, grid_shape) + tuple(...  4.94 us

profile of v4, /device:TPU:0, one launch (start us, length us, event | category | flops | bytes accessed | tf_op | source)
XLA Modules:
  0.0 113.9 jit_solution(13639494229048642847)
XLA Ops:
  0.7 108.2 %shard_map.285 = (f32[32,72,128]{2,1,0:T(8,128)}, f32[32,72,128]{2,1,0:T(8,128)}, f32[5,24,144]{2,1,0:T(8,128)}, f32[5,24,144]{2,1,0:T(8,128)}, f32[8,144]{1,0:T(8,128)}) custom-call(f32[32,72,128]{2,1,0:T(8,128)} %bitcast.12, f32[32,72,128]{2,1,0:T(8,128)} %bitcast.13, s32[32,96]{1,0:T(8,128)} %ids_ref.1, f32[24,144]{1,0:T(8,128)} %w_exp.1, ...), custom_call_target="tpu_custom_call" | custom-call | tf_op jit(solution)/shard_map/pallas_call | solution.py:1024
  108.8 4.9 %shard_map.286 = (f32[32,72,128]{2,1,0:T(8,128)}, f32[32,72,128]{2,1,0:T(8,128)}, f32[24,144]{1,0:T(8,128)}, f32[9,144]{1,0:T(8,128)}, f32[6,144]{1,0:T(8,128)},...) custom-call(f32[5,24,144]{2,1,0:T(8,128)} %get-tuple-element.43.gs, ...), custom_call_target="tpu_custom_call" | custom-call | tf_op jit(solution)/shard_map/pallas_call | solution.py:1083

commit v5 on v4

--- a/solution.py
+++ b/solution.py
@@ -91,7 +91,7 @@
     n_dev, n_space, slots, n_pos,
     feat, cot, ids_ref, w_exp, w_dep, w_red_t, w_exc, w_pro_t, vec, big, in_st, sq_st, tap_st,
     out, ing, gs_out, nw_out, vr_out,
-    xloc, xq, xs, v1, a2, hh, dn2, dh, dm, dp, a3, hot, dcat, prods, tab, msk, reg, acc, w1t, wlow, prm,
+    xloc, xq, xs, v1, a2, hh, dn2, dh, dm, dp, eh, em, ep, hidden, a3, hot, dcat, prods, tab, msk, reg, acc, w1t, wlow, prm,
     small, pooled, gates, bulk, bulk_in, bulk_all, rb1, rb, nws, fold,
     loc_sem, x_send, x_recv, c_send, c_recv, o_send, o_recv, g_send, g_recv,
     r_send, r_recv, own_sem,
@@ -748,95 +748,101 @@
     small[1] = jnp.zeros((IN, EXP), F32)
     small[2] = jnp.zeros((IN, EXP), F32)
 
-    def taps_back_slot(s, carry):
-        def frames_step(j, carry):
-            rows = pl.ds(pl.multiple_of(8 * j, 8), 8)
-            k1, k2, k3 = (tab[TAPS + i, rows, :] for i in range(3))
+    def frames_back(s, j, moved):
+        fore, back, here = moved
+        rows = tile_rows(j)
+        k1, k2, k3 = (tab[TAPS + i, rows, :] for i in range(3))
+        for half in range(2):
+            grads = []
+            for k in range(HALF_W):
+                where = on_lane(half * HALF_W + k)
+                grads.append(k1 * dn2[s, rows, where] + k2 * a2[s, rows, where] + k3)
+            for k in range(HALF_W):
+                where = on_lane(half * HALF_W + k)
+                here[rows, where] = grads[k]
+                fore[rows, where] = msk[1, s, :, where] * from_after(grads, k, half)
+                back[rows, where] = msk[0, s, :, where] * from_before(grads, k, half)
+
+    def bins_back(s, j, moved):
+        fore, back, here = moved
+        rows = tile_rows(j)
+        out = [None] * WIDE
+        wt = [tab[t, rows, :] for t in range(TAPS)]
+        for k in range(HALF_W):
+            mix = [[], [], []]
+            us, hs = [], []
             for half in range(2):
-                grads = []
-                for k in range(HALF_W):
-                    where = on_lane(half * HALF_W + k)
-                    grads.append(k1 * dn2[s, rows, where] + k2 * a2[s, rows, where] + k3)
-                for k in range(HALF_W):
-                    where = on_lane(half * HALF_W + k)
-                    dn2[s, rows, where] = grads[k]
-                    dm[rows, where] = msk[1, s, :, where] * from_after(grads, k, half)
-                    dp[rows, where] = msk[0, s, :, where] * from_before(grads, k, half)
-            return carry
-
-        def bins_tile(j):
-            rows = pl.ds(pl.multiple_of(8 * j, 8), 8)
-            out = [None] * WIDE
-            wt = [tab[t, rows, :] for t in range(TAPS)]
-            for k in range(HALF_W):
-                mix = [[], [], []]
-                us, hs = [], []
-                for half in range(2):
-                    where = on_lane(half * HALF_W + k)
-                    moved = [dm[rows, where], dn2[s, rows, where], dp[rows, where]]
-                    for q in range(3):
-                        mix[q].append(wt[q] * moved[0] + wt[3 + q] * moved[1] + wt[6 + q] * moved[2])
-                    v = v1[s, rows, where]
-                    u = 1.0 + jnp.tanh(v)
-                    us.append(u)
-                    hs.append(v * u)
-                left = later_bin(*mix[0])
-                right = earlier_bin(*mix[2])
-                for half in range(2):
-                    out[half * HALF_W + k] = (left[half] + mix[1][half] + right[half]) * (
-                        us[half] + hs[half] * (2.0 - us[half])
-                    )
-            return out
-
-        def bins_step(j, carry):
-            rows = pl.ds(pl.multiple_of(16 * j, 16), 16)
-            low_rows = pl.ds(pl.multiple_of(EXP + 16 * j, 16), 16)
-            for n, pair in enumerate(zip(bins_tile(2 * j), bins_tile(2 * j + 1))):
+                where = on_lane(half * HALF_W + k)
+                shifts = [fore[rows, where], here[rows, where], back[rows, where]]
+                for q in range(3):
+                    mix[q].append(wt[q] * shifts[0] + wt[3 + q] * shifts[1] + wt[6 + q] * shifts[2])
+                v = v1[s, rows, where]
+                u = 1.0 + jnp.tanh(v)
+                us.append(u)
+                hs.append(v * u)
+                hidden[rows, where] = hs[half]
+            left = later_bin(*mix[0])
+            right = earlier_bin(*mix[2])
+            for half in range(2):
+                out[half * HALF_W + k] = (left[half] + mix[1][half] + right[half]) * (
+                    us[half] + hs[half] * (2.0 - us[half])
+                )
+        return out
+
+    def taps_back(s, j, moved):
+        fore, back, here = moved
+        rows = tile_rows(j)
+        sums = [zero_tile] * TAPS
+        for k in range(HALF_W):
+            hs = [hidden[rows, on_lane(half * HALF_W + k)] for half in range(2)]
+            near = [earlier_bin(*hs), hs, later_bin(*hs)]
+            for half in range(2):
+                where = on_lane(half * HALF_W + k)
+                shifts = [fore[rows, where], here[rows, where], back[rows, where]]
+                for q in range(3):
+                    for p in range(3):
+                        sums[3 * p + q] = sums[3 * p + q] + shifts[p] * near[q][half]
+        for t in range(TAPS):
+            acc[t, rows, :] = acc[t, rows, :] + sums[t]
+
+    def taps_back_slot(s, moved, later):
+        for j in range(EXP // 16):
+            rows, low_rows = pl.ds(16 * j, 16), pl.ds(EXP + 16 * j, 16)
+            for n, pair in enumerate(zip(bins_back(s, 2 * j, moved), bins_back(s, 2 * j + 1, moved))):
                 high, low = halves(jnp.concatenate(pair, axis=0))
                 hh[s, rows, on_lane(n)] = high
                 hh[s, low_rows, on_lane(n)] = low
-            return carry
-
-        def taps_step(j, carry):
-            rows = tile_rows(j)
-            sums = [zero_tile] * TAPS
-            for k in range(HALF_W):
-                hs = []
-                for half in range(2):
-                    v = v1[s, rows, on_lane(half * HALF_W + k)]
-                    hs.append(v + v * jnp.tanh(v))
-                near = [earlier_bin(*hs), hs, later_bin(*hs)]
-                for half in range(2):
-                    where = on_lane(half * HALF_W + k)
-                    moved = [dm[rows, where], dn2[s, rows, where], dp[rows, where]]
-                    for q in range(3):
-                        for p in range(3):
-                            sums[3 * p + q] = sums[3 * p + q] + moved[p] * near[q][half]
-            for t in range(TAPS):
-                acc[t, rows, :] = acc[t, rows, :] + sums[t]
-            return carry
-
-        lax.fori_loop(0, EXP // 8, frames_step, 0, unroll=9)
-        lax.fori_loop(0, EXP // 16, bins_step, 0, unroll=True)
+            frames_back(jnp.minimum(s + 1, slots - 1), j, later)
         for j in range(EXP // 8):
-            taps_step(j, 0)
+            taps_back(s, j, moved)
+            if j >= EXP // 16:
+                frames_back(jnp.minimum(s + 1, slots - 1), j, later)
         main = nt(xs[s, 0:64, :], hh[s, 0:EXP, :])
         main = main[0:32] + main[32:64] + nt(xs[s, 0:32, :], hh[s, EXP:, :])
         small[1] = small[1] + 0.5 * main[0:IN]
         small[2, 0:8, :] = small[2, 0:8, :] + 0.5 * main[IN:32]
+
+    evens, odds = (dm, dp, dh), (em, ep, eh)
+
+    def taps_back_pair(i, carry):
+        s = 2 * i
+        taps_back_slot(s, evens, odds)
+        taps_back_slot(s + 1, odds, evens)
         return carry
 
-    lax.fori_loop(0, slots, taps_back_slot, 0)
+    for j in range(EXP // 8):
+        frames_back(0, j, evens)
+    lax.fori_loop(0, slots // 2, taps_back_pair, 0)
 
     cross1 = jnp.sum(small[1] * weight, axis=0, keepdims=True)
     rb[3, me, 0:2, :] = split_row(small[2, 0:1, :])
     rb[3, me, 2:4, :] = split_row(cross1)
+    spread_start(rb.at[3, me], rb.at[3, me], 7)
     tap_rows = [lane_sums(acc[t]) for t in range(TAPS)]
     late = [small[1, 8 * i : 8 * i + 8, :] for i in range(3)]
     late.append(jnp.concatenate(tap_rows[:8], axis=0))
     late.append(jnp.concatenate([tap_rows[8], jnp.zeros((7, EXP), F32)], axis=0))
     bulk_scatter(1, late, 8)
-    spread_start(rb.at[3, me], rb.at[3, me], 7)
     bulk_gather(1, 8, 9)
     spread_wait(rb.at[3, pl.ds(0, n_dev - 1)], 7)
     sums = jnp.sum(rb[3], axis=0)
@@ -912,8 +918,8 @@
     small[4, :TAPS, :TAPS] = tap_st[...]
     old_big = big[mine]
     old_big = jnp.where(turned, jnp.transpose(old_big), old_big)
-    big_m = DECAY * old_big + FRESH * tn(grad, grad, FULL)
-    small_m = DECAY * small[mine][:, :IN] + FRESH * nt(grad, grad, FULL)
+    big_m = DECAY * old_big + FRESH * tn(grad, grad, MID)
+    small_m = DECAY * small[mine][:, :IN] + FRESH * nt(grad, grad, MID)
     big_eye = (
         lax.broadcasted_iota(jnp.int32, (EXP, EXP), 0) == lax.broadcasted_iota(jnp.int32, (EXP, EXP), 1)
     ).astype(F32)
@@ -937,10 +943,12 @@
         small_k = nn(small_k, small_k, MID)
         return nn(big_k, big_m, MID), nn(small_k, small_m, MID), direction, small_h
 
-    _, _, direction, small_h = lax.fori_loop(
-        0, ROOT_ITERS, root_step, (big_m, small_m, direction, small_h)
-    )
-    direction = nn(small_h, direction, FULL)
+    big_m, small_m, direction, small_h = lax.fori_loop(
+        0, ROOT_ITERS - 1, root_step, (big_m, small_m, direction, small_h)
+    )
+    direction = nn(direction, 1.25 * big_eye - 0.25 * big_m, MID)
+    small_h = nn(small_h, 1.25 * small_eye - 0.25 * small_m, MID)
+    direction = nn(small_h, direction, MID)
     short = jnp.where(mine < 2, float(IN), jnp.where(mine == 4, float(TAPS), float(SQZ)))
     lead = jnp.where(turned, float(EXP), short)
     power = jnp.sum(jnp.sum(direction * direction, axis=0, keepdims=True), axis=1, keepdims=True)
@@ -994,8 +1002,8 @@
         store.start()
     for i in range(5):
         grad = gs[i]
-        big_new[i] = DECAY * big[i] + FRESH * tn(grad, grad, FULL)
-        inner = FRESH * nt(grad, grad, FULL)
+        big_new[i] = DECAY * big[i] + FRESH * tn(grad, grad, MID)
+        inner = FRESH * nt(grad, grad, MID)
         if i < 2:
             in_new[i] = DECAY * in_st[i] + inner
         elif i < 4:
@@ -1043,6 +1051,10 @@
             vmem((EXP, wide), F32),
             vmem((EXP, wide), F32),
             vmem((EXP, wide), F32),
+            vmem((EXP, wide), F32),
+            vmem((EXP, wide), F32),
+            vmem((EXP, wide), F32),
+            vmem((EXP, wide), F32),
             vmem((slots, IN, wide), F32),
             vmem((slots, slots * REGIONS, wide), BF16),
             vmem((slots, 448, wide), BF16),

time: 114 us -> 113 us (level)
    pallas_call x1, Pallas kernels: 108 us -> 107 us  [on_device(): pl.pallas_call(functools.partial(block_kernel, n_dev, n_space, slots, n_p...]
where the time goes in v5:
time: 113 us; the launch traced here: 112 us
  Pallas kernels  112 us (99%)
    pallas_call x1, Pallas kernels, on_device(): pl.pallas_call(functools.partial(block_kernel, n_dev, n_space, slots, n_p...  107 us
    pallas_call x1, Pallas kernels, on_device(): pl.pallas_call(finish_kernel, out_shape=(grid_shape, grid_shape) + tuple(...  4.94 us

profile of v5, /device:TPU:0, one launch (start us, length us, event | category | flops | bytes accessed | tf_op | source)
XLA Modules:
  0.0 112.3 jit_solution(32501940179962729)
XLA Ops:
  0.7 106.6 %shard_map.285 = (f32[32,72,128]{2,1,0:T(8,128)}, f32[32,72,128]{2,1,0:T(8,128)}, f32[5,24,144]{2,1,0:T(8,128)}, f32[5,24,144]{2,1,0:T(8,128)}, f32[8,144]{1,0:T(8,128)}) custom-call(f32[32,72,128]{2,1,0:T(8,128)} %bitcast.12, f32[32,72,128]{2,1,0:T(8,128)} %bitcast.13, s32[32,96]{1,0:T(8,128)} %ids_ref.1, f32[24,144]{1,0:T(8,128)} %w_exp.1, ...), custom_call_target="tpu_custom_call" | custom-call | tf_op jit(solution)/shard_map/pallas_call | solution.py:1032
  107.2 4.9 %shard_map.286 = (f32[32,72,128]{2,1,0:T(8,128)}, f32[32,72,128]{2,1,0:T(8,128)}, f32[24,144]{1,0:T(8,128)}, f32[9,144]{1,0:T(8,128)}, f32[6,144]{1,0:T(8,128)},...) custom-call(f32[5,24,144]{2,1,0:T(8,128)} %get-tuple-element.43.gs, ...), custom_call_target="tpu_custom_call" | custom-call | tf_op jit(solution)/shard_map/pallas_call | solution.py:1095
